TPU v7x, 1024 devices: a whole 4x4x32 slice. The times are simulated.
1024 devices in a mesh: section: 32 (over x, z_hi, core), expert: 32 (over y, z_lo).
Axes of the slice: x: 4, y: 4, z: 32 (z_hi: 4, z_lo: 8; z = z_hi * 8 + z_lo), core: 2. Of those that a mesh axis runs over, the one named last changes fastest.
Arguments:
- cotangent: bfloat16 [32, 512, 2048], P('section', 'expert'), may hold values from -6 to 6
- expert_ids: int32 [32, 512, 8], P('section', 'expert'), may hold values from 0 to 31, all different within a row; in each aligned block of 16 rows (0 to 15, 16 to 31, ..., all dimensions but the last counted through in order) at most 8 rows name the same one
- gate_probs: bfloat16 [32, 512, 8], P('section', 'expert'), may hold values from 0.099609375 to 1
- saved: bfloat16 [32, 32, 256, 1536], P('section', 'expert'), may hold values from -5 to 5
- w_gate: bfloat16 [32, 2048, 768], P('expert'), may hold values from -0.125 to 0.125
- w_up: bfloat16 [32, 2048, 768], P('expert'), may hold values from -0.125 to 0.125
- w_down: bfloat16 [32, 768, 2048], P('expert'), may hold values from -0.21875 to 0.21875
Outputs:
- input_grad: bfloat16 [32, 512, 2048], P('section', 'expert')
Inputs may be any that keep to these rules, and one draw needn't show every extreme that they name: `expert_ids`: each token names 8 different experts. Within the 16 tokens of one device (aligned blocks along the token dimension) no expert is named by more than 8 tokens, and in every draw some expert is named by exactly 8 of them.
All inputs are finite; a program needn't handle non-finite values.
Results may differ from a plain program's by a relative error of at most 0.015.
Values may be sent and summed in bfloat16 or wider, within the bound.
No kernel may reach another device: no remote copies, remote signals or barrier semaphores. Data moves between devices by JAX's collectives and lax.ppermute only.
A program may use at most 32 MiB of HBM per device.

v0:
```python
import jax
import jax.numpy as jnp
from jax import lax
from jax.sharding import PartitionSpec as P


def shifted(x, axis, by):
    length = lax.axis_size(axis)
    return lax.ppermute(x, axis, [(i, (i + by) % length) for i in range(length)])


def slot_grad(slot_rows, slot_share, kept_acts, gate_mat, up_mat, down_mat):
    contract = (((1,), (1,)), ((), ()))
    hidden_grad = lax.dot_general(slot_rows, down_mat, contract, preferred_element_type=jnp.float32)
    hidden_grad = hidden_grad * slot_share.astype(jnp.float32)[:, None]
    width = gate_mat.shape[1]
    pre_gate = kept_acts[:, :width].astype(jnp.float32)
    pre_up = kept_acts[:, width:].astype(jnp.float32)
    gate_sig = jax.nn.sigmoid(pre_gate)
    up_grad = (hidden_grad * pre_gate * gate_sig).astype(jnp.bfloat16)
    gate_grad = (hidden_grad * pre_up * gate_sig * (1.0 + pre_gate * (1.0 - gate_sig))).astype(
        jnp.bfloat16
    )
    summed = lax.dot_general(gate_grad, gate_mat, contract, preferred_element_type=jnp.float32)
    summed = summed + lax.dot_general(up_grad, up_mat, contract, preferred_element_type=jnp.float32)
    return summed.astype(jnp.bfloat16)


def route_tables(route_ids, route_probs, experts):
    matches = route_ids[:, :, None] == jnp.arange(experts, dtype=jnp.int32)[None, None, :]
    member = jnp.any(matches, axis=1).astype(jnp.int32)
    shares = jnp.sum(jnp.where(matches, route_probs.astype(jnp.float32)[:, :, None], 0.0), axis=1)
    return (member, shares)


def slot_table(member, capacity):
    earlier = jnp.cumsum(member, axis=0) - member
    places = jnp.arange(capacity, dtype=jnp.int32)[None, None, :]
    return (member[:, :, None] * (earlier[:, :, None] == places)).astype(jnp.bfloat16)


def body(cotangent, expert_ids, gate_probs, saved, w_gate, w_up, w_down):
    experts = lax.axis_size("expert")
    capacity = saved.shape[2] // experts
    incoming = shifted(cotangent[0], "section", -1)
    gate_mat = w_gate[0]
    up_mat = w_up[0]
    down_mat = w_down[0]
    kept_acts = saved[0, 0]
    member, shares = route_tables(expert_ids[0], gate_probs[0], experts)
    slot_map = slot_table(member, capacity)
    send_rows = jnp.einsum(
        "tec,td->ecd", slot_map, incoming, preferred_element_type=jnp.float32
    ).astype(jnp.bfloat16)
    send_share = jnp.einsum("tec,te->ec", slot_map.astype(jnp.float32), shares).astype(jnp.bfloat16)
    recv_rows, recv_share = (
        lax.all_to_all(send_rows, "expert", split_axis=0, concat_axis=0, tiled=True),
        lax.all_to_all(send_share, "expert", split_axis=0, concat_axis=0, tiled=True),
    )
    slot_grads = slot_grad(
        recv_rows.reshape(experts * capacity, -1),
        recv_share.reshape(-1),
        kept_acts,
        gate_mat,
        up_mat,
        down_mat,
    )
    returned = lax.all_to_all(
        slot_grads.reshape(experts, capacity, -1), "expert", split_axis=0, concat_axis=0, tiled=True
    )
    total = jnp.einsum("tec,ecd->td", slot_map, returned, preferred_element_type=jnp.float32)
    result = total.astype(jnp.bfloat16)
    return result[None]


def solution(mesh):
    in_specs = (
        P("section", "expert", None),
        P("section", "expert", None),
        P("section", "expert", None),
        P("section", "expert", None, None),
        P("expert", None, None),
        P("expert", None, None),
        P("expert", None, None),
    )
    out_specs = P("section", "expert", None)
    return jax.shard_map(body, mesh=mesh, in_specs=in_specs, out_specs=out_specs, check_vma=False)
```

profile of v0, /device:TPU:38, one launch (start us, length us, event | category | flops | bytes accessed | tf_op | source)
XLA Modules:
  0.0 167.2 jit_solution(113114613642292895)
XLA Ops:
  0.0 0.0 copy-start
  0.0 0.8 bitcast_convert_fusion
  0.8 0.1 copy.27
  0.9 0.8 copy.25
  1.7 0.1 fusion.38
  1.8 0.1 select_reduce_fusion
  2.0 0.7 copy.28
  2.7 15.4 %all-to-all-start.1 = ((bf16[32,1,8]{2,1,0:T(2,128)(2,1)}), bf16[32,1,8]{2,1,0:T(2,128)(2,1)S(1)}, u32[]{:S(2)}, u32[]{:S(2)}) async-start(bf16[32,1,8]{2,1,0:T(2,128)(2,1)} %copy.28), calls=%async_computation.1 | async-start | bytes 32768 | tf_op jit(solution)/shard_map/all_to_all | solution.py:58
  18.2 14.6 %collective-permute-start = (bf16[16,2048]{1,0:T(8,128)(2,1)}, bf16[16,2048]{1,0:T(8,128)(2,1)S(1)}, u32[]{:S(2)}, u32[]{:S(2)}) collective-permute-start(bf16[16,2048]{1,0:T(8,128)(2,1)} %bitcast.51), channel_id=1, source_target_pairs={{0,992},{32,0},{64,32},{96,64},{128,96},{160,128},{192,160},{224,1... | collective-permute-start | bytes 196616 | tf_op jit(solution)/shard_map/ppermute | solution.py:9
  32.8 0.1 copy.26
  32.9 2.1 %collective-permute-done = bf16[16,2048]{1,0:T(8,128)(2,1)S(1)} collective-permute-done((bf16[16,2048]{1,0:T(8,128)(2,1)}, bf16[16,2048]{1,0:T(8,128)(2,1)S(1)}, u32[]{:S(2)}, u32[]{:S(2)}) %collective-permute-start) | collective-permute-done | bytes 65568 | tf_op jit(solution)/shard_map/ppermute | solution.py:9
  35.0 1.4 convolution_convert_fusion
  36.5 0.0 all-to-all-done.1
  36.5 12.8 %all-to-all-start = ((bf16[32,8,2048]{2,1,0:T(8,128)(2,1)}), bf16[32,8,2048]{2,1,0:T(8,128)(2,1)}, u32[]{:S(2)}, u32[]{:S(2)}) async-start(bf16[32,8,2048]{2,1,0:T(8,128)(2,1)} %convolution_convert_fusion), calls=%async_computation | async-start | bytes 2097152 | tf_op jit(solution)/shard_map/all_to_all | solution.py:57
  49.2 0.1 convert_reduce_fusion
  49.3 0.1 reshape.42
  49.4 52.7 %all-to-all-done = bf16[32,8,2048]{2,1,0:T(8,128)(2,1)} async-done(((bf16[32,8,2048]{2,1,0:T(8,128)(2,1)}), bf16[32,8,2048]{2,1,0:T(8,128)(2,1)}, u32[]{:S(2)}, u32[]{:S(2)}) %all-to-all-start) | async-done | bytes 1048608 | tf_op jit(solution)/shard_map/all_to_all | solution.py:57
  102.0 0.0 copy-start.2
  102.0 3.3 %fusion.17 = f32[256,768]{1,0:T(8,128)S(1)} fusion(bf16[1,768,2048]{2,1,0:T(8,128)(2,1)} %param.13, bf16[32,8,2048]{2,1,0:T(8,128)(2,1)} %all-to-all-done, f32[256]{0:T(256)S(1)} %reshape.42), kind=kOutput, calls=%fused_computation.13 | convolution fusion | flops 805502976 | bytes 4981760 | tf_op jit(solution)/shard_map/dot_general | solution.py:14
  105.3 0.0 copy-done
  105.4 0.0 copy-done.2
  105.4 0.0 copy-start.1
  105.4 1.0 fusion
  106.4 0.9 copy-done.1
  107.3 1.1 fusion.12
  108.4 57.5 %all_to_all.19 = bf16[32,8,2048]{2,1,0:T(8,128)(2,1)S(1)} all-to-all(bf16[32,8,2048]{2,1,0:T(8,128)(2,1)S(1)} %fusion.12), channel_id=1, replica_groups=mesh['section'=32,'expert'=32] {'expert'}, dimensions={0} | all-to-all | bytes 2097152 | tf_op jit(solution)/shard_map/all_to_all | solution.py:68
  165.9 1.3 fusion.16
  (5 shorter events, 0.1 us)
Async XLA Ops:
  0.0 105.3 %copy-start = (bf16[1,2048,768]{2,1,0:T(8,128)(2,1)S(1)}, bf16[1,2048,768]{2,1,0:T(8,128)(2,1)}, u32[]{:S(2)}) copy-start(bf16[1,2048,768]{2,1,0:T(8,128)(2,1)} %param.12) | copy-start | bytes 9437188
  2.7 33.7 %all-to-all-start.1 = ((bf16[32,1,8]{2,1,0:T(2,128)(2,1)}), bf16[32,1,8]{2,1,0:T(2,128)(2,1)S(1)}, u32[]{:S(2)}, u32[]{:S(2)}) async-start(bf16[32,1,8]{2,1,0:T(2,128)(2,1)} %copy.28), calls=%async_computation.1 | async-start | bytes 32768 | tf_op jit(solution)/shard_map/all_to_all | solution.py:58
  18.2 16.8 %collective-permute-start = (bf16[16,2048]{1,0:T(8,128)(2,1)}, bf16[16,2048]{1,0:T(8,128)(2,1)S(1)}, u32[]{:S(2)}, u32[]{:S(2)}) collective-permute-start(bf16[16,2048]{1,0:T(8,128)(2,1)} %bitcast.51), channel_id=1, source_target_pairs={{0,992},{32,0},{64,32},{96,64},{128,96},{160,128},{192,160},{224,1... | collective-permute-start | bytes 196616 | tf_op jit(solution)/shard_map/ppermute | solution.py:9
  36.5 65.6 %all-to-all-start = ((bf16[32,8,2048]{2,1,0:T(8,128)(2,1)}), bf16[32,8,2048]{2,1,0:T(8,128)(2,1)}, u32[]{:S(2)}, u32[]{:S(2)}) async-start(bf16[32,8,2048]{2,1,0:T(8,128)(2,1)} %convolution_convert_fusion), calls=%async_computation | async-start | bytes 2097152 | tf_op jit(solution)/shard_map/all_to_all | solution.py:57
  102.0 3.3 %copy-start.2 = (bf16[1,1,256,1536]{3,2,1,0:T(8,128)(2,1)S(1)}, bf16[1,1,256,1536]{3,2,1,0:T(8,128)(2,1)}, u32[]{:S(2)}) copy-start(bf16[1,1,256,1536]{3,2,1,0:T(8,128)(2,1)} %param.10) | copy-start | bytes 2359300
  105.4 1.9 %copy-start.1 = (bf16[1,2048,768]{2,1,0:T(8,128)(2,1)S(1)}, bf16[1,2048,768]{2,1,0:T(8,128)(2,1)}, u32[]{:S(2)}) copy-start(bf16[1,2048,768]{2,1,0:T(8,128)(2,1)} %param.11) | copy-start | bytes 9437188
where the time goes:
time: 168 us; the launch traced here: 167 us
  blocking collectives  57.5 us (34%)
  waiting for transfers between devices  54.7 us (33%)
  starting transfers between devices  42.8 us (25%)
  matrix products  8.21 us (5%)
  local copies, waits for them, and re-layouts  2.64 us (2%)
    all_to_all x1, blocking collectives, body(): lax.all_to_all(slot_grads.reshape(experts, capacity, -1), 'expert', split...  57.5 us
    all_to_all x1, waiting for transfers between devices, body(): lax.all_to_all(send_rows, 'expert', split_axis=0, concat_axis=0, tiled=True)  52.7 us
    all_to_all x1, starting transfers between devices, body(): lax.all_to_all(send_share, 'expert', split_axis=0, concat_axis=0, tiled=T...  15.4 us
    ppermute x1, starting transfers between devices, shifted(): lax.ppermute(x, axis, [(i, (i + by) % length) for i in range(length)])  14.6 us
    all_to_all x1, starting transfers between devices, body(): lax.all_to_all(send_rows, 'expert', split_axis=0, concat_axis=0, tiled=True)  12.8 us
  transfers between devices with their start and end apart: 3, of which 2 were waited for; matrix products, arithmetic and copies ran while one was open for 1% of the time, Pallas kernels for 0%

commit v1 on v0

v1 whole, which is shorter than its diff:
```python
import jax
import jax.numpy as jnp
from jax import lax
from jax.experimental import pallas as pl
from jax.experimental.pallas import tpu as pltpu
from jax.sharding import Mesh, PartitionSpec as P

BF = jnp.bfloat16
F32 = jnp.float32
YS = 4
ZS = 8


def call(kernel, outs, limit, cost):
    return pl.pallas_call(
        kernel,
        out_shape=outs,
        compiler_params=pltpu.CompilerParams(vmem_limit_bytes=limit),
        cost_estimate=pl.CostEstimate(flops=cost[0], bytes_accessed=cost[1], transcendentals=0),
    )


def iota(shape, dim):
    return lax.broadcasted_iota(jnp.int32, shape, dim)


def shares_kernel(ids_ref, probs_ref, out_ref):
    rows, tokens = out_ref.shape
    r = iota((rows, tokens), 0)
    expert = (r % YS) * ZS + r // YS
    acc = jnp.zeros((rows, tokens), F32)
    for k in range(ids_ref.shape[0]):
        acc = acc + jnp.where(ids_ref[k : k + 1, :] == expert, probs_ref[k : k + 1, :].astype(F32), 0.0)
    out_ref[...] = acc.astype(BF)


def dot(a, b, dims=((1,), (0,))):
    return lax.dot_general(a, b, (dims, ((), ())), preferred_element_type=F32)


def maps_kernel(cap, share_ref, pick_ref, give_ref):
    slots, toks = pick_ref.shape
    rows, own = share_ref.shape
    share = share_ref[...]
    r = iota((slots, rows), 0)
    k = iota((slots, rows), 1)
    place = ((r // cap) % ZS) * YS + r // (cap * ZS)
    spread_rows = jnp.where(place == k, 1.0, 0.0).astype(BF)
    per_slot = dot(spread_rows, share)
    member = jnp.where(per_slot > 0, 1.0, 0.0).astype(BF)
    before = jnp.where(iota((own, own), 0) < iota((own, own), 1), 1.0, 0.0).astype(BF)
    earlier = dot(member, before)
    spread = jnp.where(iota((own, toks), 0) == iota((own, toks), 1) % own, 1.0, 0.0).astype(BF)
    share_at = dot(per_slot.astype(BF), spread)
    earlier_at = dot(earlier.astype(BF), spread)
    rr = iota((slots, toks), 0)
    tt = iota((slots, toks), 1)
    hit = (share_at > 0) & (tt // own == (rr // cap) % ZS) & (earlier_at == (rr % cap).astype(F32))
    pick_ref[...] = jnp.where(hit, 1.0, 0.0).astype(BF)
    give_ref[...] = jnp.where(hit, share_at, 0.0).astype(BF)


def compress_kernel(pick_ref, rows_ref, out_ref):
    out_ref[...] = dot(pick_ref[...], rows_ref[...]).astype(BF)


def combine_kernel(give_ref, rows_ref, out_ref):
    out_ref[...] = dot(give_ref[...], rows_ref[...], ((0,), (0,))).astype(BF)


def expert_kernel(rows_ref, kept_ref, gate_ref, up_ref, down_ref, out_ref):
    width = gate_ref.shape[1]
    hidden = dot(rows_ref[...], down_ref[...], ((1,), (1,)))
    g = kept_ref[:, :width].astype(F32)
    u = kept_ref[:, width:].astype(F32)
    s = jax.nn.sigmoid(g)
    hs = hidden * s
    up_grad = (hs * g).astype(BF)
    gate_grad = (hs * u * (1.0 + g * (1.0 - s))).astype(BF)
    total = dot(gate_grad, gate_ref[...], ((1,), (1,))) + dot(up_grad, up_ref[...], ((1,), (1,)))
    out_ref[...] = total.astype(BF)


def total_kernel(parts_ref, out_ref):
    acc = parts_ref[0].astype(F32)
    for k in range(1, parts_ref.shape[0]):
        acc = acc + parts_ref[k].astype(F32)
    out_ref[...] = acc.astype(BF)


def body(cotangent, expert_ids, gate_probs, saved, w_gate, w_up, w_down):
    sections = lax.axis_size("section")
    tokens, width = cotangent.shape[1:]
    slots = saved.shape[2]
    cap = slots // (YS * ZS)
    mib = 1 << 20
    incoming = lax.ppermute(cotangent[0], "section", [(i, (i - 1) % sections) for i in range(sections)])
    shares = call(shares_kernel, jax.ShapeDtypeStruct((YS * ZS, tokens), BF), 4 * mib, (10**5, 10**4))(
        expert_ids[0].T, gate_probs[0].T
    )
    shares = lax.all_to_all(shares.reshape(ZS, YS, tokens), "z", 0, 0, tiled=True)
    map_shape = jax.ShapeDtypeStruct((slots, ZS * tokens), BF)
    pick, give = call(
        lambda *refs: maps_kernel(cap, *refs), (map_shape, map_shape), 8 * mib, (10**7, 10**5)
    )(shares.reshape(ZS * YS, tokens))
    spread = jnp.broadcast_to(incoming[None], (ZS, tokens, width))
    row_tokens = lax.all_to_all(spread, "z", 0, 0, tiled=True).reshape(ZS * tokens, width)
    sent = call(compress_kernel, jax.ShapeDtypeStruct((slots, width), BF), 8 * mib, (10**8, 10**6))(pick, row_tokens)
    slot_rows = lax.all_to_all(sent.reshape(YS, -1, width), "y", 0, 0, tiled=True).reshape(slots, width)
    grads = call(expert_kernel, jax.ShapeDtypeStruct((slots, width), BF), 16 * mib, (24 * 10**8, 11 * 10**6))(
        slot_rows, saved[0, 0], w_gate[0], w_up[0], w_down[0]
    )
    back = lax.all_to_all(grads.reshape(YS, -1, width), "y", 0, 0, tiled=True).reshape(slots, width)
    partial = call(combine_kernel, jax.ShapeDtypeStruct((ZS * tokens, width), BF), 8 * mib, (10**8, 10**6))(give, back)
    parts = lax.all_to_all(partial.reshape(ZS, tokens, width), "z", 0, 0, tiled=True)
    out = call(total_kernel, jax.ShapeDtypeStruct((tokens, width), BF), 4 * mib, (10**6, 10**6))(parts)
    return out[None]


def solution(mesh):
    split = Mesh(mesh.devices.reshape(-1, YS, ZS), ("section", "y", "z"))
    over = P("section", ("y", "z"), None)
    weight = P(("y", "z"), None, None)
    in_specs = (over, over, over, P("section", ("y", "z"), None, None), weight, weight, weight)
    return jax.shard_map(body, mesh=split, in_specs=in_specs, out_specs=over, check_vma=False)
```

time: 168 us -> 134 us (0.80)
  the two profiles are of different devices: /device:TPU:38 before, /device:TPU:256 now
where the time goes in v1:
time: 134 us
  blocking collectives  87.4 us (65%)
  waiting for transfers between devices  27.8 us (21%)
  Pallas kernels  6.41 us (5%)
  starting transfers between devices  6.31 us (5%)
  local copies, waits for them, and re-layouts  5.98 us (4%)
    all_to_all x1, blocking collectives, body(): lax.all_to_all(partial.reshape(ZS, tokens, width), 'z', 0, 0, tiled=True)  36.1 us
    all_to_all x1, waiting for transfers between devices, body(): lax.all_to_all(spread, 'z', 0, 0, tiled=True).reshape(ZS * tokens, width)  27.8 us
    all_to_all x1, blocking collectives, body(): lax.all_to_all(shares.reshape(ZS, YS, tokens), 'z', 0, 0, tiled=True)  22.8 us
    all_to_all x1, blocking collectives, body(): lax.all_to_all(sent.reshape(YS, -1, width), 'y', 0, 0, tiled=True)  15.2 us
    all_to_all x1, blocking collectives, body(): lax.all_to_all(grads.reshape(YS, -1, width), 'y', 0, 0, tiled=True)  13.3 us
    unnamed x12, local copies, waits for them, and re-layouts  5.15 us
    all_to_all x1, starting transfers between devices, body(): lax.all_to_all(spread, 'z', 0, 0, tiled=True).reshape(ZS * tokens, width)  4.14 us
    pallas_call x1, Pallas kernels, body(): call(expert_kernel, jax.ShapeDtypeStruct((slots, width), BF), 16 * mib, (...  3.42 us
  transfers between devices with their start and end apart: 2, of which 1 were waited for; matrix products, arithmetic and copies ran while one was open for 0% of the time, Pallas kernels for 0%

profile of v1, /device:TPU:256, one launch (start us, length us, event | category | flops | bytes accessed | tf_op | source)
XLA Modules:
  0.0 134.0 jit_solution(17718645486227934941)
XLA Ops:
  0.0 0.0 copy-start
  0.0 2.2 %collective-permute-start = (bf16[16,2048]{1,0:T(8,128)(2,1)}, bf16[16,2048]{1,0:T(8,128)(2,1)S(1)}, u32[]{:S(2)}, u32[]{:S(2)}) collective-permute-start(bf16[16,2048]{1,0:T(8,128)(2,1)} %bitcast.33), channel_id=1, source_target_pairs={{0,992},{32,0},{64,32},{96,64},{128,96},{160,128},{192,160},{224,1... | collective-permute-start | bytes 196616 | tf_op jit(solution)/shard_map/ppermute | solution.py:97
  2.2 0.0 copy-start.4
  2.2 0.7 copy-done.4
  2.9 0.0 copy-start.5
  2.9 0.7 copy-done.5
  3.6 22.8 %all_to_all.25 = bf16[8,4,16]{2,1,0:T(4,128)(2,1)S(1)} all-to-all(bf16[8,4,16]{2,1,0:T(4,128)(2,1)S(1)} %bitcast.29), channel_id=1, replica_groups=mesh['section'=32,'y'=4,'z'=8] {'z'}, dimensions={0} | all-to-all | bytes 2048 | tf_op jit(solution)/shard_map/all_to_all | solution.py:101
  26.3 0.0 collective-permute-done
  26.3 0.8 broadcast_in_dim.4
  27.2 4.1 %all-to-all-start.1 = ((bf16[8,16,2048]{2,1,0:T(8,128)(2,1)}), bf16[8,16,2048]{2,1,0:T(8,128)(2,1)}, u32[]{:S(2)}, u32[]{:S(2)}) async-start(bf16[8,16,2048]{2,1,0:T(8,128)(2,1)} %broadcast_in_dim.4), calls=%async_computation.1 | async-start | bytes 1048576 | tf_op jit(solution)/shard_map/all_to_all | solution.py:107
  31.3 0.4 shard_map.74
  31.7 27.8 %all-to-all-done.1 = bf16[8,16,2048]{2,1,0:T(8,128)(2,1)} async-done(((bf16[8,16,2048]{2,1,0:T(8,128)(2,1)}), bf16[8,16,2048]{2,1,0:T(8,128)(2,1)}, u32[]{:S(2)}, u32[]{:S(2)}) %all-to-all-start.1) | async-done | bytes 524320 | tf_op jit(solution)/shard_map/all_to_all | solution.py:107
  59.6 0.0 copy-start.3
  59.6 1.5 %shard_map.75 = bf16[256,2048]{1,0:T(8,128)(2,1)S(1)} custom-call(bf16[256,128]{1,0:T(8,128)(2,1)S(1)} %get-tuple-element.8.pick_ref, bf16[128,2048]{1,0:T(8,128)(2,1)} %bitcast.7.rows_ref), custom_call_target="tpu_custom_call" | custom-call | flops 100000000 | bytes 1000000 | tf_op jit(solution)/shard_map/pallas_call | solution.py:108
  61.1 15.2 %all_to_all.26 = bf16[4,64,2048]{2,1,0:T(8,128)(2,1)S(1)} all-to-all(bf16[4,64,2048]{2,1,0:T(8,128)(2,1)S(1)} %bitcast.23), channel_id=1, replica_groups=mesh['section'=32,'y'=4,'z'=8] {'y'}, dimensions={0} | all-to-all | bytes 2097152 | tf_op jit(solution)/shard_map/all_to_all | solution.py:109
  76.3 0.0 copy-done
  76.3 0.0 copy-done.3
  76.3 0.0 copy-start.1
  76.3 1.9 %copy-done.1 = bf16[1,2048,768]{2,1,0:T(8,128)(2,1)S(1)} copy-done((bf16[1,2048,768]{2,1,0:T(8,128)(2,1)S(1)}, bf16[1,2048,768]{2,1,0:T(8,128)(2,1)}, u32[]{:S(2)}) %copy-start.1) | copy-done | bytes 3145752
  78.2 0.0 copy-start.2
  78.2 1.9 %copy-done.2 = bf16[1,768,2048]{2,1,0:T(8,128)(2,1)S(1)} copy-done((bf16[1,768,2048]{2,1,0:T(8,128)(2,1)S(1)}, bf16[1,768,2048]{2,1,0:T(8,128)(2,1)}, u32[]{:S(2)}) %copy-start.2) | copy-done | bytes 3145752
  80.0 3.4 %shard_map.76 = bf16[256,2048]{1,0:T(8,128)(2,1)S(1)} custom-call(bf16[256,2048]{1,0:T(8,128)(2,1)S(1)} %bitcast.20, bf16[256,1536]{1,0:T(8,128)(2,1)S(1)} %bitcast.28, bf16[2048,768]{1,0:T(8,128)(2,1)S(1)} %bitcast.24, bf16[2048,768]{1,0:T(8,128)(2,1)S(1)} %bitcast.25, bf16[768,2048]{1,0:T(8,128)(2,1)S(1)} %bitcast.26), custom_call_target="tpu_custom_call" | custom-call | flops 2400000000 | bytes 11000000 | tf_op jit(solution)/shard_map/pallas_call | solution.py:110
  83.5 13.3 %all_to_all.27 = bf16[4,64,2048]{2,1,0:T(8,128)(2,1)S(1)} all-to-all(bf16[4,64,2048]{2,1,0:T(8,128)(2,1)S(1)} %bitcast.21), channel_id=1, replica_groups=mesh['section'=32,'y'=4,'z'=8] {'y'}, dimensions={0} | all-to-all | bytes 2097152 | tf_op jit(solution)/shard_map/all_to_all | solution.py:113
  96.8 0.3 shard_map.77
  97.1 36.1 %all_to_all.28.parts_ref = bf16[8,16,2048]{2,1,0:T(8,128)(2,1)S(1)} all-to-all(bf16[8,16,2048]{2,1,0:T(8,128)(2,1)S(1)} %bitcast.27), channel_id=1, replica_groups=mesh['section'=32,'y'=4,'z'=8] {'z'}, dimensions={0} | all-to-all | bytes 1048576 | tf_op jit(solution)/shard_map/all_to_all | solution.py:115
  133.3 0.7 shard_map.78
  (1 shorter events, 0.0 us)
Async XLA Ops:
  0.0 76.3 %copy-start = (bf16[1,2048,768]{2,1,0:T(8,128)(2,1)S(1)}, bf16[1,2048,768]{2,1,0:T(8,128)(2,1)}, u32[]{:S(2)}) copy-start(bf16[1,2048,768]{2,1,0:T(8,128)(2,1)} %param.11) | copy-start | bytes 9437188
  0.0 26.3 %collective-permute-start = (bf16[16,2048]{1,0:T(8,128)(2,1)}, bf16[16,2048]{1,0:T(8,128)(2,1)S(1)}, u32[]{:S(2)}, u32[]{:S(2)}) collective-permute-start(bf16[16,2048]{1,0:T(8,128)(2,1)} %bitcast.33), channel_id=1, source_target_pairs={{0,992},{32,0},{64,32},{96,64},{128,96},{160,128},{192,160},{224,1... | collective-permute-start | bytes 196616 | tf_op jit(solution)/shard_map/ppermute | solution.py:97
  2.2 0.7 copy-start.4
  2.9 0.7 copy-start.5
  27.2 32.4 %all-to-all-start.1 = ((bf16[8,16,2048]{2,1,0:T(8,128)(2,1)}), bf16[8,16,2048]{2,1,0:T(8,128)(2,1)}, u32[]{:S(2)}, u32[]{:S(2)}) async-start(bf16[8,16,2048]{2,1,0:T(8,128)(2,1)} %broadcast_in_dim.4), calls=%async_computation.1 | async-start | bytes 1048576 | tf_op jit(solution)/shard_map/all_to_all | solution.py:107
  59.6 16.7 %copy-start.3 = (bf16[1,1,256,1536]{3,2,1,0:T(8,128)(2,1)S(1)}, bf16[1,1,256,1536]{3,2,1,0:T(8,128)(2,1)}, u32[]{:S(2)}) copy-start(bf16[1,1,256,1536]{3,2,1,0:T(8,128)(2,1)} %param.10) | copy-start | bytes 2359300
  76.3 1.9 %copy-start.1 = (bf16[1,2048,768]{2,1,0:T(8,128)(2,1)S(1)}, bf16[1,2048,768]{2,1,0:T(8,128)(2,1)}, u32[]{:S(2)}) copy-start(bf16[1,2048,768]{2,1,0:T(8,128)(2,1)} %param.12) | copy-start | bytes 9437188
  78.2 1.9 %copy-start.2 = (bf16[1,768,2048]{2,1,0:T(8,128)(2,1)S(1)}, bf16[1,768,2048]{2,1,0:T(8,128)(2,1)}, u32[]{:S(2)}) copy-start(bf16[1,768,2048]{2,1,0:T(8,128)(2,1)} %param.13) | copy-start | bytes 9437188

commit v2 on v1

v2 whole, which is shorter than its diff:
```python
import jax
import jax.numpy as jnp
from jax import lax
from jax.experimental import pallas as pl
from jax.experimental.pallas import tpu as pltpu
from jax.sharding import Mesh, PartitionSpec as P

BF = jnp.bfloat16
F32 = jnp.float32
YS = 4
ZS = 8
QUAD = 4


def call(kernel, outs, limit, cost):
    return pl.pallas_call(
        kernel,
        out_shape=outs,
        compiler_params=pltpu.CompilerParams(vmem_limit_bytes=limit),
        cost_estimate=pl.CostEstimate(flops=cost[0], bytes_accessed=cost[1], transcendentals=0),
    )


def iota(shape, dim):
    return lax.broadcasted_iota(jnp.int32, shape, dim)


def shares_kernel(ids_ref, probs_ref, out_ref):
    rows, tokens = out_ref.shape
    r = iota((rows, tokens), 0)
    expert = (r % YS) * ZS + r // YS
    acc = jnp.zeros((rows, tokens), F32)
    for k in range(ids_ref.shape[0]):
        acc = acc + jnp.where(ids_ref[k : k + 1, :] == expert, probs_ref[k : k + 1, :].astype(F32), 0.0)
    out_ref[...] = acc.astype(BF)


def dot(a, b, dims=((1,), (0,))):
    return lax.dot_general(a, b, (dims, ((), ())), preferred_element_type=F32)


def maps_kernel(cap, share_ref, pick_ref, give_ref):
    slots, toks = pick_ref.shape
    rows, own = share_ref.shape
    share = share_ref[...]
    r = iota((slots, rows), 0)
    k = iota((slots, rows), 1)
    place = ((r // cap) % ZS) * YS + r // (cap * ZS)
    spread_rows = jnp.where(place == k, 1.0, 0.0).astype(BF)
    per_slot = dot(spread_rows, share)
    member = jnp.where(per_slot > 0, 1.0, 0.0).astype(BF)
    before = jnp.where(iota((own, own), 0) < iota((own, own), 1), 1.0, 0.0).astype(BF)
    earlier = dot(member, before)
    spread = jnp.where(iota((own, toks), 0) == iota((own, toks), 1) % own, 1.0, 0.0).astype(BF)
    share_at = dot(per_slot.astype(BF), spread)
    earlier_at = dot(earlier.astype(BF), spread)
    rr = iota((slots, toks), 0)
    block = iota((slots, toks), 1) // own
    mine = lax.axis_index("zh") * QUAD
    block_z = jnp.where(block < QUAD, mine + block, (ZS - QUAD - mine) + (block - QUAD))
    hit = (share_at > 0) & (block_z == (rr // cap) % ZS) & (earlier_at == (rr % cap).astype(F32))
    pick_ref[...] = jnp.where(hit, 1.0, 0.0).astype(BF)
    give_ref[...] = jnp.where(hit, share_at, 0.0).astype(BF)


def compress_kernel(pick_ref, mine_ref, other_ref, out_ref):
    half = mine_ref.shape[0]
    out_ref[...] = (dot(pick_ref[:, :half], mine_ref[...]) + dot(pick_ref[:, half:], other_ref[...])).astype(BF)


def combine_kernel(give_ref, rows_ref, mine_ref, other_ref):
    half = mine_ref.shape[0]
    rows = rows_ref[...]
    other_ref[...] = dot(give_ref[:, half:], rows, ((0,), (0,))).astype(BF)
    mine_ref[...] = dot(give_ref[:, :half], rows, ((0,), (0,))).astype(BF)


def expert_kernel(rows_ref, kept_hbm, gate_hbm, up_hbm, down_hbm, out_ref, kept, gate, up, down, hidden, sems):
    ff, width = down.shape
    copies = []

    def fetch(src, dst, parts):
        step = src.shape[0] // parts
        begun = []
        for k in range(parts):
            rows = pl.ds(k * step, step)
            copy = pltpu.make_async_copy(src.at[rows], dst.at[rows], sems.at[len(copies)])
            copy.start()
            copies.append(copy)
            begun.append((copy, rows))
        return begun

    down_parts = fetch(down_hbm, down, 3)
    kept_parts = fetch(kept_hbm, kept, 1)
    pairs = []
    step = width // 4
    for k in range(4):
        rows = pl.ds(k * step, step)
        for src, dst in ((gate_hbm, gate), (up_hbm, up)):
            copy = pltpu.make_async_copy(src.at[rows], dst.at[rows], sems.at[len(copies)])
            copy.start()
            copies.append(copy)
            pairs.append(copy)
    rows = rows_ref[...]
    for copy, part in down_parts:
        copy.wait()
        hidden[:, part] = dot(rows, down[part, :], ((1,), (1,)))
    for copy, _ in kept_parts:
        copy.wait()
    h = hidden[...]
    g = kept[:, :ff].astype(F32)
    u = kept[:, ff:].astype(F32)
    s = jax.nn.sigmoid(g)
    hs = h * s
    up_grad = (hs * g).astype(BF)
    gate_grad = (hs * u * (1.0 + g * (1.0 - s))).astype(BF)
    for k in range(4):
        pairs[2 * k].wait()
        pairs[2 * k + 1].wait()
        part = pl.ds(k * step, step)
        total = dot(gate_grad, gate[part, :], ((1,), (1,))) + dot(up_grad, up[part, :], ((1,), (1,)))
        out_ref[:, part] = total.astype(BF)


def sum_of(parts_ref):
    acc = parts_ref[0].astype(F32)
    for k in range(1, parts_ref.shape[0]):
        acc = acc + parts_ref[k].astype(F32)
    return acc


def half_kernel(parts_ref, out_ref):
    out_ref[...] = sum_of(parts_ref).astype(BF)


def total_kernel(parts_ref, far_ref, out_ref):
    out_ref[...] = (sum_of(parts_ref) + far_ref[...].astype(F32)).astype(BF)


def swapped(x):
    return lax.ppermute(x, "zh", [(0, 1), (1, 0)])


def quad(x):
    return lax.all_to_all(x, "zl", 0, 0, tiled=True)


def body(cotangent, expert_ids, gate_probs, saved, w_gate, w_up, w_down):
    sections = lax.axis_size("section")
    tokens, width = cotangent.shape[1:]
    slots = saved.shape[2]
    cap = slots // (YS * ZS)
    half = QUAD * tokens
    mib = 1 << 20
    incoming = lax.ppermute(cotangent[0], "section", [(i, (i - 1) % sections) for i in range(sections)])
    shares = call(shares_kernel, jax.ShapeDtypeStruct((YS * ZS, tokens), BF), 4 * mib, (10**5, 10**4))(
        expert_ids[0].T, gate_probs[0].T
    )
    shares = lax.all_to_all(shares.reshape(ZS, YS, tokens), ("zh", "zl"), 0, 0, tiled=True)
    map_shape = jax.ShapeDtypeStruct((slots, ZS * tokens), BF)
    pick, give = call(
        lambda *refs: maps_kernel(cap, *refs), (map_shape, map_shape), 8 * mib, (10**7, 10**5)
    )(shares.reshape(ZS * YS, tokens))
    crossed = swapped(incoming)
    mine = quad(jnp.broadcast_to(incoming[None], (QUAD, tokens, width)))
    other = quad(jnp.broadcast_to(crossed[None], (QUAD, tokens, width)))
    sent = call(compress_kernel, jax.ShapeDtypeStruct((slots, width), BF), 8 * mib, (10**8, 10**6))(
        pick, mine.reshape(half, width), other.reshape(half, width)
    )
    slot_rows = lax.all_to_all(sent.reshape(YS, -1, width), "y", 0, 0, tiled=True).reshape(slots, width)
    arrays = (saved[0, 0], w_gate[0], w_up[0], w_down[0])
    vm = pl.BlockSpec(memory_space=pltpu.VMEM)
    grads = pl.pallas_call(
        expert_kernel,
        out_shape=jax.ShapeDtypeStruct((slots, width), BF),
        in_specs=[vm] + [pl.BlockSpec(memory_space=pltpu.HBM)] * 4,
        out_specs=vm,
        scratch_shapes=[pltpu.VMEM(x.shape, x.dtype) for x in arrays]
        + [pltpu.VMEM((slots, w_down.shape[1]), F32), pltpu.SemaphoreType.DMA((12,))],
        compiler_params=pltpu.CompilerParams(vmem_limit_bytes=48 * mib),
        cost_estimate=pl.CostEstimate(flops=24 * 10**8, bytes_accessed=12 * 10**6, transcendentals=0),
    )(slot_rows, *arrays)
    back = lax.all_to_all(grads.reshape(YS, -1, width), "y", 0, 0, tiled=True).reshape(slots, width)
    half_shape = jax.ShapeDtypeStruct((half, width), BF)
    own_part, far_part = call(combine_kernel, (half_shape, half_shape), 8 * mib, (10**8, 10**6))(give, back)
    far = quad(far_part.reshape(QUAD, tokens, width))
    far = swapped(call(half_kernel, jax.ShapeDtypeStruct((tokens, width), BF), 4 * mib, (10**6, 10**6))(far))
    own = quad(own_part.reshape(QUAD, tokens, width))
    out = call(total_kernel, jax.ShapeDtypeStruct((tokens, width), BF), 4 * mib, (10**6, 10**6))(own, far)
    return out[None]


def solution(mesh):
    split = Mesh(mesh.devices.reshape(-1, YS, ZS // QUAD, QUAD), ("section", "y", "zh", "zl"))
    line = ("y", "zh", "zl")
    over = P("section", line, None)
    weight = P(line, None, None)
    in_specs = (over, over, over, P("section", line, None, None), weight, weight, weight)
    return jax.shard_map(body, mesh=split, in_specs=in_specs, out_specs=over, check_vma=False)
```

time: 134 us -> 134 us (level)
  the two profiles are of different devices: /device:TPU:256 before, /device:TPU:32 now
where the time goes in v2:
time: 134 us; the launch traced here: 133 us
  blocking collectives  53.7 us (40%)
  starting transfers between devices  45 us (34%)
  waiting for transfers between devices  19.2 us (14%)
  Pallas kernels  12.1 us (9%)
  local copies, waits for them, and re-layouts  2.82 us (2%)
    ppermute x1, starting transfers between devices, body(): lax.ppermute(cotangent[0], 'section', [(i, (i - 1) % sections) for i in r...  24 us
    all_to_all x1, blocking collectives, body(): lax.all_to_all(sent.reshape(YS, -1, width), 'y', 0, 0, tiled=True)  16.2 us
    all_to_all x1, blocking collectives, body(): lax.all_to_all(shares.reshape(ZS, YS, tokens), ('zh', 'zl'), 0, 0, tiled=...  14.9 us
    all_to_all x3, starting transfers between devices, quad(): return lax.all_to_all(x, 'zl', 0, 0, tiled=True)  14.2 us
    all_to_all x1, blocking collectives, body(): lax.all_to_all(grads.reshape(YS, -1, width), 'y', 0, 0, tiled=True)  13.3 us
    ppermute x2, waiting for transfers between devices, swapped(): return lax.ppermute(x, 'zh', [(0, 1), (1, 0)])  11.6 us
    all_to_all x1, blocking collectives, quad(): return lax.all_to_all(x, 'zl', 0, 0, tiled=True)  9.3 us
    pallas_call x1, Pallas kernels, body(): pl.pallas_call(expert_kernel, out_shape=jax.ShapeDtypeStruct((slots, widt...  7.94 us
  transfers between devices with their start and end apart: 6, of which 4 were waited for; matrix products, arithmetic and copies ran while one was open for 0% of the time, Pallas kernels for 0%

profile of v2, /device:TPU:32, one launch (start us, length us, event | category | flops | bytes accessed | tf_op | source)
XLA Modules:
  0.0 132.9 jit_solution(2231604000823975817)
XLA Ops:
  0.0 0.0 copy-start
  0.0 24.0 %collective-permute-start = (bf16[16,2048]{1,0:T(8,128)(2,1)}, bf16[16,2048]{1,0:T(8,128)(2,1)S(1)}, u32[]{:S(2)}, u32[]{:S(2)}) collective-permute-start(bf16[16,2048]{1,0:T(8,128)(2,1)} %bitcast.36), channel_id=1, source_target_pairs={{0,992},{32,0},{64,32},{96,64},{128,96},{160,128},{192,160},{224,1... | collective-permute-start | bytes 196616 | tf_op jit(solution)/shard_map/ppermute | solution.py:155
  24.0 0.0 copy-start.2
  24.0 0.7 copy-done.2
  24.7 0.0 copy-start.3
  24.7 0.7 copy-done.3
  25.4 14.9 %all_to_all.35 = bf16[8,4,16]{2,1,0:T(4,128)(2,1)S(1)} all-to-all(bf16[8,4,16]{2,1,0:T(4,128)(2,1)S(1)} %bitcast.30), channel_id=1, replica_groups=mesh['section'=32,'y'=4,'zh'=2,'zl'=4] {'zh','zl'}, dimensions={0} | all-to-all | bytes 2048 | tf_op jit(solution)/shard_map/all_to_all | solution.py:159
  40.3 0.0 collective-permute-done
  40.3 0.7 broadcast_in_dim.6
  41.0 4.8 %all-to-all-start.1 = ((bf16[4,16,2048]{2,1,0:T(8,128)(2,1)}), bf16[4,16,2048]{2,1,0:T(8,128)(2,1)S(1)}, u32[]{:S(2)}, u32[]{:S(2)}) async-start(bf16[4,16,2048]{2,1,0:T(8,128)(2,1)} %broadcast_in_dim.6), calls=%async_computation.1 | async-start | bytes 524288 | tf_op jit(solution)/shard_map/all_to_all | solution.py:145
  45.8 2.4 %collective-permute-start.1 = (bf16[16,2048]{1,0:T(8,128)(2,1)S(1)}, bf16[16,2048]{1,0:T(8,128)(2,1)S(1)}, u32[]{:S(2)}, u32[]{:S(2)}) collective-permute-start(bf16[16,2048]{1,0:T(8,128)(2,1)S(1)} %collective-permute-done), channel_id=1, source_target_pairs={{0,4},{4,0},{1,5},{5,1},{2,6},{6,2},{3,7},{7,3},{8,12},{12,8},{9,1... | collective-permute-start | bytes 196616 | tf_op jit(solution)/shard_map/ppermute | solution.py:141
  48.2 7.7 %collective-permute-done.1 = bf16[16,2048]{1,0:T(8,128)(2,1)S(1)} collective-permute-done((bf16[16,2048]{1,0:T(8,128)(2,1)S(1)}, bf16[16,2048]{1,0:T(8,128)(2,1)S(1)}, u32[]{:S(2)}, u32[]{:S(2)}) %collective-permute-start.1) | collective-permute-done | bytes 65568 | tf_op jit(solution)/shard_map/ppermute | solution.py:141
  55.9 0.0 all-to-all-done.1
  55.9 0.7 broadcast_in_dim.7
  56.6 5.1 %all-to-all-start.2 = ((bf16[4,16,2048]{2,1,0:T(8,128)(2,1)}), bf16[4,16,2048]{2,1,0:T(8,128)(2,1)}, u32[]{:S(2)}, u32[]{:S(2)}) async-start(bf16[4,16,2048]{2,1,0:T(8,128)(2,1)} %broadcast_in_dim.7), calls=%async_computation.2 | async-start | bytes 524288 | tf_op jit(solution)/shard_map/all_to_all | solution.py:145
  61.7 0.4 shard_map.74
  62.1 5.9 %all-to-all-done.2 = bf16[4,16,2048]{2,1,0:T(8,128)(2,1)} async-done(((bf16[4,16,2048]{2,1,0:T(8,128)(2,1)}), bf16[4,16,2048]{2,1,0:T(8,128)(2,1)}, u32[]{:S(2)}, u32[]{:S(2)}) %all-to-all-start.2) | async-done | bytes 262176 | tf_op jit(solution)/shard_map/all_to_all | solution.py:145
  68.0 0.0 copy-start.1
  68.0 1.8 %shard_map.75 = bf16[256,2048]{1,0:T(8,128)(2,1)S(1)} custom-call(bf16[256,128]{1,0:T(8,128)(2,1)S(1)} %get-tuple-element.10.pick_ref, bf16[64,2048]{1,0:T(8,128)(2,1)S(1)} %bitcast.27, bf16[64,2048]{1,0:T(8,128)(2,1)} %bitcast.8.other_ref), custom_call_target="tpu_custom_call" | custom-call | flops 100000000 | bytes 1000000 | tf_op jit(solution)/shard_map/pallas_call | solution.py:167
  69.8 16.2 %all_to_all.36 = bf16[4,64,2048]{2,1,0:T(8,128)(2,1)S(1)} all-to-all(bf16[4,64,2048]{2,1,0:T(8,128)(2,1)S(1)} %bitcast.25), channel_id=1, replica_groups=mesh['section'=32,'y'=4,'zh'=2,'zl'=4] {'y'}, dimensions={0} | all-to-all | bytes 2097152 | tf_op jit(solution)/shard_map/all_to_all | solution.py:170
  86.0 0.0 copy-done
  86.0 0.0 copy-done.1
  86.0 7.9 %shard_map.76 = bf16[256,2048]{1,0:T(8,128)(2,1)S(1)} custom-call(bf16[256,2048]{1,0:T(8,128)(2,1)S(1)} %bitcast.22, bf16[256,1536]{1,0:T(8,128)(2,1)S(1)} %bitcast.28, bf16[2048,768]{1,0:T(8,128)(2,1)S(1)} %bitcast.26, bf16[2048,768]{1,0:T(8,128)(2,1)} %bitcast.34, bf16[768,2048]{1,0:T(8,128)(2,1)} %bitcast.35), custom_call_target="tpu_custom_call" | custom-call | flops 2400000000 | bytes 12000000 | tf_op jit(solution)/shard_map/pallas_call | solution.py:173
  94.0 13.3 %all_to_all.37 = bf16[4,64,2048]{2,1,0:T(8,128)(2,1)S(1)} all-to-all(bf16[4,64,2048]{2,1,0:T(8,128)(2,1)S(1)} %bitcast.23), channel_id=1, replica_groups=mesh['section'=32,'y'=4,'zh'=2,'zl'=4] {'y'}, dimensions={0} | all-to-all | bytes 2097152 | tf_op jit(solution)/shard_map/all_to_all | solution.py:183
  107.3 1.3 shard_map.77
  108.6 9.3 %all_to_all.38.parts_ref = bf16[4,16,2048]{2,1,0:T(8,128)(2,1)S(1)} all-to-all(bf16[4,16,2048]{2,1,0:T(8,128)(2,1)S(1)} %bitcast.29), channel_id=1, replica_groups=mesh['section'=32,'y'=4,'zh'=2,'zl'=4] {'zl'}, dimensions={0} | all-to-all | bytes 524288 | tf_op jit(solution)/shard_map/all_to_all | solution.py:145
  117.9 4.3 %all-to-all-start.5 = ((bf16[4,16,2048]{2,1,0:T(8,128)(2,1)}), bf16[4,16,2048]{2,1,0:T(8,128)(2,1)S(1)}, u32[]{:S(2)}, u32[]{:S(2)}) async-start(bf16[4,16,2048]{2,1,0:T(8,128)(2,1)} %bitcast.17), calls=%async_computation.5 | async-start | bytes 524288 | tf_op jit(solution)/shard_map/all_to_all | solution.py:145
  122.2 4.5 %collective-permute-start.2 = (bf16[16,2048]{1,0:T(8,128)(2,1)S(1)}, bf16[16,2048]{1,0:T(8,128)(2,1)S(1)}, u32[]{:S(2)}, u32[]{:S(2)}) collective-permute-start(bf16[16,2048]{1,0:T(8,128)(2,1)S(1)} %shard_map.78), channel_id=1, source_target_pairs={{0,4},{4,0},{1,5},{5,1},{2,6},{6,2},{3,7},{7,3},{8,12},{12,8},{9,1... | collective-permute-start | bytes 196616 | tf_op jit(solution)/shard_map/ppermute | solution.py:141
  126.7 1.7 %all-to-all-done.5.parts_ref = bf16[4,16,2048]{2,1,0:T(8,128)(2,1)S(1)} async-done(((bf16[4,16,2048]{2,1,0:T(8,128)(2,1)}), bf16[4,16,2048]{2,1,0:T(8,128)(2,1)S(1)}, u32[]{:S(2)}, u32[]{:S(2)}) %all-to-all-start.5) | async-done | bytes 262176 | tf_op jit(solution)/shard_map/all_to_all | solution.py:145
  128.4 3.9 %collective-permute-done.2.far_ref = bf16[16,2048]{1,0:T(8,128)(2,1)S(1)} collective-permute-done((bf16[16,2048]{1,0:T(8,128)(2,1)S(1)}, bf16[16,2048]{1,0:T(8,128)(2,1)S(1)}, u32[]{:S(2)}, u32[]{:S(2)}) %collective-permute-start.2) | collective-permute-done | bytes 65568 | tf_op jit(solution)/shard_map/ppermute | solution.py:141
  132.3 0.7 shard_map.79
  (2 shorter events, 0.1 us)
Async XLA Ops:
  0.0 86.0 %copy-start = (bf16[1,2048,768]{2,1,0:T(8,128)(2,1)S(1)}, bf16[1,2048,768]{2,1,0:T(8,128)(2,1)}, u32[]{:S(2)}) copy-start(bf16[1,2048,768]{2,1,0:T(8,128)(2,1)} %param.11) | copy-start | bytes 9437188
  0.0 40.3 %collective-permute-start = (bf16[16,2048]{1,0:T(8,128)(2,1)}, bf16[16,2048]{1,0:T(8,128)(2,1)S(1)}, u32[]{:S(2)}, u32[]{:S(2)}) collective-permute-start(bf16[16,2048]{1,0:T(8,128)(2,1)} %bitcast.36), channel_id=1, source_target_pairs={{0,992},{32,0},{64,32},{96,64},{128,96},{160,128},{192,160},{224,1... | collective-permute-start | bytes 196616 | tf_op jit(solution)/shard_map/ppermute | solution.py:155
  24.0 0.7 copy-start.2
  24.7 0.7 copy-start.3
  41.0 14.9 %all-to-all-start.1 = ((bf16[4,16,2048]{2,1,0:T(8,128)(2,1)}), bf16[4,16,2048]{2,1,0:T(8,128)(2,1)S(1)}, u32[]{:S(2)}, u32[]{:S(2)}) async-start(bf16[4,16,2048]{2,1,0:T(8,128)(2,1)} %broadcast_in_dim.6), calls=%async_computation.1 | async-start | bytes 524288 | tf_op jit(solution)/shard_map/all_to_all | solution.py:145
  45.8 10.1 %collective-permute-start.1 = (bf16[16,2048]{1,0:T(8,128)(2,1)S(1)}, bf16[16,2048]{1,0:T(8,128)(2,1)S(1)}, u32[]{:S(2)}, u32[]{:S(2)}) collective-permute-start(bf16[16,2048]{1,0:T(8,128)(2,1)S(1)} %collective-permute-done), channel_id=1, source_target_pairs={{0,4},{4,0},{1,5},{5,1},{2,6},{6,2},{3,7},{7,3},{8,12},{12,8},{9,1... | collective-permute-start | bytes 196616 | tf_op jit(solution)/shard_map/ppermute | solution.py:141
  56.6 11.4 %all-to-all-start.2 = ((bf16[4,16,2048]{2,1,0:T(8,128)(2,1)}), bf16[4,16,2048]{2,1,0:T(8,128)(2,1)}, u32[]{:S(2)}, u32[]{:S(2)}) async-start(bf16[4,16,2048]{2,1,0:T(8,128)(2,1)} %broadcast_in_dim.7), calls=%async_computation.2 | async-start | bytes 524288 | tf_op jit(solution)/shard_map/all_to_all | solution.py:145
  68.0 18.0 %copy-start.1 = (bf16[1,1,256,1536]{3,2,1,0:T(8,128)(2,1)S(1)}, bf16[1,1,256,1536]{3,2,1,0:T(8,128)(2,1)}, u32[]{:S(2)}) copy-start(bf16[1,1,256,1536]{3,2,1,0:T(8,128)(2,1)} %param.10) | copy-start | bytes 2359300
  117.9 10.5 %all-to-all-start.5 = ((bf16[4,16,2048]{2,1,0:T(8,128)(2,1)}), bf16[4,16,2048]{2,1,0:T(8,128)(2,1)S(1)}, u32[]{:S(2)}, u32[]{:S(2)}) async-start(bf16[4,16,2048]{2,1,0:T(8,128)(2,1)} %bitcast.17), calls=%async_computation.5 | async-start | bytes 524288 | tf_op jit(solution)/shard_map/all_to_all | solution.py:145
  122.2 10.1 %collective-permute-start.2 = (bf16[16,2048]{1,0:T(8,128)(2,1)S(1)}, bf16[16,2048]{1,0:T(8,128)(2,1)S(1)}, u32[]{:S(2)}, u32[]{:S(2)}) collective-permute-start(bf16[16,2048]{1,0:T(8,128)(2,1)S(1)} %shard_map.78), channel_id=1, source_target_pairs={{0,4},{4,0},{1,5},{5,1},{2,6},{6,2},{3,7},{7,3},{8,12},{12,8},{9,1... | collective-permute-start | bytes 196616 | tf_op jit(solution)/shard_map/ppermute | solution.py:141

commit v3 on v1

v3 whole, which is shorter than its diff:
```python
import jax
import jax.numpy as jnp
from jax import lax
from jax.experimental import pallas as pl
from jax.experimental.pallas import tpu as pltpu
from jax.sharding import Mesh, PartitionSpec as P

BF = jnp.bfloat16
F32 = jnp.float32
YS = 4
ZS = 8
QUAD = 4
LANES = 128
MIB = 1 << 20
PARTS = 2


def call(kernel, outs, limit, cost):
    return pl.pallas_call(
        kernel,
        out_shape=outs,
        compiler_params=pltpu.CompilerParams(vmem_limit_bytes=limit * MIB),
        cost_estimate=pl.CostEstimate(flops=cost[0], bytes_accessed=cost[1], transcendentals=0),
    )


def bf16(*shape):
    return jax.ShapeDtypeStruct(shape, BF)


def iota(shape, dim):
    return lax.broadcasted_iota(jnp.int32, shape, dim)


def dot(a, b, dims=((1,), (0,))):
    return lax.dot_general(a, b, (dims, ((), ())), preferred_element_type=F32)


def flag(mask):
    return jnp.where(mask, 1.0, 0.0).astype(BF)


def shares_kernel(ids_ref, probs_ref, out_ref):
    shape = out_ref.shape
    expert = iota(shape, 1)
    acc = jnp.zeros(shape, F32)
    for k in range(ids_ref.shape[1]):
        acc = acc + jnp.where(ids_ref[:, k : k + 1] == expert, probs_ref[:, k : k + 1].astype(F32), 0.0)
    out_ref[...] = acc.astype(BF)


def payload_kernel(rows_ref, share_ref, quad_ref, one_ref):
    width = rows_ref.shape[1]
    one_ref[:, :width] = rows_ref[...]
    one_ref[:, width:] = share_ref[...]
    for k in range(QUAD):
        quad_ref[k, :, :width] = rows_ref[...]
        quad_ref[k, :, width:] = share_ref[...]


def pack_kernel(cap, own, near_ref, far_ref, sent_ref, give_ref):
    _, slots, toks = give_ref.shape
    width = sent_ref.shape[3]
    mine = lax.axis_index("zh")
    z = mine * QUAD + lax.axis_index("zl")
    r = iota((slots, LANES), 0)
    wanted = flag((r // (cap * QUAD)) * ZS + z == iota((slots, LANES), 1))
    i, j = iota((toks, toks), 0), iota((toks, toks), 1)
    before = flag((i < j) & (i // own == j // own))
    rr, tt = iota((slots, toks), 0), iota((slots, toks), 1)
    for k, rows_ref in enumerate((near_ref, far_ref)):
        share_at = dot(wanted, rows_ref[:, width:], ((1,), (1,)))
        earlier = dot(flag(share_at > 0), before)
        hit = (share_at > 0) & (tt // own == (rr // cap) % QUAD) & (earlier == (rr % cap).astype(F32))
        give_ref[k] = jnp.where(hit, share_at, 0.0).astype(BF)
        packed = dot(flag(hit), rows_ref[:, :width]).astype(BF)
        sent_ref[:, pl.ds((mine + k) % 2, 1)] = packed.reshape(YS, 1, slots // YS, width)


def combine_kernel(give_ref, rows_ref, near_ref, far_ref):
    mine = lax.axis_index("zh")
    slots = give_ref.shape[1]
    for k, out_ref in ((1, far_ref), (0, near_ref)):
        rows = rows_ref[:, pl.ds((mine + k) % 2, 1)].reshape(slots, -1)
        out_ref[...] = dot(give_ref[k], rows, ((0,), (0,))).astype(BF)


def expert_kernel(rows_ref, kept_ref, gate_ref, up_hbm, down_hbm, out_ref, up, down, hidden, sems):
    ff, width = down.shape
    parts = sems.shape[0] // 2
    begun = []
    for src, dst in ((down_hbm, down), (up_hbm, up)):
        step = src.shape[0] // parts
        for k in range(parts):
            at = pl.ds(k * step, step)
            copy = pltpu.make_async_copy(src.at[at], dst.at[at], sems.at[len(begun)])
            copy.start()
            begun.append((copy, at))
    for copy, at in begun[:parts]:
        copy.wait()
        hidden[:, at] = dot(rows_ref[...], down[at, :], ((1,), (1,)))
    h = hidden[...]
    g = kept_ref[:, :ff].astype(F32)
    u = kept_ref[:, ff:].astype(F32)
    s = jax.nn.sigmoid(g)
    hs = h * s
    up_grad = (hs * g).astype(BF)
    gate_grad = (hs * u * (1.0 + g * (1.0 - s))).astype(BF)
    for copy, at in begun[parts:]:
        copy.wait()
        total = dot(gate_grad, gate_ref[at, :], ((1,), (1,))) + dot(up_grad, up[at, :], ((1,), (1,)))
        out_ref[:, at] = total.astype(BF)


def sum_of(parts_ref):
    acc = parts_ref[0].astype(F32)
    for k in range(1, parts_ref.shape[0]):
        acc = acc + parts_ref[k].astype(F32)
    return acc


def half_kernel(parts_ref, out_ref):
    out_ref[...] = sum_of(parts_ref).astype(BF)


def total_kernel(parts_ref, far_ref, out_ref):
    out_ref[...] = (sum_of(parts_ref) + far_ref[...].astype(F32)).astype(BF)


def swapped(x):
    return lax.ppermute(x, "zh", [(0, 1), (1, 0)])


def quad(x):
    return lax.all_to_all(x, "zl", 0, 0, tiled=True)


def across(x):
    return lax.all_to_all(x.reshape(YS, -1, x.shape[-1]), "y", 0, 0, tiled=True).reshape(x.shape)


def body(cotangent, expert_ids, gate_probs, saved, w_gate, w_up, w_down):
    sections = lax.axis_size("section")
    tokens, width = cotangent.shape[1:]
    slots = saved.shape[2]
    cap = slots // (YS * ZS)
    half = QUAD * tokens
    incoming = lax.ppermute(cotangent[0], "section", [(i, (i - 1) % sections) for i in range(sections)])
    shares = call(shares_kernel, bf16(tokens, LANES), 4, (10**5, 10**4))(expert_ids[0], gate_probs[0])
    copies, one = call(
        payload_kernel, (bf16(QUAD, tokens, width + LANES), bf16(tokens, width + LANES)), 4, (10**5, 10**6)
    )(incoming, shares)
    crossed = swapped(one)
    near_rows = quad(copies)
    far_rows = quad(jnp.broadcast_to(crossed[None], (QUAD, tokens, width + LANES)))
    sent, give = call(
        lambda *refs: pack_kernel(cap, tokens, *refs),
        (bf16(YS, 2, slots // (2 * YS), width), bf16(2, slots // 2, half)),
        8,
        (10**8, 10**6),
    )(near_rows.reshape(half, -1), far_rows.reshape(half, -1))
    vm = pl.BlockSpec(memory_space=pltpu.VMEM)
    anywhere = pl.BlockSpec(memory_space=pl.ANY)
    grads = pl.pallas_call(
        expert_kernel,
        out_shape=bf16(slots, width),
        in_specs=[vm, vm, vm, anywhere, anywhere],
        out_specs=vm,
        scratch_shapes=[
            pltpu.VMEM(w_up.shape[1:], BF),
            pltpu.VMEM(w_down.shape[1:], BF),
            pltpu.VMEM((slots, w_down.shape[1]), F32),
            pltpu.SemaphoreType.DMA((2 * PARTS,)),
        ],
        compiler_params=pltpu.CompilerParams(vmem_limit_bytes=48 * MIB),
        cost_estimate=pl.CostEstimate(flops=24 * 10**8, bytes_accessed=12 * 10**6, transcendentals=0),
    )(across(sent).reshape(slots, width), saved[0, 0], w_gate[0], w_up[0], w_down[0])
    back = across(grads).reshape(sent.shape)
    near, far = call(combine_kernel, (bf16(half, width), bf16(half, width)), 8, (10**8, 10**6))(give, back)
    far = quad(far.reshape(QUAD, tokens, width))
    far = swapped(call(half_kernel, bf16(tokens, width), 4, (10**6, 10**6))(far))
    near = quad(near.reshape(QUAD, tokens, width))
    out = call(total_kernel, bf16(tokens, width), 4, (10**6, 10**6))(near, far)
    return out[None]


def solution(mesh):
    split = Mesh(mesh.devices.reshape(-1, YS, ZS // QUAD, QUAD), ("section", "y", "zh", "zl"))
    line = ("y", "zh", "zl")
    over = P("section", line, None)
    weight = P(line, None, None)
    in_specs = (over, over, over, P("section", line, None, None), weight, weight, weight)
    return jax.shard_map(body, mesh=split, in_specs=in_specs, out_specs=over, check_vma=False)
```

time: 134 us -> 123 us (0.918)
  the two profiles are of different devices: /device:TPU:256 before, /device:TPU:38 now
where the time goes in v3:
time: 123 us
  blocking collectives  54.8 us (45%)
  starting transfers between devices  43 us (35%)
  waiting for transfers between devices  13.6 us (11%)
  Pallas kernels  7.94 us (6%)
  local copies, waits for them, and re-layouts  3.2 us (3%)
    all_to_all x2, blocking collectives, across(): lax.all_to_all(x.reshape(YS, -1, x.shape[-1]), 'y', 0, 0, tiled=True)  30.7 us
    all_to_all x2, blocking collectives, quad(): return lax.all_to_all(x, 'zl', 0, 0, tiled=True)  24.1 us
    ppermute x1, starting transfers between devices, body(): lax.ppermute(cotangent[0], 'section', [(i, (i - 1) % sections) for i in r...  22.1 us
    ppermute x2, waiting for transfers between devices, swapped(): return lax.ppermute(x, 'zh', [(0, 1), (1, 0)])  13 us
    ppermute x2, starting transfers between devices, swapped(): return lax.ppermute(x, 'zh', [(0, 1), (1, 0)])  12.2 us
    all_to_all x2, starting transfers between devices, quad(): return lax.all_to_all(x, 'zl', 0, 0, tiled=True)  8.71 us
    pallas_call x1, Pallas kernels, body(): pl.pallas_call(expert_kernel, out_shape=bf16(slots, width), in_specs=[vm,...  5.14 us
  transfers between devices with their start and end apart: 5, of which 3 were waited for; matrix products, arithmetic and copies ran while one was open for 1% of the time, Pallas kernels for 0%

profile of v3, /device:TPU:38, one launch (start us, length us, event | category | flops | bytes accessed | tf_op | source)
XLA Modules:
  0.0 122.6 jit_solution(12352164555496504133)
XLA Ops:
  0.0 0.0 copy-start
  0.0 22.1 %collective-permute-start = (bf16[16,2048]{1,0:T(8,128)(2,1)}, bf16[16,2048]{1,0:T(8,128)(2,1)S(1)}, u32[]{:S(2)}, u32[]{:S(2)}) collective-permute-start(bf16[16,2048]{1,0:T(8,128)(2,1)} %bitcast.29), channel_id=1, source_target_pairs={{0,992},{32,0},{64,32},{96,64},{128,96},{160,128},{192,160},{224,1... | collective-permute-start | bytes 196616 | tf_op jit(solution)/shard_map/ppermute | solution.py:148
  22.1 0.8 copy.9.probs_ref
  22.8 0.8 copy.8.ids_ref
  23.6 0.1 shard_map.73.share_ref
  23.7 0.6 collective-permute-done.rows_ref
  24.3 0.0 copy-start.2
  24.3 0.7 copy-done.2
  25.0 4.4 %all-to-all-start = ((bf16[4,16,2176]{2,1,0:T(8,128)(2,1)}), bf16[4,16,2176]{2,1,0:T(8,128)(2,1)S(1)}, u32[]{:S(2)}, u32[]{:S(2)}) async-start(bf16[4,16,2176]{2,1,0:T(8,128)(2,1)} %copy-done.2), calls=%async_computation | async-start | bytes 557056 | tf_op jit(solution)/shard_map/all_to_all | solution.py:135
  29.4 4.3 %collective-permute-start.1 = (bf16[16,2176]{1,0:T(8,128)(2,1)S(1)}, bf16[16,2176]{1,0:T(8,128)(2,1)}, u32[]{:S(2)}, u32[]{:S(2)}) collective-permute-start(bf16[16,2176]{1,0:T(8,128)(2,1)S(1)} %get-tuple-element.12), channel_id=1, source_target_pairs={{0,4},{4,0},{1,5},{5,1},{2,6},{6,2},{3,7},{7,3},{8,12},{12,8},{9,1... | collective-permute-start | bytes 208904 | tf_op jit(solution)/shard_map/ppermute | solution.py:131
  33.7 9.3 %collective-permute-done.1 = bf16[16,2176]{1,0:T(8,128)(2,1)} collective-permute-done((bf16[16,2176]{1,0:T(8,128)(2,1)S(1)}, bf16[16,2176]{1,0:T(8,128)(2,1)}, u32[]{:S(2)}, u32[]{:S(2)}) %collective-permute-start.1) | collective-permute-done | bytes 69664 | tf_op jit(solution)/shard_map/ppermute | solution.py:131
  43.0 0.0 all-to-all-done
  43.0 0.0 copy-start.1
  43.0 1.0 broadcast_in_dim.4
  43.9 9.8 %all_to_all.30 = bf16[4,16,2176]{2,1,0:T(8,128)(2,1)S(1)} all-to-all(bf16[4,16,2176]{2,1,0:T(8,128)(2,1)S(1)} %broadcast_in_dim.4), channel_id=1, replica_groups=mesh['section'=32,'y'=4,'zh'=2,'zl'=4] {'zl'}, dimensions={0} | all-to-all | bytes 557056 | tf_op jit(solution)/shard_map/all_to_all | solution.py:135
  53.8 0.9 shard_map.75
  54.7 16.9 %all_to_all.31 = bf16[4,64,2048]{2,1,0:T(8,128)(2,1)S(1)} all-to-all(bf16[4,64,2048]{2,1,0:T(8,128)(2,1)S(1)} %bitcast.22), channel_id=1, replica_groups=mesh['section'=32,'y'=4,'zh'=2,'zl'=4] {'y'}, dimensions={0} | all-to-all | bytes 2097152 | tf_op jit(solution)/shard_map/all_to_all | solution.py:139
  71.6 0.0 copy-done
  71.6 0.0 copy-done.1
  71.6 5.1 %shard_map.76 = bf16[256,2048]{1,0:T(8,128)(2,1)S(1)} custom-call(bf16[256,2048]{1,0:T(8,128)(2,1)S(1)} %bitcast.16, bf16[256,1536]{1,0:T(8,128)(2,1)S(1)} %bitcast.23, bf16[2048,768]{1,0:T(8,128)(2,1)S(1)} %bitcast.19, bf16[2048,768]{1,0:T(8,128)(2,1)} %bitcast.25, bf16[768,2048]{1,0:T(8,128)(2,1)} %bitcast.26), custom_call_target="tpu_custom_call" | custom-call | flops 2400000000 | bytes 12000000 | tf_op jit(solution)/shard_map/pallas_call | solution.py:164
  76.7 13.8 %all_to_all.32 = bf16[4,64,2048]{2,1,0:T(8,128)(2,1)S(1)} all-to-all(bf16[4,64,2048]{2,1,0:T(8,128)(2,1)S(1)} %bitcast.17), channel_id=1, replica_groups=mesh['section'=32,'y'=4,'zh'=2,'zl'=4] {'y'}, dimensions={0} | all-to-all | bytes 2097152 | tf_op jit(solution)/shard_map/all_to_all | solution.py:139
  90.5 1.0 shard_map.77
  91.6 14.2 %all_to_all.33.parts_ref = bf16[4,16,2048]{2,1,0:T(8,128)(2,1)S(1)} all-to-all(bf16[4,16,2048]{2,1,0:T(8,128)(2,1)S(1)} %bitcast.24), channel_id=1, replica_groups=mesh['section'=32,'y'=4,'zh'=2,'zl'=4] {'zl'}, dimensions={0} | all-to-all | bytes 524288 | tf_op jit(solution)/shard_map/all_to_all | solution.py:135
  105.8 4.3 %all-to-all-start.4 = ((bf16[4,16,2048]{2,1,0:T(8,128)(2,1)}), bf16[4,16,2048]{2,1,0:T(8,128)(2,1)S(1)}, u32[]{:S(2)}, u32[]{:S(2)}) async-start(bf16[4,16,2048]{2,1,0:T(8,128)(2,1)} %bitcast.13), calls=%async_computation.4 | async-start | bytes 524288 | tf_op jit(solution)/shard_map/all_to_all | solution.py:135
  110.2 7.9 %collective-permute-start.2 = (bf16[16,2048]{1,0:T(8,128)(2,1)S(1)}, bf16[16,2048]{1,0:T(8,128)(2,1)S(1)}, u32[]{:S(2)}, u32[]{:S(2)}) collective-permute-start(bf16[16,2048]{1,0:T(8,128)(2,1)S(1)} %shard_map.78), channel_id=1, source_target_pairs={{0,4},{4,0},{1,5},{5,1},{2,6},{6,2},{3,7},{7,3},{8,12},{12,8},{9,1... | collective-permute-start | bytes 196616 | tf_op jit(solution)/shard_map/ppermute | solution.py:131
  118.1 0.0 all-to-all-done.4.parts_ref
  118.1 3.8 %collective-permute-done.2.far_ref = bf16[16,2048]{1,0:T(8,128)(2,1)S(1)} collective-permute-done((bf16[16,2048]{1,0:T(8,128)(2,1)S(1)}, bf16[16,2048]{1,0:T(8,128)(2,1)S(1)}, u32[]{:S(2)}, u32[]{:S(2)}) %collective-permute-start.2) | collective-permute-done | bytes 65568 | tf_op jit(solution)/shard_map/ppermute | solution.py:131
  121.9 0.7 shard_map.79
  (2 shorter events, 0.1 us)
Async XLA Ops:
  0.0 71.6 %copy-start = (bf16[1,2048,768]{2,1,0:T(8,128)(2,1)S(1)}, bf16[1,2048,768]{2,1,0:T(8,128)(2,1)}, u32[]{:S(2)}) copy-start(bf16[1,2048,768]{2,1,0:T(8,128)(2,1)} %param.11) | copy-start | bytes 9437188
  0.0 24.3 %collective-permute-start = (bf16[16,2048]{1,0:T(8,128)(2,1)}, bf16[16,2048]{1,0:T(8,128)(2,1)S(1)}, u32[]{:S(2)}, u32[]{:S(2)}) collective-permute-start(bf16[16,2048]{1,0:T(8,128)(2,1)} %bitcast.29), channel_id=1, source_target_pairs={{0,992},{32,0},{64,32},{96,64},{128,96},{160,128},{192,160},{224,1... | collective-permute-start | bytes 196616 | tf_op jit(solution)/shard_map/ppermute | solution.py:148
  24.3 0.7 copy-start.2
  25.0 18.0 %all-to-all-start = ((bf16[4,16,2176]{2,1,0:T(8,128)(2,1)}), bf16[4,16,2176]{2,1,0:T(8,128)(2,1)S(1)}, u32[]{:S(2)}, u32[]{:S(2)}) async-start(bf16[4,16,2176]{2,1,0:T(8,128)(2,1)} %copy-done.2), calls=%async_computation | async-start | bytes 557056 | tf_op jit(solution)/shard_map/all_to_all | solution.py:135
  29.4 13.5 %collective-permute-start.1 = (bf16[16,2176]{1,0:T(8,128)(2,1)S(1)}, bf16[16,2176]{1,0:T(8,128)(2,1)}, u32[]{:S(2)}, u32[]{:S(2)}) collective-permute-start(bf16[16,2176]{1,0:T(8,128)(2,1)S(1)} %get-tuple-element.12), channel_id=1, source_target_pairs={{0,4},{4,0},{1,5},{5,1},{2,6},{6,2},{3,7},{7,3},{8,12},{12,8},{9,1... | collective-permute-start | bytes 208904 | tf_op jit(solution)/shard_map/ppermute | solution.py:131
  43.0 28.6 %copy-start.1 = (bf16[1,1,256,1536]{3,2,1,0:T(8,128)(2,1)S(1)}, bf16[1,1,256,1536]{3,2,1,0:T(8,128)(2,1)}, u32[]{:S(2)}) copy-start(bf16[1,1,256,1536]{3,2,1,0:T(8,128)(2,1)} %param.10) | copy-start | bytes 2359300
  105.8 12.3 %all-to-all-start.4 = ((bf16[4,16,2048]{2,1,0:T(8,128)(2,1)}), bf16[4,16,2048]{2,1,0:T(8,128)(2,1)S(1)}, u32[]{:S(2)}, u32[]{:S(2)}) async-start(bf16[4,16,2048]{2,1,0:T(8,128)(2,1)} %bitcast.13), calls=%async_computation.4 | async-start | bytes 524288 | tf_op jit(solution)/shard_map/all_to_all | solution.py:135
  110.2 11.7 %collective-permute-start.2 = (bf16[16,2048]{1,0:T(8,128)(2,1)S(1)}, bf16[16,2048]{1,0:T(8,128)(2,1)S(1)}, u32[]{:S(2)}, u32[]{:S(2)}) collective-permute-start(bf16[16,2048]{1,0:T(8,128)(2,1)S(1)} %shard_map.78), channel_id=1, source_target_pairs={{0,4},{4,0},{1,5},{5,1},{2,6},{6,2},{3,7},{7,3},{8,12},{12,8},{9,1... | collective-permute-start | bytes 196616 | tf_op jit(solution)/shard_map/ppermute | solution.py:131

commit v4 on v3

--- a/solution.py
+++ b/solution.py
@@ -49,16 +49,16 @@
     out_ref[...] = acc.astype(BF)
 
 
-def payload_kernel(rows_ref, share_ref, quad_ref, one_ref):
-    width = rows_ref.shape[1]
-    one_ref[:, :width] = rows_ref[...]
-    one_ref[:, width:] = share_ref[...]
+def payload_kernel(near_ref, far_ref, near_share_ref, far_share_ref, out_ref):
+    own, width = near_ref.shape
     for k in range(QUAD):
-        quad_ref[k, :, :width] = rows_ref[...]
-        quad_ref[k, :, width:] = share_ref[...]
-
-
-def pack_kernel(cap, own, near_ref, far_ref, sent_ref, give_ref):
+        out_ref[k, :own, :width] = near_ref[...]
+        out_ref[k, own:, :width] = far_ref[...]
+        out_ref[k, :own, width:] = near_share_ref[...]
+        out_ref[k, own:, width:] = far_share_ref[...]
+
+
+def pack_kernel(cap, own, rows_ref, sent_ref, give_ref):
     _, slots, toks = give_ref.shape
     width = sent_ref.shape[3]
     mine = lax.axis_index("zh")
@@ -68,21 +68,24 @@
     i, j = iota((toks, toks), 0), iota((toks, toks), 1)
     before = flag((i < j) & (i // own == j // own))
     rr, tt = iota((slots, toks), 0), iota((slots, toks), 1)
-    for k, rows_ref in enumerate((near_ref, far_ref)):
-        share_at = dot(wanted, rows_ref[:, width:], ((1,), (1,)))
+    for k in range(2):
+        rows = rows_ref[:, k * own : (k + 1) * own, :].reshape(toks, -1)
+        share_at = dot(wanted, rows[:, width:], ((1,), (1,)))
         earlier = dot(flag(share_at > 0), before)
         hit = (share_at > 0) & (tt // own == (rr // cap) % QUAD) & (earlier == (rr % cap).astype(F32))
         give_ref[k] = jnp.where(hit, share_at, 0.0).astype(BF)
-        packed = dot(flag(hit), rows_ref[:, :width]).astype(BF)
+        packed = dot(flag(hit), rows[:, :width]).astype(BF)
         sent_ref[:, pl.ds((mine + k) % 2, 1)] = packed.reshape(YS, 1, slots // YS, width)
 
 
-def combine_kernel(give_ref, rows_ref, near_ref, far_ref):
+def combine_kernel(give_ref, rows_ref, out_ref):
     mine = lax.axis_index("zh")
     slots = give_ref.shape[1]
-    for k, out_ref in ((1, far_ref), (0, near_ref)):
+    own = out_ref.shape[1] // 2
+    for k in range(2):
         rows = rows_ref[:, pl.ds((mine + k) % 2, 1)].reshape(slots, -1)
-        out_ref[...] = dot(give_ref[k], rows, ((0,), (0,))).astype(BF)
+        part = dot(give_ref[k], rows, ((0,), (0,))).astype(BF)
+        out_ref[:, k * own : (k + 1) * own] = part.reshape(QUAD, own, -1)
 
 
 def expert_kernel(rows_ref, kept_ref, gate_ref, up_hbm, down_hbm, out_ref, up, down, hidden, sems):
@@ -112,19 +115,21 @@
         out_ref[:, at] = total.astype(BF)
 
 
-def sum_of(parts_ref):
-    acc = parts_ref[0].astype(F32)
+def sum_of(parts_ref, at):
+    acc = parts_ref[0, at].astype(F32)
     for k in range(1, parts_ref.shape[0]):
-        acc = acc + parts_ref[k].astype(F32)
+        acc = acc + parts_ref[k, at].astype(F32)
     return acc
 
 
 def half_kernel(parts_ref, out_ref):
-    out_ref[...] = sum_of(parts_ref).astype(BF)
+    own = out_ref.shape[0]
+    out_ref[...] = sum_of(parts_ref, slice(own, 2 * own)).astype(BF)
 
 
 def total_kernel(parts_ref, far_ref, out_ref):
-    out_ref[...] = (sum_of(parts_ref) + far_ref[...].astype(F32)).astype(BF)
+    own = out_ref.shape[0]
+    out_ref[...] = (sum_of(parts_ref, slice(0, own)) + far_ref[...].astype(F32)).astype(BF)
 
 
 def swapped(x):
@@ -145,20 +150,25 @@
     slots = saved.shape[2]
     cap = slots // (YS * ZS)
     half = QUAD * tokens
+    halves = ZS // QUAD
+    moves = [
+        ((q * halves + h) * QUAD + k, ((q - 1) % sections * halves + (h + 1) % halves) * QUAD + k)
+        for q in range(sections)
+        for h in range(halves)
+        for k in range(QUAD)
+    ]
+    crossed = lax.ppermute(cotangent[0], ("section", "zh", "zl"), moves)
     incoming = lax.ppermute(cotangent[0], "section", [(i, (i - 1) % sections) for i in range(sections)])
     shares = call(shares_kernel, bf16(tokens, LANES), 4, (10**5, 10**4))(expert_ids[0], gate_probs[0])
-    copies, one = call(
-        payload_kernel, (bf16(QUAD, tokens, width + LANES), bf16(tokens, width + LANES)), 4, (10**5, 10**6)
-    )(incoming, shares)
-    crossed = swapped(one)
-    near_rows = quad(copies)
-    far_rows = quad(jnp.broadcast_to(crossed[None], (QUAD, tokens, width + LANES)))
+    payload = call(payload_kernel, bf16(QUAD, 2 * tokens, width + LANES), 4, (10**5, 10**6))(
+        incoming, crossed, shares, swapped(shares)
+    )
     sent, give = call(
         lambda *refs: pack_kernel(cap, tokens, *refs),
         (bf16(YS, 2, slots // (2 * YS), width), bf16(2, slots // 2, half)),
         8,
         (10**8, 10**6),
-    )(near_rows.reshape(half, -1), far_rows.reshape(half, -1))
+    )(quad(payload))
     vm = pl.BlockSpec(memory_space=pltpu.VMEM)
     anywhere = pl.BlockSpec(memory_space=pl.ANY)
     grads = pl.pallas_call(
@@ -176,11 +186,9 @@
         cost_estimate=pl.CostEstimate(flops=24 * 10**8, bytes_accessed=12 * 10**6, transcendentals=0),
     )(across(sent).reshape(slots, width), saved[0, 0], w_gate[0], w_up[0], w_down[0])
     back = across(grads).reshape(sent.shape)
-    near, far = call(combine_kernel, (bf16(half, width), bf16(half, width)), 8, (10**8, 10**6))(give, back)
-    far = quad(far.reshape(QUAD, tokens, width))
-    far = swapped(call(half_kernel, bf16(tokens, width), 4, (10**6, 10**6))(far))
-    near = quad(near.reshape(QUAD, tokens, width))
-    out = call(total_kernel, bf16(tokens, width), 4, (10**6, 10**6))(near, far)
+    parts = quad(call(combine_kernel, bf16(QUAD, 2 * tokens, width), 8, (10**8, 10**6))(give, back))
+    far = swapped(call(half_kernel, bf16(tokens, width), 4, (10**6, 10**6))(parts))
+    out = call(total_kernel, bf16(tokens, width), 4, (10**6, 10**6))(parts, far)
     return out[None]
 
 

time: 123 us -> 122 us (level)
  the two profiles are of different devices: /device:TPU:38 before, /device:TPU:8 now
where the time goes in v4:
time: 122 us; the launch traced here: 121 us
  blocking collectives  60.7 us (50%)
  starting transfers between devices  43.8 us (36%)
  waiting for transfers between devices  7.91 us (6%)
  Pallas kernels  7.24 us (6%)
  local copies, waits for them, and re-layouts  1.53 us (1%)
    all_to_all x2, blocking collectives, quad(): return lax.all_to_all(x, 'zl', 0, 0, tiled=True)  31.2 us
    all_to_all x2, blocking collectives, across(): lax.all_to_all(x.reshape(YS, -1, x.shape[-1]), 'y', 0, 0, tiled=True)  29.5 us
    ppermute x1, starting transfers between devices, body(): crossed = lax.ppermute(cotangent[0], ('section', 'zh', 'zl'), moves)  21.9 us
    ppermute x2, starting transfers between devices, swapped(): return lax.ppermute(x, 'zh', [(0, 1), (1, 0)])  14.4 us
    ppermute x2, waiting for transfers between devices, swapped(): return lax.ppermute(x, 'zh', [(0, 1), (1, 0)])  7.9 us
    ppermute x1, starting transfers between devices, body(): lax.ppermute(cotangent[0], 'section', [(i, (i - 1) % sections) for i in r...  7.56 us
    pallas_call x1, Pallas kernels, body(): pl.pallas_call(expert_kernel, out_shape=bf16(slots, width), in_specs=[vm,...  5.15 us
  transfers between devices with their start and end apart: 4, of which 2 were waited for; matrix products, arithmetic and copies ran while one was open for 1% of the time, Pallas kernels for 0%

profile of v4, /device:TPU:8, one launch (start us, length us, event | category | flops | bytes accessed | tf_op | source)
XLA Modules:
  0.0 121.3 jit_solution(1448725618912764460)
XLA Ops:
  0.0 0.0 copy-start
  0.0 21.9 %collective-permute-start.1 = (bf16[16,2048]{1,0:T(8,128)(2,1)}, bf16[16,2048]{1,0:T(8,128)(2,1)S(1)}, u32[]{:S(2)}, u32[]{:S(2)}) collective-permute-start(bf16[16,2048]{1,0:T(8,128)(2,1)} %bitcast.22), channel_id=1, source_target_pairs={{0,996},{1,997},{2,998},{3,999},{4,992},{5,993},{6,994},{7,995},{3... | collective-permute-start | bytes 196616 | tf_op jit(solution)/shard_map/ppermute | solution.py:160
  21.9 7.6 %collective-permute-start = (bf16[16,2048]{1,0:T(8,128)(2,1)}, bf16[16,2048]{1,0:T(8,128)(2,1)S(1)}, u32[]{:S(2)}, u32[]{:S(2)}) collective-permute-start(bf16[16,2048]{1,0:T(8,128)(2,1)} %bitcast.23), channel_id=1, source_target_pairs={{0,992},{32,0},{64,32},{96,64},{128,96},{160,128},{192,160},{224,1... | collective-permute-start | bytes 196616 | tf_op jit(solution)/shard_map/ppermute | solution.py:161
  29.5 0.8 copy.9.probs_ref
  30.2 0.8 copy.8.ids_ref
  31.0 0.0 copy-start.1
  31.0 0.1 shard_map.73.near_share_ref
  31.1 5.6 %collective-permute-start.2 = (bf16[16,128]{1,0:T(8,128)(2,1)S(1)}, bf16[16,128]{1,0:T(8,128)(2,1)S(1)}, u32[]{:S(2)}, u32[]{:S(2)}) collective-permute-start(bf16[16,128]{1,0:T(8,128)(2,1)S(1)} %shard_map.73.near_share_ref), channel_id=1, source_target_pairs={{0,4},{4,0},{1,5},{5,1},{2,6},{6,2},{3,7},{7,3},{8,12},{12,8},{9,1... | collective-permute-start | bytes 12296 | tf_op jit(solution)/shard_map/ppermute | solution.py:136
  36.7 3.9 %collective-permute-done.2.far_share_ref = bf16[16,128]{1,0:T(8,128)(2,1)S(1)} collective-permute-done((bf16[16,128]{1,0:T(8,128)(2,1)S(1)}, bf16[16,128]{1,0:T(8,128)(2,1)S(1)}, u32[]{:S(2)}, u32[]{:S(2)}) %collective-permute-start.2) | collective-permute-done | bytes 4128 | tf_op jit(solution)/shard_map/ppermute | solution.py:136
  40.6 0.0 collective-permute-done.1.far_ref
  40.6 0.0 collective-permute-done.near_ref
  40.7 15.0 %all_to_all.20.refs_0_ = bf16[4,32,2176]{2,1,0:T(8,128)(2,1)S(1)} all-to-all(bf16[4,32,2176]{2,1,0:T(8,128)(2,1)S(1)} %shard_map.74), channel_id=1, replica_groups=mesh['section'=32,'y'=4,'zh'=2,'zl'=4] {'zl'}, dimensions={0} | all-to-all | bytes 1114112 | tf_op jit(solution)/shard_map/all_to_all | solution.py:140
  55.7 0.9 shard_map.75
  56.6 15.8 %all_to_all.21 = bf16[4,64,2048]{2,1,0:T(8,128)(2,1)S(1)} all-to-all(bf16[4,64,2048]{2,1,0:T(8,128)(2,1)S(1)} %bitcast.16), channel_id=1, replica_groups=mesh['section'=32,'y'=4,'zh'=2,'zl'=4] {'y'}, dimensions={0} | all-to-all | bytes 2097152 | tf_op jit(solution)/shard_map/all_to_all | solution.py:144
  72.4 0.0 copy-done
  72.4 0.0 copy-done.1
  72.4 5.1 %shard_map.76 = bf16[256,2048]{1,0:T(8,128)(2,1)S(1)} custom-call(bf16[256,2048]{1,0:T(8,128)(2,1)S(1)} %bitcast.12, bf16[256,1536]{1,0:T(8,128)(2,1)S(1)} %bitcast.17, bf16[2048,768]{1,0:T(8,128)(2,1)S(1)} %bitcast.15, bf16[2048,768]{1,0:T(8,128)(2,1)} %bitcast.18, bf16[768,2048]{1,0:T(8,128)(2,1)} %bitcast.19), custom_call_target="tpu_custom_call" | custom-call | flops 2400000000 | bytes 12000000 | tf_op jit(solution)/shard_map/pallas_call | solution.py:174
  77.5 13.7 %all_to_all.22 = bf16[4,64,2048]{2,1,0:T(8,128)(2,1)S(1)} all-to-all(bf16[4,64,2048]{2,1,0:T(8,128)(2,1)S(1)} %bitcast.13), channel_id=1, replica_groups=mesh['section'=32,'y'=4,'zh'=2,'zl'=4] {'y'}, dimensions={0} | all-to-all | bytes 2097152 | tf_op jit(solution)/shard_map/all_to_all | solution.py:144
  91.2 0.3 shard_map.77
  91.6 16.2 %all_to_all.23.parts_ref = bf16[4,32,2048]{2,1,0:T(8,128)(2,1)S(1)} all-to-all(bf16[4,32,2048]{2,1,0:T(8,128)(2,1)S(1)} %shard_map.77), channel_id=1, replica_groups=mesh['section'=32,'y'=4,'zh'=2,'zl'=4] {'zl'}, dimensions={0} | all-to-all | bytes 1048576 | tf_op jit(solution)/shard_map/all_to_all | solution.py:140
  107.9 8.8 %collective-permute-start.3 = (bf16[16,2048]{1,0:T(8,128)(2,1)S(1)}, bf16[16,2048]{1,0:T(8,128)(2,1)S(1)}, u32[]{:S(2)}, u32[]{:S(2)}) collective-permute-start(bf16[16,2048]{1,0:T(8,128)(2,1)S(1)} %shard_map.78), channel_id=1, source_target_pairs={{0,4},{4,0},{1,5},{5,1},{2,6},{6,2},{3,7},{7,3},{8,12},{12,8},{9,1... | collective-permute-start | bytes 196616 | tf_op jit(solution)/shard_map/ppermute | solution.py:136
  116.6 4.0 %collective-permute-done.3.far_ref = bf16[16,2048]{1,0:T(8,128)(2,1)S(1)} collective-permute-done((bf16[16,2048]{1,0:T(8,128)(2,1)S(1)}, bf16[16,2048]{1,0:T(8,128)(2,1)S(1)}, u32[]{:S(2)}, u32[]{:S(2)}) %collective-permute-start.3) | collective-permute-done | bytes 65568 | tf_op jit(solution)/shard_map/ppermute | solution.py:136
  120.6 0.7 shard_map.79
  (2 shorter events, 0.1 us)
Async XLA Ops:
  0.0 72.4 %copy-start = (bf16[1,2048,768]{2,1,0:T(8,128)(2,1)S(1)}, bf16[1,2048,768]{2,1,0:T(8,128)(2,1)}, u32[]{:S(2)}) copy-start(bf16[1,2048,768]{2,1,0:T(8,128)(2,1)} %param.11) | copy-start | bytes 9437188
  0.0 40.6 %collective-permute-start.1 = (bf16[16,2048]{1,0:T(8,128)(2,1)}, bf16[16,2048]{1,0:T(8,128)(2,1)S(1)}, u32[]{:S(2)}, u32[]{:S(2)}) collective-permute-start(bf16[16,2048]{1,0:T(8,128)(2,1)} %bitcast.22), channel_id=1, source_target_pairs={{0,996},{1,997},{2,998},{3,999},{4,992},{5,993},{6,994},{7,995},{3... | collective-permute-start | bytes 196616 | tf_op jit(solution)/shard_map/ppermute | solution.py:160
  21.9 18.7 %collective-permute-start = (bf16[16,2048]{1,0:T(8,128)(2,1)}, bf16[16,2048]{1,0:T(8,128)(2,1)S(1)}, u32[]{:S(2)}, u32[]{:S(2)}) collective-permute-start(bf16[16,2048]{1,0:T(8,128)(2,1)} %bitcast.23), channel_id=1, source_target_pairs={{0,992},{32,0},{64,32},{96,64},{128,96},{160,128},{192,160},{224,1... | collective-permute-start | bytes 196616 | tf_op jit(solution)/shard_map/ppermute | solution.py:161
  31.0 41.4 %copy-start.1 = (bf16[1,1,256,1536]{3,2,1,0:T(8,128)(2,1)S(1)}, bf16[1,1,256,1536]{3,2,1,0:T(8,128)(2,1)}, u32[]{:S(2)}) copy-start(bf16[1,1,256,1536]{3,2,1,0:T(8,128)(2,1)} %param.10) | copy-start | bytes 2359300
  31.1 9.5 %collective-permute-start.2 = (bf16[16,128]{1,0:T(8,128)(2,1)S(1)}, bf16[16,128]{1,0:T(8,128)(2,1)S(1)}, u32[]{:S(2)}, u32[]{:S(2)}) collective-permute-start(bf16[16,128]{1,0:T(8,128)(2,1)S(1)} %shard_map.73.near_share_ref), channel_id=1, source_target_pairs={{0,4},{4,0},{1,5},{5,1},{2,6},{6,2},{3,7},{7,3},{8,12},{12,8},{9,1... | collective-permute-start | bytes 12296 | tf_op jit(solution)/shard_map/ppermute | solution.py:136
  107.9 12.7 %collective-permute-start.3 = (bf16[16,2048]{1,0:T(8,128)(2,1)S(1)}, bf16[16,2048]{1,0:T(8,128)(2,1)S(1)}, u32[]{:S(2)}, u32[]{:S(2)}) collective-permute-start(bf16[16,2048]{1,0:T(8,128)(2,1)S(1)} %shard_map.78), channel_id=1, source_target_pairs={{0,4},{4,0},{1,5},{5,1},{2,6},{6,2},{3,7},{7,3},{8,12},{12,8},{9,1... | collective-permute-start | bytes 196616 | tf_op jit(solution)/shard_map/ppermute | solution.py:136

commit v5 on v4

--- a/solution.py
+++ b/solution.py
@@ -40,13 +40,22 @@
     return jnp.where(mask, 1.0, 0.0).astype(BF)
 
 
-def shares_kernel(ids_ref, probs_ref, out_ref):
-    shape = out_ref.shape
-    expert = iota(shape, 1)
-    acc = jnp.zeros(shape, F32)
-    for k in range(ids_ref.shape[1]):
-        acc = acc + jnp.where(ids_ref[:, k : k + 1] == expert, probs_ref[:, k : k + 1].astype(F32), 0.0)
-    out_ref[...] = acc.astype(BF)
+def shares_kernel(ids_hbm, probs_hbm, out_ref, ids, probs, sems):
+    copies = [
+        pltpu.make_async_copy(src, dst, sems.at[k])
+        for k, (src, dst) in enumerate(((ids_hbm, ids), (probs_hbm, probs)))
+    ]
+    for copy in copies:
+        copy.start()
+    for copy in copies:
+        copy.wait()
+    tokens, lanes = out_ref.shape
+    expert = iota((lanes, tokens), 0)
+    acc = jnp.zeros((lanes, tokens), F32)
+    for k in range(ids.shape[0]):
+        acc = acc + jnp.where(ids[k : k + 1, :] == expert, probs[k : k + 1, :].astype(F32), 0.0)
+    eye = flag(iota((tokens, tokens), 0) == iota((tokens, tokens), 1))
+    out_ref[...] = dot(eye, acc.astype(BF), ((1,), (1,))).astype(BF)
 
 
 def payload_kernel(near_ref, far_ref, near_share_ref, far_share_ref, out_ref):
@@ -78,14 +87,12 @@
         sent_ref[:, pl.ds((mine + k) % 2, 1)] = packed.reshape(YS, 1, slots // YS, width)
 
 
-def combine_kernel(give_ref, rows_ref, out_ref):
+def combine_kernel(give_ref, rows_ref, near_ref, far_ref):
     mine = lax.axis_index("zh")
     slots = give_ref.shape[1]
-    own = out_ref.shape[1] // 2
-    for k in range(2):
+    for k, out_ref in ((1, far_ref), (0, near_ref)):
         rows = rows_ref[:, pl.ds((mine + k) % 2, 1)].reshape(slots, -1)
-        part = dot(give_ref[k], rows, ((0,), (0,))).astype(BF)
-        out_ref[:, k * own : (k + 1) * own] = part.reshape(QUAD, own, -1)
+        out_ref[...] = dot(give_ref[k], rows, ((0,), (0,))).astype(BF)
 
 
 def expert_kernel(rows_ref, kept_ref, gate_ref, up_hbm, down_hbm, out_ref, up, down, hidden, sems):
@@ -115,21 +122,19 @@
         out_ref[:, at] = total.astype(BF)
 
 
-def sum_of(parts_ref, at):
-    acc = parts_ref[0, at].astype(F32)
+def sum_of(parts_ref):
+    acc = parts_ref[0].astype(F32)
     for k in range(1, parts_ref.shape[0]):
-        acc = acc + parts_ref[k, at].astype(F32)
+        acc = acc + parts_ref[k].astype(F32)
     return acc
 
 
 def half_kernel(parts_ref, out_ref):
-    own = out_ref.shape[0]
-    out_ref[...] = sum_of(parts_ref, slice(own, 2 * own)).astype(BF)
+    out_ref[...] = sum_of(parts_ref).astype(BF)
 
 
 def total_kernel(parts_ref, far_ref, out_ref):
-    own = out_ref.shape[0]
-    out_ref[...] = (sum_of(parts_ref, slice(0, own)) + far_ref[...].astype(F32)).astype(BF)
+    out_ref[...] = (sum_of(parts_ref) + far_ref[...].astype(F32)).astype(BF)
 
 
 def swapped(x):
@@ -157,11 +162,23 @@
         for h in range(halves)
         for k in range(QUAD)
     ]
+    shares = pl.pallas_call(
+        shares_kernel,
+        out_shape=bf16(tokens, LANES),
+        in_specs=[pl.BlockSpec(memory_space=pl.ANY)] * 2,
+        scratch_shapes=[
+            pltpu.VMEM((expert_ids.shape[2], tokens), jnp.int32),
+            pltpu.VMEM((expert_ids.shape[2], tokens), BF),
+            pltpu.SemaphoreType.DMA((2,)),
+        ],
+        compiler_params=pltpu.CompilerParams(vmem_limit_bytes=58 * MIB),
+        cost_estimate=pl.CostEstimate(flops=10**5, bytes_accessed=10**4, transcendentals=0),
+    )(expert_ids[0].T, gate_probs[0].T)
+    far_shares, cotangent = lax.optimization_barrier((swapped(shares), cotangent))
     crossed = lax.ppermute(cotangent[0], ("section", "zh", "zl"), moves)
     incoming = lax.ppermute(cotangent[0], "section", [(i, (i - 1) % sections) for i in range(sections)])
-    shares = call(shares_kernel, bf16(tokens, LANES), 4, (10**5, 10**4))(expert_ids[0], gate_probs[0])
     payload = call(payload_kernel, bf16(QUAD, 2 * tokens, width + LANES), 4, (10**5, 10**6))(
-        incoming, crossed, shares, swapped(shares)
+        incoming, crossed, shares, far_shares
     )
     sent, give = call(
         lambda *refs: pack_kernel(cap, tokens, *refs),
@@ -186,9 +203,11 @@
         cost_estimate=pl.CostEstimate(flops=24 * 10**8, bytes_accessed=12 * 10**6, transcendentals=0),
     )(across(sent).reshape(slots, width), saved[0, 0], w_gate[0], w_up[0], w_down[0])
     back = across(grads).reshape(sent.shape)
-    parts = quad(call(combine_kernel, bf16(QUAD, 2 * tokens, width), 8, (10**8, 10**6))(give, back))
-    far = swapped(call(half_kernel, bf16(tokens, width), 4, (10**6, 10**6))(parts))
-    out = call(total_kernel, bf16(tokens, width), 4, (10**6, 10**6))(parts, far)
+    near, far = call(combine_kernel, (bf16(half, width), bf16(half, width)), 8, (10**8, 10**6))(give, back)
+    far = quad(far.reshape(QUAD, tokens, width))
+    far = swapped(call(half_kernel, bf16(tokens, width), 4, (10**6, 10**6))(far))
+    near = quad(near.reshape(QUAD, tokens, width))
+    out = call(total_kernel, bf16(tokens, width), 4, (10**6, 10**6))(near, far)
     return out[None]
 
 

time: 122 us -> 128 us (1.049)
  the two profiles are of different devices: /device:TPU:8 before, /device:TPU:32 now
where the time goes in v5:
time: 128 us; the launch traced here: 127 us
  blocking collectives  51.6 us (40%)
  starting transfers between devices  51.2 us (40%)
  waiting for transfers between devices  14.4 us (11%)
  Pallas kernels  9.49 us (7%)
    all_to_all x2, blocking collectives, across(): lax.all_to_all(x.reshape(YS, -1, x.shape[-1]), 'y', 0, 0, tiled=True)  28.7 us
    all_to_all x2, blocking collectives, quad(): return lax.all_to_all(x, 'zl', 0, 0, tiled=True)  22.9 us
    ppermute x2, starting transfers between devices, swapped(): return lax.ppermute(x, 'zh', [(0, 1), (1, 0)])  18.9 us
    ppermute x1, starting transfers between devices, body(): crossed = lax.ppermute(cotangent[0], ('section', 'zh', 'zl'), moves)  18.3 us
    ppermute x1, waiting for transfers between devices, body(): lax.ppermute(cotangent[0], 'section', [(i, (i - 1) % sections) for i in r...  8.79 us
    ppermute x1, starting transfers between devices, body(): lax.ppermute(cotangent[0], 'section', [(i, (i - 1) % sections) for i in r...  8.71 us
    ppermute x2, waiting for transfers between devices, swapped(): return lax.ppermute(x, 'zh', [(0, 1), (1, 0)])  5.58 us
    all_to_all x1, starting transfers between devices, quad(): return lax.all_to_all(x, 'zl', 0, 0, tiled=True)  5.18 us
  transfers between devices with their start and end apart: 5, of which 3 were waited for; matrix products, arithmetic and copies ran while one was open for 0% of the time, Pallas kernels for 0%

profile of v5, /device:TPU:32, one launch (start us, length us, event | category | flops | bytes accessed | tf_op | source)
XLA Modules:
  0.0 127.4 jit_solution(18173282595254026944)
XLA Ops:
  0.0 0.0 copy-start
  0.0 0.0 copy-start.1
  0.0 1.6 %shard_map.73.near_share_ref = bf16[16,128]{1,0:T(8,128)(2,1)} custom-call(s32[8,16]{1,0:T(8,128)} %bitcast.27, bf16[8,16]{1,0:T(8,128)(2,1)} %bitcast.28), custom_call_target="tpu_custom_call" | custom-call | flops 100000 | bytes 10000 | tf_op jit(solution)/shard_map/pallas_call | solution.py:165
  1.6 9.1 %collective-permute-start = (bf16[16,128]{1,0:T(8,128)(2,1)}, bf16[16,128]{1,0:T(8,128)(2,1)S(1)}, u32[]{:S(2)}, u32[]{:S(2)}) collective-permute-start(bf16[16,128]{1,0:T(8,128)(2,1)} %shard_map.73.near_share_ref), channel_id=1, source_target_pairs={{0,4},{4,0},{1,5},{5,1},{2,6},{6,2},{3,7},{7,3},{8,12},{12,8},{9,1... | collective-permute-start | bytes 12296 | tf_op jit(solution)/shard_map/ppermute | solution.py:141
  10.8 1.8 %collective-permute-done.far_share_ref = bf16[16,128]{1,0:T(8,128)(2,1)S(1)} collective-permute-done((bf16[16,128]{1,0:T(8,128)(2,1)}, bf16[16,128]{1,0:T(8,128)(2,1)S(1)}, u32[]{:S(2)}, u32[]{:S(2)}) %collective-permute-start) | collective-permute-done | bytes 4128 | tf_op jit(solution)/shard_map/ppermute | solution.py:141
  12.5 18.3 %collective-permute-start.2 = (bf16[16,2048]{1,0:T(8,128)(2,1)}, bf16[16,2048]{1,0:T(8,128)(2,1)S(1)}, u32[]{:S(2)}, u32[]{:S(2)}) collective-permute-start(bf16[16,2048]{1,0:T(8,128)(2,1)} %bitcast.29), channel_id=1, source_target_pairs={{0,996},{1,997},{2,998},{3,999},{4,992},{5,993},{6,994},{7,995},{3... | collective-permute-start | bytes 196616 | tf_op jit(solution)/shard_map/ppermute | solution.py:178
  30.9 8.7 %collective-permute-start.1 = (bf16[16,2048]{1,0:T(8,128)(2,1)}, bf16[16,2048]{1,0:T(8,128)(2,1)S(1)}, u32[]{:S(2)}, u32[]{:S(2)}) collective-permute-start(bf16[16,2048]{1,0:T(8,128)(2,1)} %bitcast.30), channel_id=1, source_target_pairs={{0,992},{32,0},{64,32},{96,64},{128,96},{160,128},{192,160},{224,1... | collective-permute-start | bytes 196616 | tf_op jit(solution)/shard_map/ppermute | solution.py:179
  39.6 0.0 collective-permute-done.2.far_ref
  39.6 8.8 %collective-permute-done.1.near_ref = bf16[16,2048]{1,0:T(8,128)(2,1)S(1)} collective-permute-done((bf16[16,2048]{1,0:T(8,128)(2,1)}, bf16[16,2048]{1,0:T(8,128)(2,1)S(1)}, u32[]{:S(2)}, u32[]{:S(2)}) %collective-permute-start.1) | collective-permute-done | bytes 65568 | tf_op jit(solution)/shard_map/ppermute | solution.py:179
  48.4 0.0 copy-start.2
  48.4 0.7 copy-done.2
  49.1 12.7 %all_to_all.25.refs_0_ = bf16[4,32,2176]{2,1,0:T(8,128)(2,1)S(1)} all-to-all(bf16[4,32,2176]{2,1,0:T(8,128)(2,1)S(1)} %shard_map.74), channel_id=1, replica_groups=mesh['section'=32,'y'=4,'zh'=2,'zl'=4] {'zl'}, dimensions={0} | all-to-all | bytes 1114112 | tf_op jit(solution)/shard_map/all_to_all | solution.py:145
  61.8 0.9 shard_map.75
  62.7 15.3 %all_to_all.26 = bf16[4,64,2048]{2,1,0:T(8,128)(2,1)S(1)} all-to-all(bf16[4,64,2048]{2,1,0:T(8,128)(2,1)S(1)} %bitcast.22), channel_id=1, replica_groups=mesh['section'=32,'y'=4,'zh'=2,'zl'=4] {'y'}, dimensions={0} | all-to-all | bytes 2097152 | tf_op jit(solution)/shard_map/all_to_all | solution.py:149
  78.1 0.0 copy-done
  78.1 0.0 copy-done.1
  78.1 5.1 %shard_map.76 = bf16[256,2048]{1,0:T(8,128)(2,1)S(1)} custom-call(bf16[256,2048]{1,0:T(8,128)(2,1)S(1)} %bitcast.18, bf16[256,1536]{1,0:T(8,128)(2,1)S(1)} %bitcast.23, bf16[2048,768]{1,0:T(8,128)(2,1)S(1)} %bitcast.21, bf16[2048,768]{1,0:T(8,128)(2,1)} %bitcast.25, bf16[768,2048]{1,0:T(8,128)(2,1)} %bitcast.26), custom_call_target="tpu_custom_call" | custom-call | flops 2400000000 | bytes 12000000 | tf_op jit(solution)/shard_map/pallas_call | solution.py:191
  83.2 13.3 %all_to_all.27 = bf16[4,64,2048]{2,1,0:T(8,128)(2,1)S(1)} all-to-all(bf16[4,64,2048]{2,1,0:T(8,128)(2,1)S(1)} %bitcast.19), channel_id=1, replica_groups=mesh['section'=32,'y'=4,'zh'=2,'zl'=4] {'y'}, dimensions={0} | all-to-all | bytes 2097152 | tf_op jit(solution)/shard_map/all_to_all | solution.py:149
  96.6 1.0 shard_map.77
  97.6 10.2 %all_to_all.28.parts_ref = bf16[4,16,2048]{2,1,0:T(8,128)(2,1)S(1)} all-to-all(bf16[4,16,2048]{2,1,0:T(8,128)(2,1)S(1)} %bitcast.24), channel_id=1, replica_groups=mesh['section'=32,'y'=4,'zh'=2,'zl'=4] {'zl'}, dimensions={0} | all-to-all | bytes 524288 | tf_op jit(solution)/shard_map/all_to_all | solution.py:145
  107.8 5.2 %all-to-all-start.3 = ((bf16[4,16,2048]{2,1,0:T(8,128)(2,1)}), bf16[4,16,2048]{2,1,0:T(8,128)(2,1)S(1)}, u32[]{:S(2)}, u32[]{:S(2)}) async-start(bf16[4,16,2048]{2,1,0:T(8,128)(2,1)} %bitcast.13), calls=%async_computation.3 | async-start | bytes 524288 | tf_op jit(solution)/shard_map/all_to_all | solution.py:145
  113.1 9.8 %collective-permute-start.3 = (bf16[16,2048]{1,0:T(8,128)(2,1)S(1)}, bf16[16,2048]{1,0:T(8,128)(2,1)S(1)}, u32[]{:S(2)}, u32[]{:S(2)}) collective-permute-start(bf16[16,2048]{1,0:T(8,128)(2,1)S(1)} %shard_map.78), channel_id=1, source_target_pairs={{0,4},{4,0},{1,5},{5,1},{2,6},{6,2},{3,7},{7,3},{8,12},{12,8},{9,1... | collective-permute-start | bytes 196616 | tf_op jit(solution)/shard_map/ppermute | solution.py:141
  122.9 0.0 all-to-all-done.3.parts_ref
  122.9 3.8 %collective-permute-done.3.far_ref = bf16[16,2048]{1,0:T(8,128)(2,1)S(1)} collective-permute-done((bf16[16,2048]{1,0:T(8,128)(2,1)S(1)}, bf16[16,2048]{1,0:T(8,128)(2,1)S(1)}, u32[]{:S(2)}, u32[]{:S(2)}) %collective-permute-start.3) | collective-permute-done | bytes 65568 | tf_op jit(solution)/shard_map/ppermute | solution.py:141
  126.7 0.7 shard_map.79
  (2 shorter events, 0.1 us)
Async XLA Ops:
  0.0 78.1 %copy-start = (bf16[1,2048,768]{2,1,0:T(8,128)(2,1)S(1)}, bf16[1,2048,768]{2,1,0:T(8,128)(2,1)}, u32[]{:S(2)}) copy-start(bf16[1,2048,768]{2,1,0:T(8,128)(2,1)} %param.11) | copy-start | bytes 9437188
  0.0 78.1 %copy-start.1 = (bf16[1,1,256,1536]{3,2,1,0:T(8,128)(2,1)S(1)}, bf16[1,1,256,1536]{3,2,1,0:T(8,128)(2,1)}, u32[]{:S(2)}) copy-start(bf16[1,1,256,1536]{3,2,1,0:T(8,128)(2,1)} %param.10) | copy-start | bytes 2359300
  1.6 10.9 %collective-permute-start = (bf16[16,128]{1,0:T(8,128)(2,1)}, bf16[16,128]{1,0:T(8,128)(2,1)S(1)}, u32[]{:S(2)}, u32[]{:S(2)}) collective-permute-start(bf16[16,128]{1,0:T(8,128)(2,1)} %shard_map.73.near_share_ref), channel_id=1, source_target_pairs={{0,4},{4,0},{1,5},{5,1},{2,6},{6,2},{3,7},{7,3},{8,12},{12,8},{9,1... | collective-permute-start | bytes 12296 | tf_op jit(solution)/shard_map/ppermute | solution.py:141
  12.5 27.0 %collective-permute-start.2 = (bf16[16,2048]{1,0:T(8,128)(2,1)}, bf16[16,2048]{1,0:T(8,128)(2,1)S(1)}, u32[]{:S(2)}, u32[]{:S(2)}) collective-permute-start(bf16[16,2048]{1,0:T(8,128)(2,1)} %bitcast.29), channel_id=1, source_target_pairs={{0,996},{1,997},{2,998},{3,999},{4,992},{5,993},{6,994},{7,995},{3... | collective-permute-start | bytes 196616 | tf_op jit(solution)/shard_map/ppermute | solution.py:178
  30.9 17.5 %collective-permute-start.1 = (bf16[16,2048]{1,0:T(8,128)(2,1)}, bf16[16,2048]{1,0:T(8,128)(2,1)S(1)}, u32[]{:S(2)}, u32[]{:S(2)}) collective-permute-start(bf16[16,2048]{1,0:T(8,128)(2,1)} %bitcast.30), channel_id=1, source_target_pairs={{0,992},{32,0},{64,32},{96,64},{128,96},{160,128},{192,160},{224,1... | collective-permute-start | bytes 196616 | tf_op jit(solution)/shard_map/ppermute | solution.py:179
  48.4 0.7 copy-start.2
  107.8 15.1 %all-to-all-start.3 = ((bf16[4,16,2048]{2,1,0:T(8,128)(2,1)}), bf16[4,16,2048]{2,1,0:T(8,128)(2,1)S(1)}, u32[]{:S(2)}, u32[]{:S(2)}) async-start(bf16[4,16,2048]{2,1,0:T(8,128)(2,1)} %bitcast.13), calls=%async_computation.3 | async-start | bytes 524288 | tf_op jit(solution)/shard_map/all_to_all | solution.py:145
  113.1 13.7 %collective-permute-start.3 = (bf16[16,2048]{1,0:T(8,128)(2,1)S(1)}, bf16[16,2048]{1,0:T(8,128)(2,1)S(1)}, u32[]{:S(2)}, u32[]{:S(2)}) collective-permute-start(bf16[16,2048]{1,0:T(8,128)(2,1)S(1)} %shard_map.78), channel_id=1, source_target_pairs={{0,4},{4,0},{1,5},{5,1},{2,6},{6,2},{3,7},{7,3},{8,12},{12,8},{9,1... | collective-permute-start | bytes 196616 | tf_op jit(solution)/shard_map/ppermute | solution.py:141

commit v6 on v3

--- a/solution.py
+++ b/solution.py
@@ -49,16 +49,14 @@
     out_ref[...] = acc.astype(BF)
 
 
-def payload_kernel(rows_ref, share_ref, quad_ref, one_ref):
+def payload_kernel(rows_ref, share_ref, out_ref):
     width = rows_ref.shape[1]
-    one_ref[:, :width] = rows_ref[...]
-    one_ref[:, width:] = share_ref[...]
-    for k in range(QUAD):
-        quad_ref[k, :, :width] = rows_ref[...]
-        quad_ref[k, :, width:] = share_ref[...]
+    for k in range(ZS):
+        out_ref[k, :, :width] = rows_ref[...]
+        out_ref[k, :, width:] = share_ref[...]
 
 
-def pack_kernel(cap, own, near_ref, far_ref, sent_ref, give_ref):
+def pack_kernel(cap, own, rows_ref, sent_ref, give_ref):
     _, slots, toks = give_ref.shape
     width = sent_ref.shape[3]
     mine = lax.axis_index("zh")
@@ -68,12 +66,13 @@
     i, j = iota((toks, toks), 0), iota((toks, toks), 1)
     before = flag((i < j) & (i // own == j // own))
     rr, tt = iota((slots, toks), 0), iota((slots, toks), 1)
-    for k, rows_ref in enumerate((near_ref, far_ref)):
-        share_at = dot(wanted, rows_ref[:, width:], ((1,), (1,)))
+    for k in range(2):
+        rows = rows_ref[pl.ds((mine + k) % 2 * QUAD, QUAD)].reshape(toks, -1)
+        share_at = dot(wanted, rows[:, width:], ((1,), (1,)))
         earlier = dot(flag(share_at > 0), before)
         hit = (share_at > 0) & (tt // own == (rr // cap) % QUAD) & (earlier == (rr % cap).astype(F32))
         give_ref[k] = jnp.where(hit, share_at, 0.0).astype(BF)
-        packed = dot(flag(hit), rows_ref[:, :width]).astype(BF)
+        packed = dot(flag(hit), rows[:, :width]).astype(BF)
         sent_ref[:, pl.ds((mine + k) % 2, 1)] = packed.reshape(YS, 1, slots // YS, width)
 
 
@@ -147,18 +146,14 @@
     half = QUAD * tokens
     incoming = lax.ppermute(cotangent[0], "section", [(i, (i - 1) % sections) for i in range(sections)])
     shares = call(shares_kernel, bf16(tokens, LANES), 4, (10**5, 10**4))(expert_ids[0], gate_probs[0])
-    copies, one = call(
-        payload_kernel, (bf16(QUAD, tokens, width + LANES), bf16(tokens, width + LANES)), 4, (10**5, 10**6)
-    )(incoming, shares)
-    crossed = swapped(one)
-    near_rows = quad(copies)
-    far_rows = quad(jnp.broadcast_to(crossed[None], (QUAD, tokens, width + LANES)))
+    payload = call(payload_kernel, bf16(ZS, tokens, width + LANES), 4, (10**5, 10**6))(incoming, shares)
+    gathered = lax.all_to_all(payload, ("zh", "zl"), 0, 0, tiled=True)
     sent, give = call(
         lambda *refs: pack_kernel(cap, tokens, *refs),
         (bf16(YS, 2, slots // (2 * YS), width), bf16(2, slots // 2, half)),
         8,
         (10**8, 10**6),
-    )(near_rows.reshape(half, -1), far_rows.reshape(half, -1))
+    )(gathered)
     vm = pl.BlockSpec(memory_space=pltpu.VMEM)
     anywhere = pl.BlockSpec(memory_space=pl.ANY)
     grads = pl.pallas_call(

time: 123 us -> 128 us (1.041)
  the two profiles are of different devices: /device:TPU:38 before, /device:TPU:2 now
where the time goes in v6:
time: 128 us
  blocking collectives  81.5 us (64%)
  starting transfers between devices  30.5 us (24%)
  Pallas kernels  7.96 us (6%)
  waiting for transfers between devices  6.3 us (5%)
  local copies, waits for them, and re-layouts  1.53 us (1%)
    all_to_all x1, blocking collectives, body(): gathered = lax.all_to_all(payload, ('zh', 'zl'), 0, 0, tiled=True)  36 us
    all_to_all x2, blocking collectives, across(): lax.all_to_all(x.reshape(YS, -1, x.shape[-1]), 'y', 0, 0, tiled=True)  36 us
    ppermute x1, starting transfers between devices, body(): lax.ppermute(cotangent[0], 'section', [(i, (i - 1) % sections) for i in r...  22.7 us
    all_to_all x1, blocking collectives, quad(): return lax.all_to_all(x, 'zl', 0, 0, tiled=True)  9.5 us
    pallas_call x1, Pallas kernels, body(): pl.pallas_call(expert_kernel, out_shape=bf16(slots, width), in_specs=[vm,...  5.15 us
    ppermute x1, starting transfers between devices, swapped(): return lax.ppermute(x, 'zh', [(0, 1), (1, 0)])  4.47 us
    all_to_all x1, waiting for transfers between devices, quad(): return lax.all_to_all(x, 'zl', 0, 0, tiled=True)  3.63 us
    all_to_all x1, starting transfers between devices, quad(): return lax.all_to_all(x, 'zl', 0, 0, tiled=True)  3.4 us
  transfers between devices with their start and end apart: 3, of which 3 were waited for; matrix products, arithmetic and copies ran while one was open for 1% of the time, Pallas kernels for 0%

profile of v6, /device:TPU:2, one launch (start us, length us, event | category | flops | bytes accessed | tf_op | source)
XLA Modules:
  0.0 127.8 jit_solution(9765894124322513739)
XLA Ops:
  0.0 0.0 copy-start
  0.0 22.7 %collective-permute-start = (bf16[16,2048]{1,0:T(8,128)(2,1)}, bf16[16,2048]{1,0:T(8,128)(2,1)S(1)}, u32[]{:S(2)}, u32[]{:S(2)}) collective-permute-start(bf16[16,2048]{1,0:T(8,128)(2,1)} %bitcast.25), channel_id=1, source_target_pairs={{0,992},{32,0},{64,32},{96,64},{128,96},{160,128},{192,160},{224,1... | collective-permute-start | bytes 196616 | tf_op jit(solution)/shard_map/ppermute | solution.py:147
  22.7 0.8 copy.9.probs_ref
  23.4 0.8 copy.8.ids_ref
  24.2 0.0 copy-start.1
  24.2 0.1 shard_map.73.share_ref
  24.3 0.6 collective-permute-done.rows_ref
  24.9 36.0 %all_to_all.25.refs_0_ = bf16[8,16,2176]{2,1,0:T(8,128)(2,1)S(1)} all-to-all(bf16[8,16,2176]{2,1,0:T(8,128)(2,1)S(1)} %shard_map.74), channel_id=1, replica_groups=mesh['section'=32,'y'=4,'zh'=2,'zl'=4] {'zh','zl'}, dimensions={0} | all-to-all | bytes 1114112 | tf_op jit(solution)/shard_map/all_to_all | solution.py:150
  60.9 0.9 shard_map.75
  61.9 19.4 %all_to_all.26 = bf16[4,64,2048]{2,1,0:T(8,128)(2,1)S(1)} all-to-all(bf16[4,64,2048]{2,1,0:T(8,128)(2,1)S(1)} %bitcast.18), channel_id=1, replica_groups=mesh['section'=32,'y'=4,'zh'=2,'zl'=4] {'y'}, dimensions={0} | all-to-all | bytes 2097152 | tf_op jit(solution)/shard_map/all_to_all | solution.py:138
  81.2 0.0 copy-done
  81.2 0.0 copy-done.1
  81.2 5.1 %shard_map.76 = bf16[256,2048]{1,0:T(8,128)(2,1)S(1)} custom-call(bf16[256,2048]{1,0:T(8,128)(2,1)S(1)} %bitcast.14, bf16[256,1536]{1,0:T(8,128)(2,1)S(1)} %bitcast.19, bf16[2048,768]{1,0:T(8,128)(2,1)S(1)} %bitcast.17, bf16[2048,768]{1,0:T(8,128)(2,1)} %bitcast.21, bf16[768,2048]{1,0:T(8,128)(2,1)} %bitcast.22), custom_call_target="tpu_custom_call" | custom-call | flops 2400000000 | bytes 12000000 | tf_op jit(solution)/shard_map/pallas_call | solution.py:159
  86.4 16.6 %all_to_all.27 = bf16[4,64,2048]{2,1,0:T(8,128)(2,1)S(1)} all-to-all(bf16[4,64,2048]{2,1,0:T(8,128)(2,1)S(1)} %bitcast.15), channel_id=1, replica_groups=mesh['section'=32,'y'=4,'zh'=2,'zl'=4] {'y'}, dimensions={0} | all-to-all | bytes 2097152 | tf_op jit(solution)/shard_map/all_to_all | solution.py:138
  103.0 1.0 shard_map.77
  104.0 9.5 %all_to_all.28.parts_ref = bf16[4,16,2048]{2,1,0:T(8,128)(2,1)S(1)} all-to-all(bf16[4,16,2048]{2,1,0:T(8,128)(2,1)S(1)} %bitcast.20), channel_id=1, replica_groups=mesh['section'=32,'y'=4,'zh'=2,'zl'=4] {'zl'}, dimensions={0} | all-to-all | bytes 524288 | tf_op jit(solution)/shard_map/all_to_all | solution.py:134
  113.5 3.4 %all-to-all-start.3 = ((bf16[4,16,2048]{2,1,0:T(8,128)(2,1)}), bf16[4,16,2048]{2,1,0:T(8,128)(2,1)S(1)}, u32[]{:S(2)}, u32[]{:S(2)}) async-start(bf16[4,16,2048]{2,1,0:T(8,128)(2,1)} %bitcast.11), calls=%async_computation.3 | async-start | bytes 524288 | tf_op jit(solution)/shard_map/all_to_all | solution.py:134
  117.0 4.5 %collective-permute-start.1 = (bf16[16,2048]{1,0:T(8,128)(2,1)S(1)}, bf16[16,2048]{1,0:T(8,128)(2,1)S(1)}, u32[]{:S(2)}, u32[]{:S(2)}) collective-permute-start(bf16[16,2048]{1,0:T(8,128)(2,1)S(1)} %shard_map.78), channel_id=1, source_target_pairs={{0,4},{4,0},{1,5},{5,1},{2,6},{6,2},{3,7},{7,3},{8,12},{12,8},{9,1... | collective-permute-start | bytes 196616 | tf_op jit(solution)/shard_map/ppermute | solution.py:130
  121.4 3.6 %all-to-all-done.3.parts_ref = bf16[4,16,2048]{2,1,0:T(8,128)(2,1)S(1)} async-done(((bf16[4,16,2048]{2,1,0:T(8,128)(2,1)}), bf16[4,16,2048]{2,1,0:T(8,128)(2,1)S(1)}, u32[]{:S(2)}, u32[]{:S(2)}) %all-to-all-start.3) | async-done | bytes 262176 | tf_op jit(solution)/shard_map/all_to_all | solution.py:134
  125.1 2.1 %collective-permute-done.1.far_ref = bf16[16,2048]{1,0:T(8,128)(2,1)S(1)} collective-permute-done((bf16[16,2048]{1,0:T(8,128)(2,1)S(1)}, bf16[16,2048]{1,0:T(8,128)(2,1)S(1)}, u32[]{:S(2)}, u32[]{:S(2)}) %collective-permute-start.1) | collective-permute-done | bytes 65568 | tf_op jit(solution)/shard_map/ppermute | solution.py:130
  127.2 0.7 shard_map.79
  (2 shorter events, 0.1 us)
Async XLA Ops:
  0.0 81.2 %copy-start = (bf16[1,2048,768]{2,1,0:T(8,128)(2,1)S(1)}, bf16[1,2048,768]{2,1,0:T(8,128)(2,1)}, u32[]{:S(2)}) copy-start(bf16[1,2048,768]{2,1,0:T(8,128)(2,1)} %param.11) | copy-start | bytes 9437188
  0.0 24.9 %collective-permute-start = (bf16[16,2048]{1,0:T(8,128)(2,1)}, bf16[16,2048]{1,0:T(8,128)(2,1)S(1)}, u32[]{:S(2)}, u32[]{:S(2)}) collective-permute-start(bf16[16,2048]{1,0:T(8,128)(2,1)} %bitcast.25), channel_id=1, source_target_pairs={{0,992},{32,0},{64,32},{96,64},{128,96},{160,128},{192,160},{224,1... | collective-permute-start | bytes 196616 | tf_op jit(solution)/shard_map/ppermute | solution.py:147
  24.2 57.0 %copy-start.1 = (bf16[1,1,256,1536]{3,2,1,0:T(8,128)(2,1)S(1)}, bf16[1,1,256,1536]{3,2,1,0:T(8,128)(2,1)}, u32[]{:S(2)}) copy-start(bf16[1,1,256,1536]{3,2,1,0:T(8,128)(2,1)} %param.10) | copy-start | bytes 2359300
  113.5 11.6 %all-to-all-start.3 = ((bf16[4,16,2048]{2,1,0:T(8,128)(2,1)}), bf16[4,16,2048]{2,1,0:T(8,128)(2,1)S(1)}, u32[]{:S(2)}, u32[]{:S(2)}) async-start(bf16[4,16,2048]{2,1,0:T(8,128)(2,1)} %bitcast.11), calls=%async_computation.3 | async-start | bytes 524288 | tf_op jit(solution)/shard_map/all_to_all | solution.py:134
  117.0 10.2 %collective-permute-start.1 = (bf16[16,2048]{1,0:T(8,128)(2,1)S(1)}, bf16[16,2048]{1,0:T(8,128)(2,1)S(1)}, u32[]{:S(2)}, u32[]{:S(2)}) collective-permute-start(bf16[16,2048]{1,0:T(8,128)(2,1)S(1)} %shard_map.78), channel_id=1, source_target_pairs={{0,4},{4,0},{1,5},{5,1},{2,6},{6,2},{3,7},{7,3},{8,12},{12,8},{9,1... | collective-permute-start | bytes 196616 | tf_op jit(solution)/shard_map/ppermute | solution.py:130

commit v7 on v5

--- a/solution.py
+++ b/solution.py
@@ -58,13 +58,14 @@
     out_ref[...] = dot(eye, acc.astype(BF), ((1,), (1,))).astype(BF)
 
 
-def payload_kernel(near_ref, far_ref, near_share_ref, far_share_ref, out_ref):
+def payload_kernel(near_ref, far_ref, near_share_ref, early_ref, late_ref, out_ref):
     own, width = near_ref.shape
+    far_share = early_ref[...] + late_ref[...]
     for k in range(QUAD):
         out_ref[k, :own, :width] = near_ref[...]
         out_ref[k, own:, :width] = far_ref[...]
         out_ref[k, :own, width:] = near_share_ref[...]
-        out_ref[k, own:, width:] = far_share_ref[...]
+        out_ref[k, own:, width:] = far_share
 
 
 def pack_kernel(cap, own, rows_ref, sent_ref, give_ref):
@@ -104,10 +105,14 @@
         for k in range(parts):
             at = pl.ds(k * step, step)
             copy = pltpu.make_async_copy(src.at[at], dst.at[at], sems.at[len(begun)])
-            copy.start()
             begun.append((copy, at))
     for copy, at in begun[:parts]:
+        copy.start()
+    for k, (copy, at) in enumerate(begun[:parts]):
         copy.wait()
+        if k == 0:
+            for later, _ in begun[parts:]:
+                later.start()
         hidden[:, at] = dot(rows_ref[...], down[at, :], ((1,), (1,)))
     h = hidden[...]
     g = kept_ref[:, :ff].astype(F32)
@@ -174,11 +179,16 @@
         compiler_params=pltpu.CompilerParams(vmem_limit_bytes=58 * MIB),
         cost_estimate=pl.CostEstimate(flops=10**5, bytes_accessed=10**4, transcendentals=0),
     )(expert_ids[0].T, gate_probs[0].T)
-    far_shares, cotangent = lax.optimization_barrier((swapped(shares), cotangent))
+    early, late = (
+        [(q * halves + h, q * halves + (h + 1) % halves) for q in range(first, sections, 2) for h in range(halves)]
+        for first in (0, 1)
+    )
+    early_shares, cotangent = lax.optimization_barrier((lax.ppermute(shares, ("section", "zh"), early), cotangent))
+    late_shares = lax.ppermute(shares, ("section", "zh"), late)
     crossed = lax.ppermute(cotangent[0], ("section", "zh", "zl"), moves)
     incoming = lax.ppermute(cotangent[0], "section", [(i, (i - 1) % sections) for i in range(sections)])
     payload = call(payload_kernel, bf16(QUAD, 2 * tokens, width + LANES), 4, (10**5, 10**6))(
-        incoming, crossed, shares, far_shares
+        incoming, crossed, shares, early_shares, late_shares
     )
     sent, give = call(
         lambda *refs: pack_kernel(cap, tokens, *refs),

time: 128 us -> 129 us (level)
  blocking collectives: 51.6 us -> 59.1 us
  waiting for transfers between devices: 14.4 us -> 8.6 us
    ppermute x2 -> x1, starting transfers between devices: 18.9 us -> 9.1 us  [swapped(): return lax.ppermute(x, 'zh', [(0, 1), (1, 0)])]
    ppermute x0 -> x2, starting transfers between devices: none -> 9.76 us  [the longest x1 9.1 us: body(): lax.ppermute(shares, ('section', 'zh'), early)]
    ppermute x1, starting transfers between devices: 18.3 us -> 10.5 us  [body(): crossed = lax.ppermute(cotangent[0], ('section', 'zh', 'zl'), moves)]
    ppermute x1, starting transfers between devices: 8.71 us -> 16.5 us  [body(): lax.ppermute(cotangent[0], 'section', [(i, (i - 1) % sections) for i in r...]
    ppermute x1, waiting for transfers between devices: 8.79 us -> 3.02 us  [body(): lax.ppermute(cotangent[0], 'section', [(i, (i - 1) % sections) for i in r...]
    all_to_all x2, blocking collectives: 22.9 us -> 27.9 us  [quad(): return lax.all_to_all(x, 'zl', 0, 0, tiled=True)]
    all_to_all x2, blocking collectives: 28.7 us -> 31.2 us  [across(): lax.all_to_all(x.reshape(YS, -1, x.shape[-1]), 'y', 0, 0, tiled=True)]
    ppermute x0 -> x2, waiting for transfers between devices: none -> 1.78 us  [the longest x1 1.78 us: body(): lax.ppermute(shares, ('section', 'zh'), early)]
  transfers between devices with their start and end apart: 5 -> 6, of which waited for: 3 -> 3; matrix products, arithmetic and copies ran while one was open for 0% -> 0% of each run, Pallas kernels for 0% -> 0%
where the time goes in v7:
time: 129 us; the launch traced here: 128 us
  blocking collectives  59.1 us (46%)
  starting transfers between devices  50.2 us (39%)
  Pallas kernels  9.49 us (7%)
  waiting for transfers between devices  8.6 us (7%)
    all_to_all x2, blocking collectives, across(): lax.all_to_all(x.reshape(YS, -1, x.shape[-1]), 'y', 0, 0, tiled=True)  31.2 us
    all_to_all x2, blocking collectives, quad(): return lax.all_to_all(x, 'zl', 0, 0, tiled=True)  27.9 us
    ppermute x1, starting transfers between devices, body(): lax.ppermute(cotangent[0], 'section', [(i, (i - 1) % sections) for i in r...  16.5 us
    ppermute x1, starting transfers between devices, body(): crossed = lax.ppermute(cotangent[0], ('section', 'zh', 'zl'), moves)  10.5 us
    ppermute x1, starting transfers between devices, swapped(): return lax.ppermute(x, 'zh', [(0, 1), (1, 0)])  9.1 us
    ppermute x1, starting transfers between devices, body(): lax.ppermute(shares, ('section', 'zh'), early)  9.1 us
    pallas_call x1, Pallas kernels, body(): pl.pallas_call(expert_kernel, out_shape=bf16(slots, width), in_specs=[vm,...  5.15 us
    all_to_all x1, starting transfers between devices, quad(): return lax.all_to_all(x, 'zl', 0, 0, tiled=True)  4.29 us
  transfers between devices with their start and end apart: 6, of which 3 were waited for; matrix products, arithmetic and copies ran while one was open for 0% of the time, Pallas kernels for 0%

profile of v7, /device:TPU:32, one launch (start us, length us, event | category | flops | bytes accessed | tf_op | source)
XLA Modules:
  0.0 128.2 jit_solution(3284927286995221522)
XLA Ops:
  0.0 0.0 copy-start
  0.0 0.0 copy-start.1
  0.0 1.6 %shard_map.73.near_share_ref = bf16[16,128]{1,0:T(8,128)(2,1)} custom-call(s32[8,16]{1,0:T(8,128)} %bitcast.27, bf16[8,16]{1,0:T(8,128)(2,1)} %bitcast.28), custom_call_target="tpu_custom_call" | custom-call | flops 100000 | bytes 10000 | tf_op jit(solution)/shard_map/pallas_call | solution.py:170
  1.6 9.1 %collective-permute-start = (bf16[16,128]{1,0:T(8,128)(2,1)}, bf16[16,128]{1,0:T(8,128)(2,1)S(1)}, u32[]{:S(2)}, u32[]{:S(2)}) collective-permute-start(bf16[16,128]{1,0:T(8,128)(2,1)} %shard_map.73.near_share_ref), channel_id=1, source_target_pairs={{0,4},{4,0},{64,68},{68,64},{128,132},{132,128},{192,196},{196,192... | collective-permute-start | bytes 12296 | tf_op jit(solution)/shard_map/ppermute | solution.py:186
  10.8 1.8 %collective-permute-done.early_ref = bf16[16,128]{1,0:T(8,128)(2,1)S(1)} collective-permute-done((bf16[16,128]{1,0:T(8,128)(2,1)}, bf16[16,128]{1,0:T(8,128)(2,1)S(1)}, u32[]{:S(2)}, u32[]{:S(2)}) %collective-permute-start) | collective-permute-done | bytes 4128 | tf_op jit(solution)/shard_map/ppermute | solution.py:186
  12.5 10.5 %collective-permute-start.2 = (bf16[16,2048]{1,0:T(8,128)(2,1)}, bf16[16,2048]{1,0:T(8,128)(2,1)S(1)}, u32[]{:S(2)}, u32[]{:S(2)}) collective-permute-start(bf16[16,2048]{1,0:T(8,128)(2,1)} %bitcast.29), channel_id=1, source_target_pairs={{0,996},{1,997},{2,998},{3,999},{4,992},{5,993},{6,994},{7,995},{3... | collective-permute-start | bytes 196616 | tf_op jit(solution)/shard_map/ppermute | solution.py:188
  23.1 16.5 %collective-permute-start.1 = (bf16[16,2048]{1,0:T(8,128)(2,1)}, bf16[16,2048]{1,0:T(8,128)(2,1)S(1)}, u32[]{:S(2)}, u32[]{:S(2)}) collective-permute-start(bf16[16,2048]{1,0:T(8,128)(2,1)} %bitcast.30), channel_id=1, source_target_pairs={{0,992},{32,0},{64,32},{96,64},{128,96},{160,128},{192,160},{224,1... | collective-permute-start | bytes 196616 | tf_op jit(solution)/shard_map/ppermute | solution.py:189
  39.6 0.7 collective-permute-start.3
  40.2 0.0 collective-permute-done.3.late_ref
  40.3 0.0 collective-permute-done.2.far_ref
  40.3 3.0 %collective-permute-done.1.near_ref = bf16[16,2048]{1,0:T(8,128)(2,1)S(1)} collective-permute-done((bf16[16,2048]{1,0:T(8,128)(2,1)}, bf16[16,2048]{1,0:T(8,128)(2,1)S(1)}, u32[]{:S(2)}, u32[]{:S(2)}) %collective-permute-start.1) | collective-permute-done | bytes 65568 | tf_op jit(solution)/shard_map/ppermute | solution.py:189
  43.3 0.0 copy-start.2
  43.3 0.7 copy-done.2
  44.0 16.5 %all_to_all.25.refs_0_ = bf16[4,32,2176]{2,1,0:T(8,128)(2,1)S(1)} all-to-all(bf16[4,32,2176]{2,1,0:T(8,128)(2,1)S(1)} %shard_map.74), channel_id=1, replica_groups=mesh['section'=32,'y'=4,'zh'=2,'zl'=4] {'zl'}, dimensions={0} | all-to-all | bytes 1114112 | tf_op jit(solution)/shard_map/all_to_all | solution.py:150
  60.5 0.9 shard_map.75
  61.4 16.7 %all_to_all.26 = bf16[4,64,2048]{2,1,0:T(8,128)(2,1)S(1)} all-to-all(bf16[4,64,2048]{2,1,0:T(8,128)(2,1)S(1)} %bitcast.22), channel_id=1, replica_groups=mesh['section'=32,'y'=4,'zh'=2,'zl'=4] {'y'}, dimensions={0} | all-to-all | bytes 2097152 | tf_op jit(solution)/shard_map/all_to_all | solution.py:154
  78.1 0.0 copy-done
  78.1 0.0 copy-done.1
  78.1 5.1 %shard_map.76 = bf16[256,2048]{1,0:T(8,128)(2,1)S(1)} custom-call(bf16[256,2048]{1,0:T(8,128)(2,1)S(1)} %bitcast.18, bf16[256,1536]{1,0:T(8,128)(2,1)S(1)} %bitcast.23, bf16[2048,768]{1,0:T(8,128)(2,1)S(1)} %bitcast.21, bf16[2048,768]{1,0:T(8,128)(2,1)} %bitcast.25, bf16[768,2048]{1,0:T(8,128)(2,1)} %bitcast.26), custom_call_target="tpu_custom_call" | custom-call | flops 2400000000 | bytes 12000000 | tf_op jit(solution)/shard_map/pallas_call | solution.py:201
  83.3 14.6 %all_to_all.27 = bf16[4,64,2048]{2,1,0:T(8,128)(2,1)S(1)} all-to-all(bf16[4,64,2048]{2,1,0:T(8,128)(2,1)S(1)} %bitcast.19), channel_id=1, replica_groups=mesh['section'=32,'y'=4,'zh'=2,'zl'=4] {'y'}, dimensions={0} | all-to-all | bytes 2097152 | tf_op jit(solution)/shard_map/all_to_all | solution.py:154
  97.8 1.0 shard_map.77
  98.9 11.4 %all_to_all.28.parts_ref = bf16[4,16,2048]{2,1,0:T(8,128)(2,1)S(1)} all-to-all(bf16[4,16,2048]{2,1,0:T(8,128)(2,1)S(1)} %bitcast.24), channel_id=1, replica_groups=mesh['section'=32,'y'=4,'zh'=2,'zl'=4] {'zl'}, dimensions={0} | all-to-all | bytes 524288 | tf_op jit(solution)/shard_map/all_to_all | solution.py:150
  110.2 4.3 %all-to-all-start.3 = ((bf16[4,16,2048]{2,1,0:T(8,128)(2,1)}), bf16[4,16,2048]{2,1,0:T(8,128)(2,1)S(1)}, u32[]{:S(2)}, u32[]{:S(2)}) async-start(bf16[4,16,2048]{2,1,0:T(8,128)(2,1)} %bitcast.13), calls=%async_computation.3 | async-start | bytes 524288 | tf_op jit(solution)/shard_map/all_to_all | solution.py:150
  114.6 9.1 %collective-permute-start.4 = (bf16[16,2048]{1,0:T(8,128)(2,1)S(1)}, bf16[16,2048]{1,0:T(8,128)(2,1)S(1)}, u32[]{:S(2)}, u32[]{:S(2)}) collective-permute-start(bf16[16,2048]{1,0:T(8,128)(2,1)S(1)} %shard_map.78), channel_id=1, source_target_pairs={{0,4},{4,0},{1,5},{5,1},{2,6},{6,2},{3,7},{7,3},{8,12},{12,8},{9,1... | collective-permute-start | bytes 196616 | tf_op jit(solution)/shard_map/ppermute | solution.py:146
  123.7 0.0 all-to-all-done.3.parts_ref
  123.7 3.8 %collective-permute-done.4.far_ref = bf16[16,2048]{1,0:T(8,128)(2,1)S(1)} collective-permute-done((bf16[16,2048]{1,0:T(8,128)(2,1)S(1)}, bf16[16,2048]{1,0:T(8,128)(2,1)S(1)}, u32[]{:S(2)}, u32[]{:S(2)}) %collective-permute-start.4) | collective-permute-done | bytes 65568 | tf_op jit(solution)/shard_map/ppermute | solution.py:146
  127.5 0.7 shard_map.79
  (2 shorter events, 0.1 us)
Async XLA Ops:
  0.0 78.1 %copy-start = (bf16[1,2048,768]{2,1,0:T(8,128)(2,1)S(1)}, bf16[1,2048,768]{2,1,0:T(8,128)(2,1)}, u32[]{:S(2)}) copy-start(bf16[1,2048,768]{2,1,0:T(8,128)(2,1)} %param.11) | copy-start | bytes 9437188
  0.0 78.1 %copy-start.1 = (bf16[1,1,256,1536]{3,2,1,0:T(8,128)(2,1)S(1)}, bf16[1,1,256,1536]{3,2,1,0:T(8,128)(2,1)}, u32[]{:S(2)}) copy-start(bf16[1,1,256,1536]{3,2,1,0:T(8,128)(2,1)} %param.10) | copy-start | bytes 2359300
  1.6 10.9 %collective-permute-start = (bf16[16,128]{1,0:T(8,128)(2,1)}, bf16[16,128]{1,0:T(8,128)(2,1)S(1)}, u32[]{:S(2)}, u32[]{:S(2)}) collective-permute-start(bf16[16,128]{1,0:T(8,128)(2,1)} %shard_map.73.near_share_ref), channel_id=1, source_target_pairs={{0,4},{4,0},{64,68},{68,64},{128,132},{132,128},{192,196},{196,192... | collective-permute-start | bytes 12296 | tf_op jit(solution)/shard_map/ppermute | solution.py:186
  12.5 27.7 %collective-permute-start.2 = (bf16[16,2048]{1,0:T(8,128)(2,1)}, bf16[16,2048]{1,0:T(8,128)(2,1)S(1)}, u32[]{:S(2)}, u32[]{:S(2)}) collective-permute-start(bf16[16,2048]{1,0:T(8,128)(2,1)} %bitcast.29), channel_id=1, source_target_pairs={{0,996},{1,997},{2,998},{3,999},{4,992},{5,993},{6,994},{7,995},{3... | collective-permute-start | bytes 196616 | tf_op jit(solution)/shard_map/ppermute | solution.py:188
  23.1 20.2 %collective-permute-start.1 = (bf16[16,2048]{1,0:T(8,128)(2,1)}, bf16[16,2048]{1,0:T(8,128)(2,1)S(1)}, u32[]{:S(2)}, u32[]{:S(2)}) collective-permute-start(bf16[16,2048]{1,0:T(8,128)(2,1)} %bitcast.30), channel_id=1, source_target_pairs={{0,992},{32,0},{64,32},{96,64},{128,96},{160,128},{192,160},{224,1... | collective-permute-start | bytes 196616 | tf_op jit(solution)/shard_map/ppermute | solution.py:189
  39.6 0.7 collective-permute-start.3
  43.3 0.7 copy-start.2
  110.2 13.4 %all-to-all-start.3 = ((bf16[4,16,2048]{2,1,0:T(8,128)(2,1)}), bf16[4,16,2048]{2,1,0:T(8,128)(2,1)S(1)}, u32[]{:S(2)}, u32[]{:S(2)}) async-start(bf16[4,16,2048]{2,1,0:T(8,128)(2,1)} %bitcast.13), calls=%async_computation.3 | async-start | bytes 524288 | tf_op jit(solution)/shard_map/all_to_all | solution.py:150
  114.6 12.9 %collective-permute-start.4 = (bf16[16,2048]{1,0:T(8,128)(2,1)S(1)}, bf16[16,2048]{1,0:T(8,128)(2,1)S(1)}, u32[]{:S(2)}, u32[]{:S(2)}) collective-permute-start(bf16[16,2048]{1,0:T(8,128)(2,1)S(1)} %shard_map.78), channel_id=1, source_target_pairs={{0,4},{4,0},{1,5},{5,1},{2,6},{6,2},{3,7},{7,3},{8,12},{12,8},{9,1... | collective-permute-start | bytes 196616 | tf_op jit(solution)/shard_map/ppermute | solution.py:146

commit v8 on v6

--- a/solution.py
+++ b/solution.py
@@ -12,7 +12,8 @@
 QUAD = 4
 LANES = 128
 MIB = 1 << 20
-PARTS = 2
+DOWN_PARTS = 3
+UP_PARTS = 4
 
 
 def call(kernel, outs, limit, cost):
@@ -51,9 +52,15 @@
 
 def payload_kernel(rows_ref, share_ref, out_ref):
     width = rows_ref.shape[1]
-    for k in range(ZS):
-        out_ref[k, :, :width] = rows_ref[...]
-        out_ref[k, :, width:] = share_ref[...]
+    out_ref[:, :width] = rows_ref[...]
+    out_ref[:, width:] = share_ref[...]
+
+
+def copies_kernel(near_ref, far_ref, out_ref):
+    own = near_ref.shape[0]
+    for k in range(QUAD):
+        out_ref[k, :own] = near_ref[...]
+        out_ref[k, own:] = far_ref[...]
 
 
 def pack_kernel(cap, own, rows_ref, sent_ref, give_ref):
@@ -67,7 +74,7 @@
     before = flag((i < j) & (i // own == j // own))
     rr, tt = iota((slots, toks), 0), iota((slots, toks), 1)
     for k in range(2):
-        rows = rows_ref[pl.ds((mine + k) % 2 * QUAD, QUAD)].reshape(toks, -1)
+        rows = rows_ref[:, k * own : (k + 1) * own, :].reshape(toks, -1)
         share_at = dot(wanted, rows[:, width:], ((1,), (1,)))
         earlier = dot(flag(share_at > 0), before)
         hit = (share_at > 0) & (tt // own == (rr // cap) % QUAD) & (earlier == (rr % cap).astype(F32))
@@ -86,16 +93,15 @@
 
 def expert_kernel(rows_ref, kept_ref, gate_ref, up_hbm, down_hbm, out_ref, up, down, hidden, sems):
     ff, width = down.shape
-    parts = sems.shape[0] // 2
     begun = []
-    for src, dst in ((down_hbm, down), (up_hbm, up)):
+    for src, dst, parts in ((down_hbm, down, DOWN_PARTS), (up_hbm, up, UP_PARTS)):
         step = src.shape[0] // parts
         for k in range(parts):
             at = pl.ds(k * step, step)
             copy = pltpu.make_async_copy(src.at[at], dst.at[at], sems.at[len(begun)])
             copy.start()
             begun.append((copy, at))
-    for copy, at in begun[:parts]:
+    for copy, at in begun[:DOWN_PARTS]:
         copy.wait()
         hidden[:, at] = dot(rows_ref[...], down[at, :], ((1,), (1,)))
     h = hidden[...]
@@ -105,7 +111,7 @@
     hs = h * s
     up_grad = (hs * g).astype(BF)
     gate_grad = (hs * u * (1.0 + g * (1.0 - s))).astype(BF)
-    for copy, at in begun[parts:]:
+    for copy, at in begun[DOWN_PARTS:]:
         copy.wait()
         total = dot(gate_grad, gate_ref[at, :], ((1,), (1,))) + dot(up_grad, up[at, :], ((1,), (1,)))
         out_ref[:, at] = total.astype(BF)
@@ -146,14 +152,14 @@
     half = QUAD * tokens
     incoming = lax.ppermute(cotangent[0], "section", [(i, (i - 1) % sections) for i in range(sections)])
     shares = call(shares_kernel, bf16(tokens, LANES), 4, (10**5, 10**4))(expert_ids[0], gate_probs[0])
-    payload = call(payload_kernel, bf16(ZS, tokens, width + LANES), 4, (10**5, 10**6))(incoming, shares)
-    gathered = lax.all_to_all(payload, ("zh", "zl"), 0, 0, tiled=True)
+    one = call(payload_kernel, bf16(tokens, width + LANES), 4, (10**5, 10**6))(incoming, shares)
+    payload = call(copies_kernel, bf16(QUAD, 2 * tokens, width + LANES), 4, (10**5, 10**6))(one, swapped(one))
     sent, give = call(
         lambda *refs: pack_kernel(cap, tokens, *refs),
         (bf16(YS, 2, slots // (2 * YS), width), bf16(2, slots // 2, half)),
         8,
         (10**8, 10**6),
-    )(gathered)
+    )(quad(payload))
     vm = pl.BlockSpec(memory_space=pltpu.VMEM)
     anywhere = pl.BlockSpec(memory_space=pl.ANY)
     grads = pl.pallas_call(
@@ -165,7 +171,7 @@
             pltpu.VMEM(w_up.shape[1:], BF),
             pltpu.VMEM(w_down.shape[1:], BF),
             pltpu.VMEM((slots, w_down.shape[1]), F32),
-            pltpu.SemaphoreType.DMA((2 * PARTS,)),
+            pltpu.SemaphoreType.DMA((DOWN_PARTS + UP_PARTS,)),
         ],
         compiler_params=pltpu.CompilerParams(vmem_limit_bytes=48 * MIB),
         cost_estimate=pl.CostEstimate(flops=24 * 10**8, bytes_accessed=12 * 10**6, transcendentals=0),

time: 128 us -> 125 us (0.977)
  the two profiles are of different devices: /device:TPU:2 before, /device:TPU:34 now
where the time goes in v8:
time: 125 us; the launch traced here: 124 us
  blocking collectives  60.7 us (49%)
  starting transfers between devices  39.9 us (32%)
  waiting for transfers between devices  11.8 us (9%)
  Pallas kernels  10.3 us (8%)
  local copies, waits for them, and re-layouts  1.53 us (1%)
    all_to_all x2, blocking collectives, across(): lax.all_to_all(x.reshape(YS, -1, x.shape[-1]), 'y', 0, 0, tiled=True)  32.2 us
    all_to_all x2, blocking collectives, quad(): return lax.all_to_all(x, 'zl', 0, 0, tiled=True)  28.5 us
    ppermute x1, starting transfers between devices, body(): lax.ppermute(cotangent[0], 'section', [(i, (i - 1) % sections) for i in r...  21.8 us
    ppermute x2, starting transfers between devices, swapped(): return lax.ppermute(x, 'zh', [(0, 1), (1, 0)])  13.8 us
    ppermute x2, waiting for transfers between devices, swapped(): return lax.ppermute(x, 'zh', [(0, 1), (1, 0)])  11.2 us
    pallas_call x1, Pallas kernels, body(): pl.pallas_call(expert_kernel, out_shape=bf16(slots, width), in_specs=[vm,...  7.5 us
    all_to_all x1, starting transfers between devices, quad(): return lax.all_to_all(x, 'zl', 0, 0, tiled=True)  4.29 us
  transfers between devices with their start and end apart: 4, of which 3 were waited for; matrix products, arithmetic and copies ran while one was open for 1% of the time, Pallas kernels for 0%

profile of v8, /device:TPU:34, one launch (start us, length us, event | category | flops | bytes accessed | tf_op | source)
XLA Modules:
  0.0 124.3 jit_solution(12516142537413641825)
XLA Ops:
  0.0 0.0 copy-start
  0.0 21.8 %collective-permute-start = (bf16[16,2048]{1,0:T(8,128)(2,1)}, bf16[16,2048]{1,0:T(8,128)(2,1)S(1)}, u32[]{:S(2)}, u32[]{:S(2)}) collective-permute-start(bf16[16,2048]{1,0:T(8,128)(2,1)} %bitcast.25), channel_id=1, source_target_pairs={{0,992},{32,0},{64,32},{96,64},{128,96},{160,128},{192,160},{224,1... | collective-permute-start | bytes 196616 | tf_op jit(solution)/shard_map/ppermute | solution.py:153
  21.8 0.8 copy.9.probs_ref
  22.5 0.8 copy.8.ids_ref
  23.3 0.0 copy-start.1
  23.3 0.1 shard_map.73.share_ref
  23.4 0.6 collective-permute-done.rows_ref
  24.0 4.3 %collective-permute-start.1 = (bf16[16,2176]{1,0:T(8,128)(2,1)S(1)}, bf16[16,2176]{1,0:T(8,128)(2,1)S(1)}, u32[]{:S(2)}, u32[]{:S(2)}) collective-permute-start(bf16[16,2176]{1,0:T(8,128)(2,1)S(1)} %shard_map.74.near_ref), channel_id=1, source_target_pairs={{0,4},{4,0},{1,5},{5,1},{2,6},{6,2},{3,7},{7,3},{8,12},{12,8},{9,1... | collective-permute-start | bytes 208904 | tf_op jit(solution)/shard_map/ppermute | solution.py:136
  28.3 7.4 %collective-permute-done.1.far_ref = bf16[16,2176]{1,0:T(8,128)(2,1)S(1)} collective-permute-done((bf16[16,2176]{1,0:T(8,128)(2,1)S(1)}, bf16[16,2176]{1,0:T(8,128)(2,1)S(1)}, u32[]{:S(2)}, u32[]{:S(2)}) %collective-permute-start.1) | collective-permute-done | bytes 69664 | tf_op jit(solution)/shard_map/ppermute | solution.py:136
  35.7 16.1 %all_to_all.25.refs_0_ = bf16[4,32,2176]{2,1,0:T(8,128)(2,1)S(1)} all-to-all(bf16[4,32,2176]{2,1,0:T(8,128)(2,1)S(1)} %shard_map.75), channel_id=1, replica_groups=mesh['section'=32,'y'=4,'zh'=2,'zl'=4] {'zl'}, dimensions={0} | all-to-all | bytes 1114112 | tf_op jit(solution)/shard_map/all_to_all | solution.py:140
  51.8 0.9 shard_map.76
  52.7 17.6 %all_to_all.26 = bf16[4,64,2048]{2,1,0:T(8,128)(2,1)S(1)} all-to-all(bf16[4,64,2048]{2,1,0:T(8,128)(2,1)S(1)} %bitcast.18), channel_id=1, replica_groups=mesh['section'=32,'y'=4,'zh'=2,'zl'=4] {'y'}, dimensions={0} | all-to-all | bytes 2097152 | tf_op jit(solution)/shard_map/all_to_all | solution.py:144
  70.4 0.0 copy-done
  70.4 0.0 copy-done.1
  70.4 7.5 %shard_map.77 = bf16[256,2048]{1,0:T(8,128)(2,1)S(1)} custom-call(bf16[256,2048]{1,0:T(8,128)(2,1)S(1)} %bitcast.14, bf16[256,1536]{1,0:T(8,128)(2,1)S(1)} %bitcast.19, bf16[2048,768]{1,0:T(8,128)(2,1)S(1)} %bitcast.17, bf16[2048,768]{1,0:T(8,128)(2,1)} %bitcast.21, bf16[768,2048]{1,0:T(8,128)(2,1)} %bitcast.22), custom_call_target="tpu_custom_call" | custom-call | flops 2400000000 | bytes 12000000 | tf_op jit(solution)/shard_map/pallas_call | solution.py:165
  77.9 14.6 %all_to_all.27 = bf16[4,64,2048]{2,1,0:T(8,128)(2,1)S(1)} all-to-all(bf16[4,64,2048]{2,1,0:T(8,128)(2,1)S(1)} %bitcast.15), channel_id=1, replica_groups=mesh['section'=32,'y'=4,'zh'=2,'zl'=4] {'y'}, dimensions={0} | all-to-all | bytes 2097152 | tf_op jit(solution)/shard_map/all_to_all | solution.py:144
  92.5 1.0 shard_map.78
  93.5 12.4 %all_to_all.28.parts_ref = bf16[4,16,2048]{2,1,0:T(8,128)(2,1)S(1)} all-to-all(bf16[4,16,2048]{2,1,0:T(8,128)(2,1)S(1)} %bitcast.20), channel_id=1, replica_groups=mesh['section'=32,'y'=4,'zh'=2,'zl'=4] {'zl'}, dimensions={0} | all-to-all | bytes 524288 | tf_op jit(solution)/shard_map/all_to_all | solution.py:140
  105.9 4.3 %all-to-all-start.3 = ((bf16[4,16,2048]{2,1,0:T(8,128)(2,1)}), bf16[4,16,2048]{2,1,0:T(8,128)(2,1)S(1)}, u32[]{:S(2)}, u32[]{:S(2)}) async-start(bf16[4,16,2048]{2,1,0:T(8,128)(2,1)} %bitcast.11), calls=%async_computation.3 | async-start | bytes 524288 | tf_op jit(solution)/shard_map/all_to_all | solution.py:140
  110.2 9.6 %collective-permute-start.2 = (bf16[16,2048]{1,0:T(8,128)(2,1)S(1)}, bf16[16,2048]{1,0:T(8,128)(2,1)S(1)}, u32[]{:S(2)}, u32[]{:S(2)}) collective-permute-start(bf16[16,2048]{1,0:T(8,128)(2,1)S(1)} %shard_map.79), channel_id=1, source_target_pairs={{0,4},{4,0},{1,5},{5,1},{2,6},{6,2},{3,7},{7,3},{8,12},{12,8},{9,1... | collective-permute-start | bytes 196616 | tf_op jit(solution)/shard_map/ppermute | solution.py:136
  119.8 0.0 all-to-all-done.3.parts_ref
  119.8 3.8 %collective-permute-done.2.far_ref = bf16[16,2048]{1,0:T(8,128)(2,1)S(1)} collective-permute-done((bf16[16,2048]{1,0:T(8,128)(2,1)S(1)}, bf16[16,2048]{1,0:T(8,128)(2,1)S(1)}, u32[]{:S(2)}, u32[]{:S(2)}) %collective-permute-start.2) | collective-permute-done | bytes 65568 | tf_op jit(solution)/shard_map/ppermute | solution.py:136
  123.6 0.7 shard_map.80
  (3 shorter events, 0.1 us)
Async XLA Ops:
  0.0 70.4 %copy-start = (bf16[1,2048,768]{2,1,0:T(8,128)(2,1)S(1)}, bf16[1,2048,768]{2,1,0:T(8,128)(2,1)}, u32[]{:S(2)}) copy-start(bf16[1,2048,768]{2,1,0:T(8,128)(2,1)} %param.11) | copy-start | bytes 9437188
  0.0 24.0 %collective-permute-start = (bf16[16,2048]{1,0:T(8,128)(2,1)}, bf16[16,2048]{1,0:T(8,128)(2,1)S(1)}, u32[]{:S(2)}, u32[]{:S(2)}) collective-permute-start(bf16[16,2048]{1,0:T(8,128)(2,1)} %bitcast.25), channel_id=1, source_target_pairs={{0,992},{32,0},{64,32},{96,64},{128,96},{160,128},{192,160},{224,1... | collective-permute-start | bytes 196616 | tf_op jit(solution)/shard_map/ppermute | solution.py:153
  23.3 47.1 %copy-start.1 = (bf16[1,1,256,1536]{3,2,1,0:T(8,128)(2,1)S(1)}, bf16[1,1,256,1536]{3,2,1,0:T(8,128)(2,1)}, u32[]{:S(2)}) copy-start(bf16[1,1,256,1536]{3,2,1,0:T(8,128)(2,1)} %param.10) | copy-start | bytes 2359300
  24.0 11.7 %collective-permute-start.1 = (bf16[16,2176]{1,0:T(8,128)(2,1)S(1)}, bf16[16,2176]{1,0:T(8,128)(2,1)S(1)}, u32[]{:S(2)}, u32[]{:S(2)}) collective-permute-start(bf16[16,2176]{1,0:T(8,128)(2,1)S(1)} %shard_map.74.near_ref), channel_id=1, source_target_pairs={{0,4},{4,0},{1,5},{5,1},{2,6},{6,2},{3,7},{7,3},{8,12},{12,8},{9,1... | collective-permute-start | bytes 208904 | tf_op jit(solution)/shard_map/ppermute | solution.py:136
  105.9 13.9 %all-to-all-start.3 = ((bf16[4,16,2048]{2,1,0:T(8,128)(2,1)}), bf16[4,16,2048]{2,1,0:T(8,128)(2,1)S(1)}, u32[]{:S(2)}, u32[]{:S(2)}) async-start(bf16[4,16,2048]{2,1,0:T(8,128)(2,1)} %bitcast.11), calls=%async_computation.3 | async-start | bytes 524288 | tf_op jit(solution)/shard_map/all_to_all | solution.py:140
  110.2 13.4 %collective-permute-start.2 = (bf16[16,2048]{1,0:T(8,128)(2,1)S(1)}, bf16[16,2048]{1,0:T(8,128)(2,1)S(1)}, u32[]{:S(2)}, u32[]{:S(2)}) collective-permute-start(bf16[16,2048]{1,0:T(8,128)(2,1)S(1)} %shard_map.79), channel_id=1, source_target_pairs={{0,4},{4,0},{1,5},{5,1},{2,6},{6,2},{3,7},{7,3},{8,12},{12,8},{9,1... | collective-permute-start | bytes 196616 | tf_op jit(solution)/shard_map/ppermute | solution.py:136

commit v9 on v8

--- a/solution.py
+++ b/solution.py
@@ -12,8 +12,8 @@
 QUAD = 4
 LANES = 128
 MIB = 1 << 20
-DOWN_PARTS = 3
-UP_PARTS = 4
+DOWN_PARTS = 2
+UP_PARTS = 1
 
 
 def call(kernel, outs, limit, cost):
@@ -83,12 +83,15 @@
         sent_ref[:, pl.ds((mine + k) % 2, 1)] = packed.reshape(YS, 1, slots // YS, width)
 
 
-def combine_kernel(give_ref, rows_ref, near_ref, far_ref):
+def combine_kernel(give_ref, rows_ref, out_ref):
     mine = lax.axis_index("zh")
     slots = give_ref.shape[1]
-    for k, out_ref in ((1, far_ref), (0, near_ref)):
-        rows = rows_ref[:, pl.ds((mine + k) % 2, 1)].reshape(slots, -1)
-        out_ref[...] = dot(give_ref[k], rows, ((0,), (0,))).astype(BF)
+    own = out_ref.shape[1]
+    for k in range(2):
+        half = (mine + k) % 2
+        rows = rows_ref[:, pl.ds(half, 1)].reshape(slots, -1)
+        part = dot(give_ref[k], rows, ((0,), (0,))).astype(BF)
+        out_ref[pl.ds(half * QUAD, QUAD)] = part.reshape(QUAD, own, -1)
 
 
 def expert_kernel(rows_ref, kept_ref, gate_ref, up_hbm, down_hbm, out_ref, up, down, hidden, sems):
@@ -117,19 +120,11 @@
         out_ref[:, at] = total.astype(BF)
 
 
-def sum_of(parts_ref):
+def total_kernel(parts_ref, out_ref):
     acc = parts_ref[0].astype(F32)
     for k in range(1, parts_ref.shape[0]):
         acc = acc + parts_ref[k].astype(F32)
-    return acc
-
-
-def half_kernel(parts_ref, out_ref):
-    out_ref[...] = sum_of(parts_ref).astype(BF)
-
-
-def total_kernel(parts_ref, far_ref, out_ref):
-    out_ref[...] = (sum_of(parts_ref) + far_ref[...].astype(F32)).astype(BF)
+    out_ref[...] = acc.astype(BF)
 
 
 def swapped(x):
@@ -177,11 +172,9 @@
         cost_estimate=pl.CostEstimate(flops=24 * 10**8, bytes_accessed=12 * 10**6, transcendentals=0),
     )(across(sent).reshape(slots, width), saved[0, 0], w_gate[0], w_up[0], w_down[0])
     back = across(grads).reshape(sent.shape)
-    near, far = call(combine_kernel, (bf16(half, width), bf16(half, width)), 8, (10**8, 10**6))(give, back)
-    far = quad(far.reshape(QUAD, tokens, width))
-    far = swapped(call(half_kernel, bf16(tokens, width), 4, (10**6, 10**6))(far))
-    near = quad(near.reshape(QUAD, tokens, width))
-    out = call(total_kernel, bf16(tokens, width), 4, (10**6, 10**6))(near, far)
+    parts = call(combine_kernel, bf16(ZS, tokens, width), 8, (10**8, 10**6))(give, back)
+    parts = lax.all_to_all(parts, ("zh", "zl"), 0, 0, tiled=True)
+    out = call(total_kernel, bf16(tokens, width), 4, (10**6, 10**6))(parts)
     return out[None]
 
 

time: 125 us -> 131 us (1.048)
  the two profiles are of different devices: /device:TPU:34 before, /device:TPU:2 now
where the time goes in v9:
time: 131 us; the launch traced here: 130 us
  blocking collectives  86.1 us (66%)
  starting transfers between devices  26.9 us (21%)
  waiting for transfers between devices  8.62 us (7%)
  Pallas kernels  7.03 us (5%)
  local copies, waits for them, and re-layouts  1.53 us (1%)
    all_to_all x1, blocking collectives, body(): parts = lax.all_to_all(parts, ('zh', 'zl'), 0, 0, tiled=True)  37 us
    all_to_all x2, blocking collectives, across(): lax.all_to_all(x.reshape(YS, -1, x.shape[-1]), 'y', 0, 0, tiled=True)  33.1 us
    ppermute x1, starting transfers between devices, body(): lax.ppermute(cotangent[0], 'section', [(i, (i - 1) % sections) for i in r...  22.7 us
    all_to_all x1, blocking collectives, quad(): return lax.all_to_all(x, 'zl', 0, 0, tiled=True)  16 us
    ppermute x1, waiting for transfers between devices, swapped(): return lax.ppermute(x, 'zh', [(0, 1), (1, 0)])  8.05 us
    pallas_call x1, Pallas kernels, body(): pl.pallas_call(expert_kernel, out_shape=bf16(slots, width), in_specs=[vm,...  4.94 us
    ppermute x1, starting transfers between devices, swapped(): return lax.ppermute(x, 'zh', [(0, 1), (1, 0)])  4.28 us
  transfers between devices with their start and end apart: 2, of which 2 were waited for; matrix products, arithmetic and copies ran while one was open for 1% of the time, Pallas kernels for 0%

profile of v9, /device:TPU:2, one launch (start us, length us, event | category | flops | bytes accessed | tf_op | source)
XLA Modules:
  0.0 130.3 jit_solution(3647520431518392699)
XLA Ops:
  0.0 0.0 copy-start
  0.0 22.7 %collective-permute-start = (bf16[16,2048]{1,0:T(8,128)(2,1)}, bf16[16,2048]{1,0:T(8,128)(2,1)S(1)}, u32[]{:S(2)}, u32[]{:S(2)}) collective-permute-start(bf16[16,2048]{1,0:T(8,128)(2,1)} %bitcast.22), channel_id=1, source_target_pairs={{0,992},{32,0},{64,32},{96,64},{128,96},{160,128},{192,160},{224,1... | collective-permute-start | bytes 196616 | tf_op jit(solution)/shard_map/ppermute | solution.py:148
  22.7 0.8 copy.9.probs_ref
  23.4 0.8 copy.8.ids_ref
  24.2 0.0 copy-start.1
  24.2 0.1 shard_map.73.share_ref
  24.3 0.6 collective-permute-done.rows_ref
  24.9 4.3 %collective-permute-start.1 = (bf16[16,2176]{1,0:T(8,128)(2,1)S(1)}, bf16[16,2176]{1,0:T(8,128)(2,1)S(1)}, u32[]{:S(2)}, u32[]{:S(2)}) collective-permute-start(bf16[16,2176]{1,0:T(8,128)(2,1)S(1)} %shard_map.74.near_ref), channel_id=1, source_target_pairs={{0,4},{4,0},{1,5},{5,1},{2,6},{6,2},{3,7},{7,3},{8,12},{12,8},{9,1... | collective-permute-start | bytes 208904 | tf_op jit(solution)/shard_map/ppermute | solution.py:131
  29.2 8.1 %collective-permute-done.1.far_ref = bf16[16,2176]{1,0:T(8,128)(2,1)S(1)} collective-permute-done((bf16[16,2176]{1,0:T(8,128)(2,1)S(1)}, bf16[16,2176]{1,0:T(8,128)(2,1)S(1)}, u32[]{:S(2)}, u32[]{:S(2)}) %collective-permute-start.1) | collective-permute-done | bytes 69664 | tf_op jit(solution)/shard_map/ppermute | solution.py:131
  37.3 16.0 %all_to_all.20.refs_0_ = bf16[4,32,2176]{2,1,0:T(8,128)(2,1)S(1)} all-to-all(bf16[4,32,2176]{2,1,0:T(8,128)(2,1)S(1)} %shard_map.75), channel_id=1, replica_groups=mesh['section'=32,'y'=4,'zh'=2,'zl'=4] {'zl'}, dimensions={0} | all-to-all | bytes 1114112 | tf_op jit(solution)/shard_map/all_to_all | solution.py:135
  53.3 0.9 shard_map.76
  54.2 17.9 %all_to_all.21 = bf16[4,64,2048]{2,1,0:T(8,128)(2,1)S(1)} all-to-all(bf16[4,64,2048]{2,1,0:T(8,128)(2,1)S(1)} %bitcast.16), channel_id=1, replica_groups=mesh['section'=32,'y'=4,'zh'=2,'zl'=4] {'y'}, dimensions={0} | all-to-all | bytes 2097152 | tf_op jit(solution)/shard_map/all_to_all | solution.py:139
  72.1 0.0 copy-done
  72.1 0.0 copy-done.1
  72.1 4.9 %shard_map.77 = bf16[256,2048]{1,0:T(8,128)(2,1)S(1)} custom-call(bf16[256,2048]{1,0:T(8,128)(2,1)S(1)} %bitcast.12, bf16[256,1536]{1,0:T(8,128)(2,1)S(1)} %bitcast.17, bf16[2048,768]{1,0:T(8,128)(2,1)S(1)} %bitcast.15, bf16[2048,768]{1,0:T(8,128)(2,1)} %bitcast.18, bf16[768,2048]{1,0:T(8,128)(2,1)} %bitcast.19), custom_call_target="tpu_custom_call" | custom-call | flops 2400000000 | bytes 12000000 | tf_op jit(solution)/shard_map/pallas_call | solution.py:160
  77.1 15.2 %all_to_all.22 = bf16[4,64,2048]{2,1,0:T(8,128)(2,1)S(1)} all-to-all(bf16[4,64,2048]{2,1,0:T(8,128)(2,1)S(1)} %bitcast.13), channel_id=1, replica_groups=mesh['section'=32,'y'=4,'zh'=2,'zl'=4] {'y'}, dimensions={0} | all-to-all | bytes 2097152 | tf_op jit(solution)/shard_map/all_to_all | solution.py:139
  92.3 0.3 shard_map.78
  92.6 37.0 %all_to_all.23.parts_ref = bf16[8,16,2048]{2,1,0:T(8,128)(2,1)S(1)} all-to-all(bf16[8,16,2048]{2,1,0:T(8,128)(2,1)S(1)} %shard_map.78), channel_id=1, replica_groups=mesh['section'=32,'y'=4,'zh'=2,'zl'=4] {'zh','zl'}, dimensions={0} | all-to-all | bytes 1048576 | tf_op jit(solution)/shard_map/all_to_all | solution.py:176
  129.6 0.7 shard_map.79
  (2 shorter events, 0.0 us)
Async XLA Ops:
  0.0 72.1 %copy-start = (bf16[1,2048,768]{2,1,0:T(8,128)(2,1)S(1)}, bf16[1,2048,768]{2,1,0:T(8,128)(2,1)}, u32[]{:S(2)}) copy-start(bf16[1,2048,768]{2,1,0:T(8,128)(2,1)} %param.11) | copy-start | bytes 9437188
  0.0 24.9 %collective-permute-start = (bf16[16,2048]{1,0:T(8,128)(2,1)}, bf16[16,2048]{1,0:T(8,128)(2,1)S(1)}, u32[]{:S(2)}, u32[]{:S(2)}) collective-permute-start(bf16[16,2048]{1,0:T(8,128)(2,1)} %bitcast.22), channel_id=1, source_target_pairs={{0,992},{32,0},{64,32},{96,64},{128,96},{160,128},{192,160},{224,1... | collective-permute-start | bytes 196616 | tf_op jit(solution)/shard_map/ppermute | solution.py:148
  24.2 47.9 %copy-start.1 = (bf16[1,1,256,1536]{3,2,1,0:T(8,128)(2,1)S(1)}, bf16[1,1,256,1536]{3,2,1,0:T(8,128)(2,1)}, u32[]{:S(2)}) copy-start(bf16[1,1,256,1536]{3,2,1,0:T(8,128)(2,1)} %param.10) | copy-start | bytes 2359300
  24.9 12.3 %collective-permute-start.1 = (bf16[16,2176]{1,0:T(8,128)(2,1)S(1)}, bf16[16,2176]{1,0:T(8,128)(2,1)S(1)}, u32[]{:S(2)}, u32[]{:S(2)}) collective-permute-start(bf16[16,2176]{1,0:T(8,128)(2,1)S(1)} %shard_map.74.near_ref), channel_id=1, source_target_pairs={{0,4},{4,0},{1,5},{5,1},{2,6},{6,2},{3,7},{7,3},{8,12},{12,8},{9,1... | collective-permute-start | bytes 208904 | tf_op jit(solution)/shard_map/ppermute | solution.py:131

commit v10 on v9

--- a/solution.py
+++ b/solution.py
@@ -86,12 +86,11 @@
 def combine_kernel(give_ref, rows_ref, out_ref):
     mine = lax.axis_index("zh")
     slots = give_ref.shape[1]
-    own = out_ref.shape[1]
+    own = out_ref.shape[1] // 2
     for k in range(2):
-        half = (mine + k) % 2
-        rows = rows_ref[:, pl.ds(half, 1)].reshape(slots, -1)
+        rows = rows_ref[:, pl.ds((mine + k) % 2, 1)].reshape(slots, -1)
         part = dot(give_ref[k], rows, ((0,), (0,))).astype(BF)
-        out_ref[pl.ds(half * QUAD, QUAD)] = part.reshape(QUAD, own, -1)
+        out_ref[:, k * own : (k + 1) * own] = part.reshape(QUAD, own, -1)
 
 
 def expert_kernel(rows_ref, kept_ref, gate_ref, up_hbm, down_hbm, out_ref, up, down, hidden, sems):
@@ -120,11 +119,21 @@
         out_ref[:, at] = total.astype(BF)
 
 
-def total_kernel(parts_ref, out_ref):
-    acc = parts_ref[0].astype(F32)
+def sum_of(parts_ref, at):
+    acc = parts_ref[0, at].astype(F32)
     for k in range(1, parts_ref.shape[0]):
-        acc = acc + parts_ref[k].astype(F32)
-    out_ref[...] = acc.astype(BF)
+        acc = acc + parts_ref[k, at].astype(F32)
+    return acc
+
+
+def half_kernel(parts_ref, out_ref):
+    own = out_ref.shape[0]
+    out_ref[...] = sum_of(parts_ref, slice(own, 2 * own)).astype(BF)
+
+
+def total_kernel(parts_ref, far_ref, out_ref):
+    own = out_ref.shape[0]
+    out_ref[...] = (sum_of(parts_ref, slice(0, own)) + far_ref[...].astype(F32)).astype(BF)
 
 
 def swapped(x):
@@ -172,9 +181,9 @@
         cost_estimate=pl.CostEstimate(flops=24 * 10**8, bytes_accessed=12 * 10**6, transcendentals=0),
     )(across(sent).reshape(slots, width), saved[0, 0], w_gate[0], w_up[0], w_down[0])
     back = across(grads).reshape(sent.shape)
-    parts = call(combine_kernel, bf16(ZS, tokens, width), 8, (10**8, 10**6))(give, back)
-    parts = lax.all_to_all(parts, ("zh", "zl"), 0, 0, tiled=True)
-    out = call(total_kernel, bf16(tokens, width), 4, (10**6, 10**6))(parts)
+    parts = quad(call(combine_kernel, bf16(QUAD, 2 * tokens, width), 8, (10**8, 10**6))(give, back))
+    far = swapped(call(half_kernel, bf16(tokens, width), 4, (10**6, 10**6))(parts))
+    out = call(total_kernel, bf16(tokens, width), 4, (10**6, 10**6))(parts, far)
     return out[None]
 
 

time: 131 us -> 123 us (0.939)
  blocking collectives: 86.1 us -> 64.2 us
  starting transfers between devices: 26.9 us -> 37.1 us
  waiting for transfers between devices: 8.62 us -> 12.6 us
    all_to_all x1 -> x0, blocking collectives: 37 us -> none  [body(): parts = lax.all_to_all(parts, ('zh', 'zl'), 0, 0, tiled=True)]
    all_to_all x1 -> x2, blocking collectives: 16 us -> 31 us  [quad(): return lax.all_to_all(x, 'zl', 0, 0, tiled=True)]
    ppermute x1 -> x2, starting transfers between devices: 4.28 us -> 14.5 us  [swapped(): return lax.ppermute(x, 'zh', [(0, 1), (1, 0)])]
    ppermute x1 -> x2, waiting for transfers between devices: 8.05 us -> 12 us  [swapped(): return lax.ppermute(x, 'zh', [(0, 1), (1, 0)])]
  transfers between devices with their start and end apart: 2 -> 3, of which waited for: 2 -> 3; matrix products, arithmetic and copies ran while one was open for 1% -> 1% of each run, Pallas kernels for 0% -> 0%
where the time goes in v10:
time: 123 us
  blocking collectives  64.2 us (52%)
  starting transfers between devices  37.1 us (30%)
  waiting for transfers between devices  12.6 us (10%)
  Pallas kernels  7.04 us (6%)
  local copies, waits for them, and re-layouts  1.53 us (1%)
    all_to_all x2, blocking collectives, across(): lax.all_to_all(x.reshape(YS, -1, x.shape[-1]), 'y', 0, 0, tiled=True)  33.1 us
    all_to_all x2, blocking collectives, quad(): return lax.all_to_all(x, 'zl', 0, 0, tiled=True)  31 us
    ppermute x1, starting transfers between devices, body(): lax.ppermute(cotangent[0], 'section', [(i, (i - 1) % sections) for i in r...  22.7 us
    ppermute x2, starting transfers between devices, swapped(): return lax.ppermute(x, 'zh', [(0, 1), (1, 0)])  14.5 us
    ppermute x2, waiting for transfers between devices, swapped(): return lax.ppermute(x, 'zh', [(0, 1), (1, 0)])  12 us
    pallas_call x1, Pallas kernels, body(): pl.pallas_call(expert_kernel, out_shape=bf16(slots, width), in_specs=[vm,...  4.94 us
  transfers between devices with their start and end apart: 3, of which 3 were waited for; matrix products, arithmetic and copies ran while one was open for 1% of the time, Pallas kernels for 0%

profile of v10, /device:TPU:2, one launch (start us, length us, event | category | flops | bytes accessed | tf_op | source)
XLA Modules:
  0.0 122.5 jit_solution(1702528306466443716)
XLA Ops:
  0.0 0.0 copy-start
  0.0 22.7 %collective-permute-start = (bf16[16,2048]{1,0:T(8,128)(2,1)}, bf16[16,2048]{1,0:T(8,128)(2,1)S(1)}, u32[]{:S(2)}, u32[]{:S(2)}) collective-permute-start(bf16[16,2048]{1,0:T(8,128)(2,1)} %bitcast.22), channel_id=1, source_target_pairs={{0,992},{32,0},{64,32},{96,64},{128,96},{160,128},{192,160},{224,1... | collective-permute-start | bytes 196616 | tf_op jit(solution)/shard_map/ppermute | solution.py:157
  22.7 0.8 copy.9.probs_ref
  23.4 0.8 copy.8.ids_ref
  24.2 0.0 copy-start.1
  24.2 0.1 shard_map.73.share_ref
  24.3 0.6 collective-permute-done.rows_ref
  24.9 4.3 %collective-permute-start.1 = (bf16[16,2176]{1,0:T(8,128)(2,1)S(1)}, bf16[16,2176]{1,0:T(8,128)(2,1)S(1)}, u32[]{:S(2)}, u32[]{:S(2)}) collective-permute-start(bf16[16,2176]{1,0:T(8,128)(2,1)S(1)} %shard_map.74.near_ref), channel_id=1, source_target_pairs={{0,4},{4,0},{1,5},{5,1},{2,6},{6,2},{3,7},{7,3},{8,12},{12,8},{9,1... | collective-permute-start | bytes 208904 | tf_op jit(solution)/shard_map/ppermute | solution.py:140
  29.2 8.1 %collective-permute-done.1.far_ref = bf16[16,2176]{1,0:T(8,128)(2,1)S(1)} collective-permute-done((bf16[16,2176]{1,0:T(8,128)(2,1)S(1)}, bf16[16,2176]{1,0:T(8,128)(2,1)S(1)}, u32[]{:S(2)}, u32[]{:S(2)}) %collective-permute-start.1) | collective-permute-done | bytes 69664 | tf_op jit(solution)/shard_map/ppermute | solution.py:140
  37.3 16.0 %all_to_all.20.refs_0_ = bf16[4,32,2176]{2,1,0:T(8,128)(2,1)S(1)} all-to-all(bf16[4,32,2176]{2,1,0:T(8,128)(2,1)S(1)} %shard_map.75), channel_id=1, replica_groups=mesh['section'=32,'y'=4,'zh'=2,'zl'=4] {'zl'}, dimensions={0} | all-to-all | bytes 1114112 | tf_op jit(solution)/shard_map/all_to_all | solution.py:144
  53.3 0.9 shard_map.76
  54.2 17.9 %all_to_all.21 = bf16[4,64,2048]{2,1,0:T(8,128)(2,1)S(1)} all-to-all(bf16[4,64,2048]{2,1,0:T(8,128)(2,1)S(1)} %bitcast.16), channel_id=1, replica_groups=mesh['section'=32,'y'=4,'zh'=2,'zl'=4] {'y'}, dimensions={0} | all-to-all | bytes 2097152 | tf_op jit(solution)/shard_map/all_to_all | solution.py:148
  72.1 0.0 copy-done
  72.1 0.0 copy-done.1
  72.1 4.9 %shard_map.77 = bf16[256,2048]{1,0:T(8,128)(2,1)S(1)} custom-call(bf16[256,2048]{1,0:T(8,128)(2,1)S(1)} %bitcast.12, bf16[256,1536]{1,0:T(8,128)(2,1)S(1)} %bitcast.17, bf16[2048,768]{1,0:T(8,128)(2,1)S(1)} %bitcast.15, bf16[2048,768]{1,0:T(8,128)(2,1)} %bitcast.18, bf16[768,2048]{1,0:T(8,128)(2,1)} %bitcast.19), custom_call_target="tpu_custom_call" | custom-call | flops 2400000000 | bytes 12000000 | tf_op jit(solution)/shard_map/pallas_call | solution.py:169
  77.1 15.2 %all_to_all.22 = bf16[4,64,2048]{2,1,0:T(8,128)(2,1)S(1)} all-to-all(bf16[4,64,2048]{2,1,0:T(8,128)(2,1)S(1)} %bitcast.13), channel_id=1, replica_groups=mesh['section'=32,'y'=4,'zh'=2,'zl'=4] {'y'}, dimensions={0} | all-to-all | bytes 2097152 | tf_op jit(solution)/shard_map/all_to_all | solution.py:148
  92.3 0.3 shard_map.78
  92.6 15.0 %all_to_all.23.parts_ref = bf16[4,32,2048]{2,1,0:T(8,128)(2,1)S(1)} all-to-all(bf16[4,32,2048]{2,1,0:T(8,128)(2,1)S(1)} %shard_map.78), channel_id=1, replica_groups=mesh['section'=32,'y'=4,'zh'=2,'zl'=4] {'zl'}, dimensions={0} | all-to-all | bytes 1048576 | tf_op jit(solution)/shard_map/all_to_all | solution.py:144
  107.7 10.2 %collective-permute-start.2 = (bf16[16,2048]{1,0:T(8,128)(2,1)S(1)}, bf16[16,2048]{1,0:T(8,128)(2,1)S(1)}, u32[]{:S(2)}, u32[]{:S(2)}) collective-permute-start(bf16[16,2048]{1,0:T(8,128)(2,1)S(1)} %shard_map.79), channel_id=1, source_target_pairs={{0,4},{4,0},{1,5},{5,1},{2,6},{6,2},{3,7},{7,3},{8,12},{12,8},{9,1... | collective-permute-start | bytes 196616 | tf_op jit(solution)/shard_map/ppermute | solution.py:140
  117.9 4.0 %collective-permute-done.2.far_ref = bf16[16,2048]{1,0:T(8,128)(2,1)S(1)} collective-permute-done((bf16[16,2048]{1,0:T(8,128)(2,1)S(1)}, bf16[16,2048]{1,0:T(8,128)(2,1)S(1)}, u32[]{:S(2)}, u32[]{:S(2)}) %collective-permute-start.2) | collective-permute-done | bytes 65568 | tf_op jit(solution)/shard_map/ppermute | solution.py:140
  121.8 0.7 shard_map.80
  (3 shorter events, 0.1 us)
Async XLA Ops:
  0.0 72.1 %copy-start = (bf16[1,2048,768]{2,1,0:T(8,128)(2,1)S(1)}, bf16[1,2048,768]{2,1,0:T(8,128)(2,1)}, u32[]{:S(2)}) copy-start(bf16[1,2048,768]{2,1,0:T(8,128)(2,1)} %param.11) | copy-start | bytes 9437188
  0.0 24.9 %collective-permute-start = (bf16[16,2048]{1,0:T(8,128)(2,1)}, bf16[16,2048]{1,0:T(8,128)(2,1)S(1)}, u32[]{:S(2)}, u32[]{:S(2)}) collective-permute-start(bf16[16,2048]{1,0:T(8,128)(2,1)} %bitcast.22), channel_id=1, source_target_pairs={{0,992},{32,0},{64,32},{96,64},{128,96},{160,128},{192,160},{224,1... | collective-permute-start | bytes 196616 | tf_op jit(solution)/shard_map/ppermute | solution.py:157
  24.2 47.9 %copy-start.1 = (bf16[1,1,256,1536]{3,2,1,0:T(8,128)(2,1)S(1)}, bf16[1,1,256,1536]{3,2,1,0:T(8,128)(2,1)}, u32[]{:S(2)}) copy-start(bf16[1,1,256,1536]{3,2,1,0:T(8,128)(2,1)} %param.10) | copy-start | bytes 2359300
  24.9 12.3 %collective-permute-start.1 = (bf16[16,2176]{1,0:T(8,128)(2,1)S(1)}, bf16[16,2176]{1,0:T(8,128)(2,1)S(1)}, u32[]{:S(2)}, u32[]{:S(2)}) collective-permute-start(bf16[16,2176]{1,0:T(8,128)(2,1)S(1)} %shard_map.74.near_ref), channel_id=1, source_target_pairs={{0,4},{4,0},{1,5},{5,1},{2,6},{6,2},{3,7},{7,3},{8,12},{12,8},{9,1... | collective-permute-start | bytes 208904 | tf_op jit(solution)/shard_map/ppermute | solution.py:140
  107.7 14.2 %collective-permute-start.2 = (bf16[16,2048]{1,0:T(8,128)(2,1)S(1)}, bf16[16,2048]{1,0:T(8,128)(2,1)S(1)}, u32[]{:S(2)}, u32[]{:S(2)}) collective-permute-start(bf16[16,2048]{1,0:T(8,128)(2,1)S(1)} %shard_map.79), channel_id=1, source_target_pairs={{0,4},{4,0},{1,5},{5,1},{2,6},{6,2},{3,7},{7,3},{8,12},{12,8},{9,1... | collective-permute-start | bytes 196616 | tf_op jit(solution)/shard_map/ppermute | solution.py:140

commit v11 on v8

--- a/solution.py
+++ b/solution.py
@@ -12,8 +12,8 @@
 QUAD = 4
 LANES = 128
 MIB = 1 << 20
-DOWN_PARTS = 3
-UP_PARTS = 4
+DOWN_PARTS = 2
+UP_PARTS = 1
 
 
 def call(kernel, outs, limit, cost):
@@ -50,17 +50,13 @@
     out_ref[...] = acc.astype(BF)
 
 
-def payload_kernel(rows_ref, share_ref, out_ref):
-    width = rows_ref.shape[1]
-    out_ref[:, :width] = rows_ref[...]
-    out_ref[:, width:] = share_ref[...]
-
-
-def copies_kernel(near_ref, far_ref, out_ref):
-    own = near_ref.shape[0]
+def payload_kernel(near_ref, far_ref, near_share_ref, far_share_ref, out_ref):
+    own, width = near_ref.shape
     for k in range(QUAD):
-        out_ref[k, :own] = near_ref[...]
-        out_ref[k, own:] = far_ref[...]
+        out_ref[k, :own, :width] = near_ref[...]
+        out_ref[k, own:, :width] = far_ref[...]
+        out_ref[k, :own, width:] = near_share_ref[...]
+        out_ref[k, own:, width:] = far_share_ref[...]
 
 
 def pack_kernel(cap, own, rows_ref, sent_ref, give_ref):
@@ -150,10 +146,19 @@
     slots = saved.shape[2]
     cap = slots // (YS * ZS)
     half = QUAD * tokens
+    halves = ZS // QUAD
+    moves = [
+        ((q * halves + h) * QUAD + k, ((q - 1) % sections * halves + (h + 1) % halves) * QUAD + k)
+        for q in range(sections)
+        for h in range(halves)
+        for k in range(QUAD)
+    ]
+    crossed = lax.ppermute(cotangent[0], ("section", "zh", "zl"), moves)
     incoming = lax.ppermute(cotangent[0], "section", [(i, (i - 1) % sections) for i in range(sections)])
     shares = call(shares_kernel, bf16(tokens, LANES), 4, (10**5, 10**4))(expert_ids[0], gate_probs[0])
-    one = call(payload_kernel, bf16(tokens, width + LANES), 4, (10**5, 10**6))(incoming, shares)
-    payload = call(copies_kernel, bf16(QUAD, 2 * tokens, width + LANES), 4, (10**5, 10**6))(one, swapped(one))
+    payload = call(payload_kernel, bf16(QUAD, 2 * tokens, width + LANES), 4, (10**5, 10**6))(
+        incoming, crossed, shares, swapped(shares)
+    )
     sent, give = call(
         lambda *refs: pack_kernel(cap, tokens, *refs),
         (bf16(YS, 2, slots // (2 * YS), width), bf16(2, slots // 2, half)),

time: 125 us -> 122 us (0.976)
  the two profiles are of different devices: /device:TPU:34 before, /device:TPU:32 now
where the time goes in v11:
time: 122 us
  blocking collectives  57.9 us (47%)
  starting transfers between devices  46.9 us (38%)
  Pallas kernels  7.74 us (6%)
  waiting for transfers between devices  7.74 us (6%)
  local copies, waits for them, and re-layouts  1.53 us (1%)
    all_to_all x2, blocking collectives, across(): lax.all_to_all(x.reshape(YS, -1, x.shape[-1]), 'y', 0, 0, tiled=True)  29.4 us
    all_to_all x2, blocking collectives, quad(): return lax.all_to_all(x, 'zl', 0, 0, tiled=True)  28.6 us
    ppermute x1, starting transfers between devices, body(): crossed = lax.ppermute(cotangent[0], ('section', 'zh', 'zl'), moves)  21 us
    ppermute x2, starting transfers between devices, swapped(): return lax.ppermute(x, 'zh', [(0, 1), (1, 0)])  14.1 us
    ppermute x2, waiting for transfers between devices, swapped(): return lax.ppermute(x, 'zh', [(0, 1), (1, 0)])  7.74 us
    ppermute x1, starting transfers between devices, body(): lax.ppermute(cotangent[0], 'section', [(i, (i - 1) % sections) for i in r...  7.56 us
    pallas_call x1, Pallas kernels, body(): pl.pallas_call(expert_kernel, out_shape=bf16(slots, width), in_specs=[vm,...  4.93 us
    all_to_all x1, starting transfers between devices, quad(): return lax.all_to_all(x, 'zl', 0, 0, tiled=True)  4.29 us
  transfers between devices with their start and end apart: 5, of which 2 were waited for; matrix products, arithmetic and copies ran while one was open for 1% of the time, Pallas kernels for 0%

profile of v11, /device:TPU:32, one launch (start us, length us, event | category | flops | bytes accessed | tf_op | source)
XLA Modules:
  0.0 121.9 jit_solution(15410006625752360858)
XLA Ops:
  0.0 0.0 copy-start
  0.0 21.0 %collective-permute-start.1 = (bf16[16,2048]{1,0:T(8,128)(2,1)}, bf16[16,2048]{1,0:T(8,128)(2,1)S(1)}, u32[]{:S(2)}, u32[]{:S(2)}) collective-permute-start(bf16[16,2048]{1,0:T(8,128)(2,1)} %bitcast.25), channel_id=1, source_target_pairs={{0,996},{1,997},{2,998},{3,999},{4,992},{5,993},{6,994},{7,995},{3... | collective-permute-start | bytes 196616 | tf_op jit(solution)/shard_map/ppermute | solution.py:156
  21.0 7.6 %collective-permute-start = (bf16[16,2048]{1,0:T(8,128)(2,1)}, bf16[16,2048]{1,0:T(8,128)(2,1)S(1)}, u32[]{:S(2)}, u32[]{:S(2)}) collective-permute-start(bf16[16,2048]{1,0:T(8,128)(2,1)} %bitcast.26), channel_id=1, source_target_pairs={{0,992},{32,0},{64,32},{96,64},{128,96},{160,128},{192,160},{224,1... | collective-permute-start | bytes 196616 | tf_op jit(solution)/shard_map/ppermute | solution.py:157
  28.6 0.8 copy.9.probs_ref
  29.3 0.8 copy.8.ids_ref
  30.1 0.0 copy-start.1
  30.1 0.1 shard_map.73.near_share_ref
  30.2 5.6 %collective-permute-start.2 = (bf16[16,128]{1,0:T(8,128)(2,1)S(1)}, bf16[16,128]{1,0:T(8,128)(2,1)S(1)}, u32[]{:S(2)}, u32[]{:S(2)}) collective-permute-start(bf16[16,128]{1,0:T(8,128)(2,1)S(1)} %shard_map.73.near_share_ref), channel_id=1, source_target_pairs={{0,4},{4,0},{1,5},{5,1},{2,6},{6,2},{3,7},{7,3},{8,12},{12,8},{9,1... | collective-permute-start | bytes 12296 | tf_op jit(solution)/shard_map/ppermute | solution.py:132
  35.8 3.9 %collective-permute-done.2.far_share_ref = bf16[16,128]{1,0:T(8,128)(2,1)S(1)} collective-permute-done((bf16[16,128]{1,0:T(8,128)(2,1)S(1)}, bf16[16,128]{1,0:T(8,128)(2,1)S(1)}, u32[]{:S(2)}, u32[]{:S(2)}) %collective-permute-start.2) | collective-permute-done | bytes 4128 | tf_op jit(solution)/shard_map/ppermute | solution.py:132
  39.7 0.0 collective-permute-done.1.far_ref
  39.7 0.0 collective-permute-done.near_ref
  39.8 14.5 %all_to_all.25.refs_0_ = bf16[4,32,2176]{2,1,0:T(8,128)(2,1)S(1)} all-to-all(bf16[4,32,2176]{2,1,0:T(8,128)(2,1)S(1)} %shard_map.74), channel_id=1, replica_groups=mesh['section'=32,'y'=4,'zh'=2,'zl'=4] {'zl'}, dimensions={0} | all-to-all | bytes 1114112 | tf_op jit(solution)/shard_map/all_to_all | solution.py:136
  54.3 0.9 shard_map.75
  55.2 16.1 %all_to_all.26 = bf16[4,64,2048]{2,1,0:T(8,128)(2,1)S(1)} all-to-all(bf16[4,64,2048]{2,1,0:T(8,128)(2,1)S(1)} %bitcast.18), channel_id=1, replica_groups=mesh['section'=32,'y'=4,'zh'=2,'zl'=4] {'y'}, dimensions={0} | all-to-all | bytes 2097152 | tf_op jit(solution)/shard_map/all_to_all | solution.py:140
  71.3 0.0 copy-done
  71.3 0.0 copy-done.1
  71.3 4.9 %shard_map.76 = bf16[256,2048]{1,0:T(8,128)(2,1)S(1)} custom-call(bf16[256,2048]{1,0:T(8,128)(2,1)S(1)} %bitcast.14, bf16[256,1536]{1,0:T(8,128)(2,1)S(1)} %bitcast.19, bf16[2048,768]{1,0:T(8,128)(2,1)S(1)} %bitcast.17, bf16[2048,768]{1,0:T(8,128)(2,1)} %bitcast.21, bf16[768,2048]{1,0:T(8,128)(2,1)} %bitcast.22), custom_call_target="tpu_custom_call" | custom-call | flops 2400000000 | bytes 12000000 | tf_op jit(solution)/shard_map/pallas_call | solution.py:170
  76.3 13.3 %all_to_all.27 = bf16[4,64,2048]{2,1,0:T(8,128)(2,1)S(1)} all-to-all(bf16[4,64,2048]{2,1,0:T(8,128)(2,1)S(1)} %bitcast.15), channel_id=1, replica_groups=mesh['section'=32,'y'=4,'zh'=2,'zl'=4] {'y'}, dimensions={0} | all-to-all | bytes 2097152 | tf_op jit(solution)/shard_map/all_to_all | solution.py:140
  89.6 1.0 shard_map.77
  90.6 14.0 %all_to_all.28.parts_ref = bf16[4,16,2048]{2,1,0:T(8,128)(2,1)S(1)} all-to-all(bf16[4,16,2048]{2,1,0:T(8,128)(2,1)S(1)} %bitcast.20), channel_id=1, replica_groups=mesh['section'=32,'y'=4,'zh'=2,'zl'=4] {'zl'}, dimensions={0} | all-to-all | bytes 524288 | tf_op jit(solution)/shard_map/all_to_all | solution.py:136
  104.6 4.3 %all-to-all-start.3 = ((bf16[4,16,2048]{2,1,0:T(8,128)(2,1)}), bf16[4,16,2048]{2,1,0:T(8,128)(2,1)S(1)}, u32[]{:S(2)}, u32[]{:S(2)}) async-start(bf16[4,16,2048]{2,1,0:T(8,128)(2,1)} %bitcast.11), calls=%async_computation.3 | async-start | bytes 524288 | tf_op jit(solution)/shard_map/all_to_all | solution.py:136
  109.0 8.5 %collective-permute-start.3 = (bf16[16,2048]{1,0:T(8,128)(2,1)S(1)}, bf16[16,2048]{1,0:T(8,128)(2,1)S(1)}, u32[]{:S(2)}, u32[]{:S(2)}) collective-permute-start(bf16[16,2048]{1,0:T(8,128)(2,1)S(1)} %shard_map.78), channel_id=1, source_target_pairs={{0,4},{4,0},{1,5},{5,1},{2,6},{6,2},{3,7},{7,3},{8,12},{12,8},{9,1... | collective-permute-start | bytes 196616 | tf_op jit(solution)/shard_map/ppermute | solution.py:132
  117.4 0.0 all-to-all-done.3.parts_ref
  117.5 3.8 %collective-permute-done.3.far_ref = bf16[16,2048]{1,0:T(8,128)(2,1)S(1)} collective-permute-done((bf16[16,2048]{1,0:T(8,128)(2,1)S(1)}, bf16[16,2048]{1,0:T(8,128)(2,1)S(1)}, u32[]{:S(2)}, u32[]{:S(2)}) %collective-permute-start.3) | collective-permute-done | bytes 65568 | tf_op jit(solution)/shard_map/ppermute | solution.py:132
  121.3 0.7 shard_map.79
  (2 shorter events, 0.1 us)
Async XLA Ops:
  0.0 71.3 %copy-start = (bf16[1,2048,768]{2,1,0:T(8,128)(2,1)S(1)}, bf16[1,2048,768]{2,1,0:T(8,128)(2,1)}, u32[]{:S(2)}) copy-start(bf16[1,2048,768]{2,1,0:T(8,128)(2,1)} %param.11) | copy-start | bytes 9437188
  0.0 39.7 %collective-permute-start.1 = (bf16[16,2048]{1,0:T(8,128)(2,1)}, bf16[16,2048]{1,0:T(8,128)(2,1)S(1)}, u32[]{:S(2)}, u32[]{:S(2)}) collective-permute-start(bf16[16,2048]{1,0:T(8,128)(2,1)} %bitcast.25), channel_id=1, source_target_pairs={{0,996},{1,997},{2,998},{3,999},{4,992},{5,993},{6,994},{7,995},{3... | collective-permute-start | bytes 196616 | tf_op jit(solution)/shard_map/ppermute | solution.py:156
  21.0 18.7 %collective-permute-start = (bf16[16,2048]{1,0:T(8,128)(2,1)}, bf16[16,2048]{1,0:T(8,128)(2,1)S(1)}, u32[]{:S(2)}, u32[]{:S(2)}) collective-permute-start(bf16[16,2048]{1,0:T(8,128)(2,1)} %bitcast.26), channel_id=1, source_target_pairs={{0,992},{32,0},{64,32},{96,64},{128,96},{160,128},{192,160},{224,1... | collective-permute-start | bytes 196616 | tf_op jit(solution)/shard_map/ppermute | solution.py:157
  30.1 41.2 %copy-start.1 = (bf16[1,1,256,1536]{3,2,1,0:T(8,128)(2,1)S(1)}, bf16[1,1,256,1536]{3,2,1,0:T(8,128)(2,1)}, u32[]{:S(2)}) copy-start(bf16[1,1,256,1536]{3,2,1,0:T(8,128)(2,1)} %param.10) | copy-start | bytes 2359300
  30.2 9.5 %collective-permute-start.2 = (bf16[16,128]{1,0:T(8,128)(2,1)S(1)}, bf16[16,128]{1,0:T(8,128)(2,1)S(1)}, u32[]{:S(2)}, u32[]{:S(2)}) collective-permute-start(bf16[16,128]{1,0:T(8,128)(2,1)S(1)} %shard_map.73.near_share_ref), channel_id=1, source_target_pairs={{0,4},{4,0},{1,5},{5,1},{2,6},{6,2},{3,7},{7,3},{8,12},{12,8},{9,1... | collective-permute-start | bytes 12296 | tf_op jit(solution)/shard_map/ppermute | solution.py:132
  104.6 12.8 %all-to-all-start.3 = ((bf16[4,16,2048]{2,1,0:T(8,128)(2,1)}), bf16[4,16,2048]{2,1,0:T(8,128)(2,1)S(1)}, u32[]{:S(2)}, u32[]{:S(2)}) async-start(bf16[4,16,2048]{2,1,0:T(8,128)(2,1)} %bitcast.11), calls=%async_computation.3 | async-start | bytes 524288 | tf_op jit(solution)/shard_map/all_to_all | solution.py:136
  109.0 12.3 %collective-permute-start.3 = (bf16[16,2048]{1,0:T(8,128)(2,1)S(1)}, bf16[16,2048]{1,0:T(8,128)(2,1)S(1)}, u32[]{:S(2)}, u32[]{:S(2)}) collective-permute-start(bf16[16,2048]{1,0:T(8,128)(2,1)S(1)} %shard_map.78), channel_id=1, source_target_pairs={{0,4},{4,0},{1,5},{5,1},{2,6},{6,2},{3,7},{7,3},{8,12},{12,8},{9,1... | collective-permute-start | bytes 196616 | tf_op jit(solution)/shard_map/ppermute | solution.py:132
